TPU v7x, 128 devices: a whole 4x4x4 slice. The times are simulated.
128 devices in a mesh: rep: 16 (over z, x), tp: 8 (over y, core).
Axes of the slice: x: 4, y: 4, z: 4, core: 2. Of those that a mesh axis runs over, the one named last changes fastest.
Arguments:
- x_in: bfloat16 [512, 16384], P('rep', 'tp'), may hold values from -6 to 6
- z_gate: bfloat16 [512, 16384], P('rep', 'tp'), may hold values from -6 to 6
- conv_state: bfloat16 [512, 3, 16384], P('rep', None, 'tp'), may hold values from -6 to 6
- conv_pool: bfloat16 [512, 3, 16384], P('rep', None, 'tp'), may hold values from -6 to 6
- ssm_state: float32 [512, 16, 16384], P('rep', None, 'tp'), may hold values from -6 to 6
- ssm_pool: float32 [512, 16, 16384], P('rep', None, 'tp'), may hold values from -6 to 6
- conv_weight: bfloat16 [4, 16384], P(None, 'tp'), may hold values from -3 to 3
- conv_bias: float32 [16384], P('tp'), may hold values from -0.5 to 0.5
- x_proj: bfloat16 [16384, 544], P('tp'), may hold values from -0.046875 to 0.046875
- dt_gain: float32 [512], replicated, may hold values from 0.5 to 1.5
- b_gain: float32 [16], replicated, may hold values from 0.5 to 1.5
- c_gain: float32 [16], replicated, may hold values from 0.5 to 1.5
- dt_proj: bfloat16 [512, 16384], P(None, 'tp'), may hold values from -0.25 to 0.25
- dt_bias: float32 [16384], P('tp'), may hold values from -3 to 0
- decay_rate: float32 [16, 16384], P(None, 'tp'), may hold values from 0.5 to 16
- skip: float32 [16384], P('tp'), may hold values from 0.5 to 1.5
- query: bfloat16 [512, 8192], P('rep', 'tp'), may hold values from -16 to 16
- new_kv: bfloat16 [512, 2048], P('rep', 'tp'), may hold values from -6 to 6
- kv_cache: bfloat16 [512, 512, 2048], P('rep', None, 'tp'), may hold values from -16 to 16
- kv_pool: bfloat16 [4096, 16, 2048], P('rep', None, 'tp'), may hold values from -16 to 16
- ctx_len: int32 [512], P('rep'), may hold values from 2 to 512
- row_owner: int32 [512], P('rep'), may hold values from -1 to 15, as said below
- row_pos: int32 [512], P('rep'), may hold values from 0 to 1, as said below
- swap_slot: int32 [16, 16, 2], P('rep'), may hold values from 0 to 31, as said below
- swap_lens: int32 [16, 16, 2], P('rep'), may hold values from 2 to 512
- swap_pages: int32 [16, 16, 2, 32], P('rep'), may hold values from 0 to 255
Outputs:
- mamba_out: bfloat16 [512, 16384], P('rep', 'tp')
- attn_out: bfloat16 [512, 8192], P('rep', 'tp')
- new_ssm: float32 [512, 16, 16384], P('rep', None, 'tp')
- new_conv: bfloat16 [512, 3, 16384], P('rep', None, 'tp')
Inputs may be any that keep to these rules, and one draw needn't show every extreme that they name: -1 marks a resident request; otherwise the group along rep whose pool holds it. Of one group's rows at most 2 name the same owner, and the pairs (row_owner, row_pos) of one group's resumed rows are distinct; in every draw some group resumes 2 requests from every owner. A resumed request of group g with owner o is entry [o, g, row_pos] of the owner's lists; entries that no request names are unused. `swap_slot`: slots of one owner are distinct. `swap_pages`: only the first ceil(length / 16) pages of a request are read; pages may be shared.
All inputs are finite; a program needn't handle non-finite values.
Results may differ from a plain program's by a relative error of at most 0.013.
Values may be sent and summed in bfloat16 or wider, within the bound.
No kernel may reach another device: no remote copies, remote signals or barrier semaphores. Data moves between devices by JAX's collectives and lax.ppermute only.
A program may use at most 128 MiB of HBM per device.

v0:
```python
import math

import jax
import jax.numpy as jnp
from jax import lax
from jax.sharding import PartitionSpec as P

HD = 128


def attend_block(query_heads, context, ctx_lengths):
    item_count = query_heads.shape[0]
    kv_heads = query_heads.shape[1]
    head_width = query_heads.shape[3]
    kv_pairs = context.reshape(item_count, context.shape[1], kv_heads, 2, head_width)
    key_rows = kv_pairs[:, :, :, 0, :]
    value_rows = kv_pairs[:, :, :, 1, :]
    score_block = jnp.einsum(
        "nkgd,ntkd->nkgt", query_heads, key_rows, preferred_element_type=jnp.float32
    ) * (1.0 / math.sqrt(head_width))
    live_mask = (jnp.arange(context.shape[1])[None, :] < ctx_lengths[:, None])[:, None, None, :]
    masked = jnp.where(live_mask, score_block, -1e30)
    score_top = jnp.max(masked, axis=-1)
    prob_weights = jnp.where(live_mask, jnp.exp(masked - score_top[..., None]), 0.0).astype(
        jnp.bfloat16
    )
    prob_total = jnp.sum(prob_weights.astype(jnp.float32), axis=-1)
    attn_mix = jnp.einsum(
        "nkgt,ntkd->nkgd", prob_weights, value_rows, preferred_element_type=jnp.float32
    )
    return (attn_mix, score_top, prob_total)


def finish(query_heads, new_pairs, attn_mix, score_top, prob_total):
    item_count, kv_heads, q_groups, head_width = query_heads.shape
    kv_pairs = new_pairs.reshape(item_count, kv_heads, 2, head_width)
    new_score = jnp.einsum(
        "nkgd,nkd->nkg", query_heads, kv_pairs[:, :, 0, :], preferred_element_type=jnp.float32
    ) * (1.0 / math.sqrt(head_width))
    score_peak = jnp.maximum(score_top, new_score)
    old_scale = jnp.exp(score_top - score_peak)
    new_scale = jnp.exp(new_score - score_peak)
    numerator = attn_mix * old_scale[..., None] + new_scale[..., None] * kv_pairs[
        :, :, None, 1, :
    ].astype(jnp.float32)
    result = numerator / (prob_total * old_scale + new_scale)[..., None]
    return result.reshape(item_count, -1).astype(jnp.bfloat16)


def rms_scaled(values, gain):
    return (
        values * lax.rsqrt(jnp.mean(values * values, axis=-1, keepdims=True) + 1e-06) * gain
    ).astype(jnp.bfloat16)


def shards(
    x_in,
    z_gate,
    conv_state,
    conv_pool,
    ssm_state,
    ssm_pool,
    conv_weight,
    conv_bias,
    x_proj,
    dt_gain,
    b_gain,
    c_gain,
    dt_proj,
    dt_bias,
    decay_rate,
    skip,
    query,
    new_kv,
    kv_cache,
    kv_pool,
    ctx_len,
    row_owner,
    row_pos,
    swap_slot,
    swap_lens,
    swap_pages,
):
    peer_count = lax.axis_size("rep")
    row_count = x_in.shape[0]
    slot_cap = swap_slot.shape[2]
    entry_count = peer_count * slot_cap
    head_width = HD
    kv_width = kv_cache.shape[2]
    kv_heads = kv_width // (2 * head_width)
    q_groups = query.shape[1] // (head_width * kv_heads)
    query_heads = query.reshape(row_count, kv_heads, q_groups, head_width)
    slot_list = swap_slot[0].reshape(-1)
    page_list = swap_pages[0].reshape(-1)
    ssm_send = jnp.take(ssm_pool, slot_list, axis=0).reshape(
        (peer_count, slot_cap) + ssm_pool.shape[1:]
    )
    conv_send = jnp.take(conv_pool, slot_list, axis=0).reshape(
        (peer_count, slot_cap) + conv_pool.shape[1:]
    )
    resumed = row_owner >= 0
    where_from = jnp.where(resumed, row_owner * slot_cap + row_pos, 0)

    def pick_rows(local_rows, received):
        flat = received.reshape((entry_count,) + received.shape[2:])
        picked = jnp.take(flat, where_from, axis=0)
        flag = resumed.reshape((row_count,) + (1,) * (local_rows.ndim - 1))
        return jnp.where(flag, picked, local_rows)

    page_send = jnp.take(kv_pool, page_list, axis=0).reshape(peer_count, slot_cap, -1, kv_width)
    ssm_in, lens_in = (
        lax.all_to_all(ssm_send, "rep", split_axis=0, concat_axis=0, tiled=True),
        lax.all_to_all(
            swap_lens[0].astype(jnp.float32), "rep", split_axis=0, concat_axis=0, tiled=True
        ),
    )
    conv_in, pages_in = (
        lax.all_to_all(conv_send, "rep", split_axis=0, concat_axis=0, tiled=True),
        lax.all_to_all(page_send, "rep", split_axis=0, concat_axis=0, tiled=True),
    )
    context = pick_rows(kv_cache, pages_in)
    ctx_lengths = jnp.where(
        resumed, jnp.take(lens_in.reshape(-1), where_from).astype(jnp.int32), ctx_len
    )
    attn_mix, score_top, prob_total = attend_block(query_heads, context, ctx_lengths)
    prev_conv = pick_rows(conv_state, conv_in)
    prev_ssm = pick_rows(ssm_state, ssm_in)
    conv_window = jnp.concatenate([prev_conv, x_in[:, None, :]], axis=1)
    conv_sum = (
        jnp.sum(conv_window.astype(jnp.float32) * conv_weight.astype(jnp.float32)[None], axis=1)
        + conv_bias
    )
    mixed_in = jax.nn.silu(conv_sum).astype(jnp.bfloat16)
    proj_part = jnp.dot(mixed_in, x_proj, preferred_element_type=jnp.float32)
    proj = lax.psum(proj_part, "tp")
    dt_rank = dt_proj.shape[0]
    state_size = decay_rate.shape[0]
    dt_normed = rms_scaled(proj[:, :dt_rank], dt_gain)
    dt_step = jax.nn.softplus(
        jnp.dot(dt_normed, dt_proj, preferred_element_type=jnp.float32) + dt_bias
    )
    inject = rms_scaled(proj[:, dt_rank : dt_rank + state_size], b_gain).astype(jnp.float32)
    read_out = rms_scaled(proj[:, dt_rank + state_size :], c_gain).astype(jnp.float32)
    signal = mixed_in.astype(jnp.float32)
    new_ssm = (
        jnp.exp(-dt_step[:, None, :] * decay_rate[None]) * prev_ssm
        + (dt_step * signal)[:, None, :] * inject[:, :, None]
    )
    mamba_out = (
        (jnp.sum(read_out[:, :, None] * new_ssm, axis=1) + skip * signal)
        * jax.nn.silu(z_gate.astype(jnp.float32))
    ).astype(jnp.bfloat16)
    attn_out = finish(query_heads, new_kv, attn_mix, score_top, prob_total)
    return (mamba_out, attn_out, new_ssm, conv_window[:, 1:])


def solution(mesh):
    in_specs = (
        P("rep", "tp"),
        P("rep", "tp"),
        P("rep", None, "tp"),
        P("rep", None, "tp"),
        P("rep", None, "tp"),
        P("rep", None, "tp"),
        P(None, "tp"),
        P("tp"),
        P("tp", None),
        P(),
        P(),
        P(),
        P(None, "tp"),
        P("tp"),
        P(None, "tp"),
        P("tp"),
        P("rep", "tp"),
        P("rep", "tp"),
        P("rep", None, "tp"),
        P("rep", None, "tp"),
        P("rep"),
        P("rep"),
        P("rep"),
        P("rep", None, None),
        P("rep", None, None),
        P("rep", None, None, None),
    )
    out_specs = (P("rep", "tp"), P("rep", "tp"), P("rep", None, "tp"), P("rep", None, "tp"))
    return jax.shard_map(shards, mesh=mesh, in_specs=in_specs, out_specs=out_specs, check_vma=False)
```

profile of v0, /device:TPU:1, one launch (start us, length us, event | category | flops | bytes accessed | tf_op | source)
XLA Modules:
  0.0 270.1 jit_solution(14854565590719731376)
XLA Ops:
  7.2 0.8 convert_bitcast_fusion
  8.0 0.7 copy.59
  8.7 8.4 %all-to-all-start.2 = ((f32[16,1,2]{2,1,0:T(1,128)}), f32[16,1,2]{2,1,0:T(1,128)S(1)}, u32[]{:S(2)}, u32[]{:S(2)}) async-start(f32[16,1,2]{2,1,0:T(1,128)} %copy.59), calls=%async_computation.2 | async-start | bytes 16384 | tf_op jit(solution)/shard_map/all_to_all | solution.py:113
  17.1 0.8 copy.54
  18.0 2.7 %gather_fusion.3 = bf16[32,3,2048]{2,0,1:T(8,128)(2,1)S(1)} fusion(bf16[32,3,2048]{2,0,1:T(8,128)(2,1)} %param.33, s32[1024]{0:T(1024)S(1)} %pad_clamp_fusion.1), kind=kCustom, calls=%fused_computation.clone | custom fusion | bytes 786560 | tf_op jit(solution)/shard_map/jit(_take)/gather | solution.py:98
  20.8 0.3 reshape.234
  21.1 1.0 copy.55
  22.1 5.0 %gather_fusion.5 = f32[32,16,2048]{2,1,0:T(8,128)} fusion(f32[32,16,2048]{2,1,0:T(8,128)} %param.35, s32[1024]{0:T(1024)S(1)} %pad_clamp_fusion.1), kind=kCustom, calls=%fused_computation.1.clone | custom fusion | bytes 8388736 | tf_op jit(solution)/shard_map/jit(_take)/gather | solution.py:95
  27.1 6.7 %all-to-all-start = ((bf16[16,2,3,2048]{3,1,2,0:T(2,128)(2,1)}), bf16[16,2,3,2048]{3,1,2,0:T(2,128)(2,1)S(1)}, u32[]{:S(2)}, u32[]{:S(2)}) async-start(bf16[16,2,3,2048]{3,1,2,0:T(2,128)(2,1)} %copy.55), calls=%async_computation | async-start | bytes 786432 | tf_op jit(solution)/shard_map/all_to_all | solution.py:118
  33.8 4.9 %broadcast_select_fusion.1 = f32[32,16,2048]{2,1,0:T(8,128)} fusion(f32[32,16,2048]{2,1,0:T(8,128)} %gather_fusion.5, pred[32]{0:T(512)(128)(4,1)S(1)} %compare_and_fusion.2), kind=kLoop, calls=%fused_computation.18 | loop fusion | flops 1048576 | bytes 8388640 | tf_op jit(solution)/shard_map/jit(_take)/select_n | solution.py:95
  38.7 3.5 %all-to-all-done = bf16[16,2,3,2048]{3,1,2,0:T(2,128)(2,1)S(1)} async-done(((bf16[16,2,3,2048]{3,1,2,0:T(2,128)(2,1)}), bf16[16,2,3,2048]{3,1,2,0:T(2,128)(2,1)S(1)}, u32[]{:S(2)}, u32[]{:S(2)}) %all-to-all-start) | async-done | bytes 393248 | tf_op jit(solution)/shard_map/all_to_all | solution.py:118
  42.2 0.7 copy-done.2
  43.0 4.6 %all-to-all-start.1 = ((f32[16,2,16,2048]{3,2,1,0:T(8,128)}), f32[16,2,16,2048]{3,2,1,0:T(8,128)}, u32[]{:S(2)}, u32[]{:S(2)}) async-start(f32[16,2,16,2048]{3,2,1,0:T(8,128)} %bitcast.61), calls=%async_computation.1 | async-start | bytes 8388608 | tf_op jit(solution)/shard_map/all_to_all | solution.py:112
  47.7 0.2 broadcast_in_dim.130
  47.9 0.3 broadcast_in_dim.131
  48.3 11.2 %gather_fusion.1 = bf16[1024,16,256]{2,1,0:T(8,128)(2,1)} fusion(bf16[256,16,256]{2,1,0:T(8,128)(2,1)} %param.49, s32[1024]{0:T(1024)S(1)} %broadcast_clamp_fusion), kind=kCustom, calls=%fused_computation.5 | custom fusion | bytes 16781312 | tf_op jit(solution)/shard_map/jit(_take)/gather | solution.py:110
  59.5 8.0 %broadcast_select_fusion = bf16[16,2,512,256]{3,2,1,0:T(8,128)(2,1)} fusion(bf16[16,2,512,256]{3,2,1,0:T(8,128)(2,1)} %bitcast.60, pred[16,2,512]{2,1,0:T(4,128)(4,1)S(1)} %copy.61), kind=kLoop, calls=%fused_computation.8 | loop fusion | flops 4194304 | bytes 16793600 | tf_op jit(solution)/shard_map/jit(_take)/select_n | solution.py:110
  67.6 37.0 %all-to-all-done.1 = f32[16,2,16,2048]{3,2,1,0:T(8,128)} async-done(((f32[16,2,16,2048]{3,2,1,0:T(8,128)}), f32[16,2,16,2048]{3,2,1,0:T(8,128)}, u32[]{:S(2)}, u32[]{:S(2)}) %all-to-all-start.1) | async-done | bytes 4194336 | tf_op jit(solution)/shard_map/all_to_all | solution.py:112
  104.6 4.7 %all-to-all-start.3 = ((bf16[16,2,512,256]{3,2,1,0:T(8,128)(2,1)}), bf16[16,2,512,256]{3,2,1,0:T(8,128)(2,1)}, u32[]{:S(2)}, u32[]{:S(2)}) async-start(bf16[16,2,512,256]{3,2,1,0:T(8,128)(2,1)} %broadcast_select_fusion), calls=%async_computation.3 | async-start | bytes 16777216 | tf_op jit(solution)/shard_map/all_to_all | solution.py:119
  109.3 0.2 all-reduce.2.cloned.1.call-start
  109.6 0.2 copy.58
  109.9 0.1 fusion.22
  110.1 0.5 broadcast.160
  110.6 0.7 reduce.7
  111.4 0.7 gather_fusion
  112.2 1.3 copy.56
  113.5 1.8 gather_fusion.4
  115.3 1.7 copy_select_fusion
  117.0 1.1 multiply_reduce_fusion.1
  118.1 1.4 fusion.26
  119.6 0.7 fusion.11
  120.3 1.0 copy.65
  121.3 60.5 %all-reduce.2.cloned.1.call-done = f32[32,544]{1,0:T(8,128)} async-done(((f32[32,544]{1,0:T(8,128)}), f32[32,544]{1,0:T(8,128)}) %all-reduce.2.cloned.1.call-update) | async-done | bytes 69648 | tf_op jit(solution)/shard_map/psum | solution.py:135
  181.8 1.0 multiply_reduce_fusion.4
  182.8 1.0 multiply_reduce_fusion.2
  183.8 0.9 fusion.24
  184.7 2.2 fusion.30
  187.0 5.1 %gather_fusion.6 = f32[32,16,2048]{2,1,0:T(8,128)} fusion(f32[32,16,2048]{2,1,0:T(8,128)} %bitcast.3, s32[1024]{0:T(1024)S(1)} %pad_clamp_fusion), kind=kCustom, calls=%fused_computation.3.clone | custom fusion | bytes 8388736 | tf_op jit(solution)/shard_map/jit(_take)/gather | solution.py:106
  192.0 5.8 %multiply_reduce_fusion = (f32[32,2048]{1,0:T(8,128)S(1)}, f32[32,16,2048]{2,1,0:T(8,128)}) fusion(f32[32,16]{1,0:T(8,128)S(1)} %get-tuple-element.30, f32[32,16]{1,0:T(8,128)S(1)} %get-tuple-element.29, f32[32,2048]{1,0:T(8,128)S(1)} %get-tuple-element.28, f32[32,16,2048]{2,1,0:T(8,128)} %param.34, f32[32,16,2048]{2,1,0:T(8,128)} %gather_fusion.6, ...), kind=kLoop, calls=%fused_computation.16 | loop fusion | flops 8323072 | bytes 13504576 | tf_op jit(solution)/shard_map/reduce_sum | solution.py:150
  197.9 0.8 fusion.14
  198.7 27.7 %all-to-all-done.3 = bf16[16,2,512,256]{3,2,1,0:T(8,128)(2,1)} async-done(((bf16[16,2,512,256]{3,2,1,0:T(8,128)(2,1)}), bf16[16,2,512,256]{3,2,1,0:T(8,128)(2,1)}, u32[]{:S(2)}, u32[]{:S(2)}) %all-to-all-start.3) | async-done | bytes 8388640 | tf_op jit(solution)/shard_map/all_to_all | solution.py:119
  226.3 8.4 %gather_fusion.2 = bf16[32,512,256]{2,1,0:T(8,128)(2,1)} fusion(bf16[32,512,256]{2,1,0:T(8,128)(2,1)} %bitcast.8, s32[1024]{0:T(1024)S(1)} %pad_clamp_fusion), kind=kCustom, calls=%fused_computation.6 | custom fusion | bytes 16777344 | tf_op jit(solution)/shard_map/jit(_take)/gather | solution.py:106
  234.8 9.1 %select_select_fusion = bf16[32,512,256]{2,1,0:T(8,128)(2,1)} fusion(bf16[32,512,256]{2,1,0:T(8,128)(2,1)} %param.48, bf16[32,512,256]{2,1,0:T(8,128)(2,1)} %gather_fusion.2, pred[32]{0:T(512)(128)(4,1)S(1)} %get-tuple-element.25, pred[32]{0:T(512)(128)(4,1)S(1)} %get-tuple-element.31), kind=kLoop, calls=%fused_computation.7 | loop fusion | flops 8388608 | bytes 25165888 | tf_op jit(solution)/shard_map/jit(_where)/select_n | solution.py:108
  243.9 12.0 %copy.62 = bf16[32,512,256]{1,2,0:T(8,128)(2,1)} copy(bf16[32,512,256]{2,1,0:T(8,128)(2,1)} %select_select_fusion) | data formatting | bytes 16777216 | tf_op jit(solution)/shard_map/jit(_where)/select_n | solution.py:108
  255.8 3.1 %fusion.31 = (f32[32,8]{1,0:T(8,128)S(1)}, f32[32,8,512]{2,1,0:T(8,128)S(1)}) fusion(bf16[32,8,128]{2,1,0:T(8,128)(2,1)S(1)} %bitcast.68, bf16[32,512,1,2,128]{1,4,3,0,2:T(8,128)(2,1)} %bitcast.62, pred[32,512]{1,0:T(8,128)(4,1)S(1)} %iota_compare_fusion), kind=kOutput, calls=%fused_computation.85 | convolution fusion | flops 33947392 | bytes 4801536 | tf_op jit(solution)/shard_map/nkgd,ntkd->nkgt/dot_general | solution.py:18
  258.9 0.3 convert_reduce_fusion
  259.2 3.4 %fusion.10 = bf16[32,8,128]{2,1,0:T(8,128)(2,1)S(1)} fusion(bf16[32,512,1,2,128]{1,4,3,0,2:T(8,128)(2,1)} %bitcast.63, f32[32,8]{1,0:T(8,128)S(1)} %get-tuple-element.20, f32[32,128]{1,0:T(8,128)S(1)} %bitcast.71, f32[32,8]{1,0:T(8,128)S(1)} %get-tuple-element.22, f32[32,8]{1,0:T(8,128)S(1)} %get-tuple-element.21, f32[32,8,512]{2,1,0:T(8,128)S(1)} %get-tuple-element.33, ...), kind=kOutput, calls=%fused_computation.25 | convolution fusion | flops 34111488 | bytes 4820992 | tf_op jit(solution)/shard_map/nkgt,ntkd->nkgd/dot_general | solution.py:28
  262.6 0.7 copy.74
  (62 shorter events, 0.8 us)
Async XLA Ops:
  7.2 111.0 %copy-start = (bf16[2048,544]{0,1:T(8,128)(2,1)S(1)}, bf16[2048,544]{0,1:T(8,128)(2,1)}, u32[]{:S(2)}) copy-start(bf16[2048,544]{0,1:T(8,128)(2,1)} %param.38) | copy-start | bytes 6684676
  8.7 18.4 %all-to-all-start.2 = ((f32[16,1,2]{2,1,0:T(1,128)}), f32[16,1,2]{2,1,0:T(1,128)S(1)}, u32[]{:S(2)}, u32[]{:S(2)}) async-start(f32[16,1,2]{2,1,0:T(1,128)} %copy.59), calls=%async_computation.2 | async-start | bytes 16384 | tf_op jit(solution)/shard_map/all_to_all | solution.py:113
  27.1 15.1 %all-to-all-start = ((bf16[16,2,3,2048]{3,1,2,0:T(2,128)(2,1)}), bf16[16,2,3,2048]{3,1,2,0:T(2,128)(2,1)S(1)}, u32[]{:S(2)}, u32[]{:S(2)}) async-start(bf16[16,2,3,2048]{3,1,2,0:T(2,128)(2,1)} %copy.55), calls=%async_computation | async-start | bytes 786432 | tf_op jit(solution)/shard_map/all_to_all | solution.py:118
  42.2 0.7 copy-start.2
  42.2 5.3 %copy-start.6 = (s32[1,16,2,32]{3,2,1,0:T(2,128)S(1)}, s32[1,16,2,32]{3,2,1,0:T(2,128)}, u32[]{:S(2)}) copy-start(s32[1,16,2,32]{3,2,1,0:T(2,128)} %param.55) | copy-start | bytes 12292
  43.0 61.6 %all-to-all-start.1 = ((f32[16,2,16,2048]{3,2,1,0:T(8,128)}), f32[16,2,16,2048]{3,2,1,0:T(8,128)}, u32[]{:S(2)}, u32[]{:S(2)}) async-start(f32[16,2,16,2048]{3,2,1,0:T(8,128)} %bitcast.61), calls=%async_computation.1 | async-start | bytes 8388608 | tf_op jit(solution)/shard_map/all_to_all | solution.py:112
  67.5 42.1 %copy-start.7 = (bf16[32,1024]{1,0:T(8,128)(2,1)S(1)}, bf16[32,1024]{1,0:T(8,128)(2,1)}, u32[]{:S(2)}) copy-start(bf16[32,1024]{1,0:T(8,128)(2,1)} %param.46) | copy-start | bytes 196612
  67.5 42.1 %copy-start.10 = (bf16[32,256]{1,0:T(8,128)(2,1)S(1)}, bf16[32,256]{1,0:T(8,128)(2,1)}, u32[]{:S(2)}) copy-start(bf16[32,256]{1,0:T(8,128)(2,1)} %param.47) | copy-start | bytes 49156
  67.5 42.1 %copy-start.4 = (bf16[32,2048]{1,0:T(8,128)(2,1)S(1)}, bf16[32,2048]{1,0:T(8,128)(2,1)}, u32[]{:S(2)}) copy-start(bf16[32,2048]{1,0:T(8,128)(2,1)} %param.30) | copy-start | bytes 393220
  67.5 42.3 %copy-start.9 = (bf16[4,2048]{1,0:T(4,128)(2,1)S(1)}, bf16[4,2048]{1,0:T(4,128)(2,1)}, u32[]{:S(2)}) copy-start(bf16[4,2048]{1,0:T(4,128)(2,1)} %param.36) | copy-start | bytes 49156
  67.5 42.3 %copy-start.12 = (s32[32]{0:T(128)S(1)}, s32[32]{0:T(128)}, u32[]{:S(2)}) copy-start(s32[32]{0:T(128)} %param.51) | copy-start | bytes 388
  67.5 42.3 %copy-start.15 = (s32[32]{0:T(128)S(1)}, s32[32]{0:T(128)}, u32[]{:S(2)}) copy-start(s32[32]{0:T(128)} %param.52) | copy-start | bytes 388
  67.6 44.5 %copy-start.16 = (s32[32]{0:T(128)S(1)}, s32[32]{0:T(128)}, u32[]{:S(2)}) copy-start(s32[32]{0:T(128)} %param.50) | copy-start | bytes 388
  104.6 121.8 %all-to-all-start.3 = ((bf16[16,2,512,256]{3,2,1,0:T(8,128)(2,1)}), bf16[16,2,512,256]{3,2,1,0:T(8,128)(2,1)}, u32[]{:S(2)}, u32[]{:S(2)}) async-start(bf16[16,2,512,256]{3,2,1,0:T(8,128)(2,1)} %broadcast_select_fusion), calls=%async_computation.3 | async-start | bytes 16777216 | tf_op jit(solution)/shard_map/all_to_all | solution.py:119
  109.3 8.8 %copy-start.8 = (f32[2048]{0:T(1024)S(1)}, f32[2048]{0:T(1024)}, u32[]{:S(2)}) copy-start(f32[2048]{0:T(1024)} %param.37) | copy-start | bytes 24580
  109.3 72.5 %all-reduce.2.cloned.1.call-start = ((), (), s32[]{:S(2)}) async-start(), calls=%async_computation.4 | async-start | bytes 163840 | tf_op jit(solution)/shard_map/psum | solution.py:135
  113.5 70.3 %copy-start.13 = (f32[16]{0:T(128)S(1)}, f32[16]{0:T(128)}, u32[]{:S(2)}) copy-start(f32[16]{0:T(128)} %param.40) | copy-start | bytes 196
  113.5 70.3 %copy-start.14 = (f32[16]{0:T(128)S(1)}, f32[16]{0:T(128)}, u32[]{:S(2)}) copy-start(f32[16]{0:T(128)} %param.41) | copy-start | bytes 196
  113.5 71.2 %copy-start.17 = (f32[2048]{0:T(1024)S(1)}, f32[2048]{0:T(1024)}, u32[]{:S(2)}) copy-start(f32[2048]{0:T(1024)} %param.43) | copy-start | bytes 24580
  113.5 71.2 %copy-start.18 = (f32[512]{0:T(512)S(1)}, f32[512]{0:T(512)}, u32[]{:S(2)}) copy-start(f32[512]{0:T(512)} %param.39) | copy-start | bytes 6148
  187.0 5.1 %copy-start.3 = (f32[16,2048]{1,0:T(8,128)S(1)}, f32[16,2048]{1,0:T(8,128)}, u32[]{:S(2)}) copy-start(f32[16,2048]{1,0:T(8,128)} %param.44) | copy-start | bytes 393220
  192.0 5.8 %copy-start.5 = (bf16[32,2048]{1,0:T(8,128)(2,1)S(1)}, bf16[32,2048]{1,0:T(8,128)(2,1)}, u32[]{:S(2)}) copy-start(bf16[32,2048]{1,0:T(8,128)(2,1)} %param.31) | copy-start | bytes 393220
  192.0 5.8 %copy-start.11 = (f32[2048]{0:T(1024)S(1)}, f32[2048]{0:T(1024)}, u32[]{:S(2)}) copy-start(f32[2048]{0:T(1024)} %param.45) | copy-start | bytes 24580
  255.8 7.4 %copy-start.1 = (bf16[2048,544]{0,1:T(8,128)(2,1)S(1)}, bf16[2048,544]{0,1:T(8,128)(2,1)}, u32[]{:S(2)}) copy-start(bf16[2048,544]{0,1:T(8,128)(2,1)} %param.38) | copy-start | bytes 6684676
Sparse Core Ops, SparseCore 0:
  119.7 62.0 all-reduce.1
where the time goes:
time: 275 us; the launch traced here: 270 us
  waiting for transfers between devices  129 us (47%)
  local copies, waits for them, and re-layouts  55 us (20%)
  other arithmetic  37.1 us (13%)
  starting transfers between devices  24.6 us (9%)
  between operations  14.5 us (5%)
  matrix products  10.3 us (4%)
    psum x1, waiting for transfers between devices, shards(): proj = lax.psum(proj_part, 'tp')  60.5 us
    all_to_all x1, waiting for transfers between devices, shards(): lax.all_to_all(ssm_send, 'rep', split_axis=0, concat_axis=0, tiled=True)  37 us
    all_to_all x1, waiting for transfers between devices, shards(): lax.all_to_all(page_send, 'rep', split_axis=0, concat_axis=0, tiled=True)  27.7 us
    gather x3, local copies, waits for them, and re-layouts, pick_rows(): picked = jnp.take(flat, where_from, axis=0)  15.2 us
    select_n x1, local copies, waits for them, and re-layouts, pick_rows(): return jnp.where(flag, picked, local_rows)  12 us
    gather x1, local copies, waits for them, and re-layouts, shards(): jnp.take(kv_pool, page_list, axis=0)  11.2 us
    select_n x2, other arithmetic, pick_rows(): return jnp.where(flag, picked, local_rows)  10.8 us
    all_to_all x1, starting transfers between devices, shards(): lax.all_to_all(swap_lens[0].astype(jnp.float32), 'rep', split_axis=0, con...  8.43 us
  transfers between devices with their start and end apart: 5, of which 4 were waited for; matrix products, arithmetic and copies ran while one was open for 23% of the time, Pallas kernels for 0%

commit v1 on v0

v1 whole, which is shorter than its diff:
```python
import functools
import math

import jax
import jax.numpy as jnp
from jax import lax
from jax.experimental import pallas as pl
from jax.experimental.pallas import tpu as pltpu
from jax.sharding import PartitionSpec as P

BF = jnp.bfloat16
F32 = jnp.float32
I32 = jnp.int32
PEERS = 16
CAP = 2
ENT = PEERS * CAP
ROWS = 32
EC = 2048
HALF = EC // 2
NS = 16
RANK = 512
HEADS = 8
HD = 128
CTX = 512
PAGE = 16
POOL = 256
TOK = POOL * PAGE
CHUNK = 256
LOG2E = 1.4426950408889634
LN2 = 0.6931471805599453
NEG = -1e30

VM = pl.BlockSpec(memory_space=pltpu.VMEM)
SM = pl.BlockSpec(memory_space=pltpu.SMEM)
HB = pl.BlockSpec(memory_space=pl.ANY)


def iota(shape, dim):
    return lax.broadcasted_iota(I32, shape, dim)


def params(mib):
    return pltpu.CompilerParams(vmem_limit_bytes=mib * 1024 * 1024)


def cost(flops, byts):
    return pl.CostEstimate(flops=flops, bytes_accessed=byts, transcendentals=0)


def source_of(owner_ref, pos_ref, r):
    owner = owner_ref[r]
    return jnp.where(owner >= 0, owner * CAP + pos_ref[r], -1)


def pack_kernel(slot_ref, owner_ref, pos_ref, conv_ref, query_ref, out_ref, stack, inverse):
    for j in range(3):
        for h in range(2):
            stack[32 * (2 * j + h) : 32 * (2 * j + h) + 32, :] = conv_ref[
                j, :, h * HALF : (h + 1) * HALF
            ]
    stack[192:224, :] = query_ref[...]
    stack[224:256, :] = jnp.zeros((32, HALF), BF)
    for e in range(ENT):
        inverse[e] = -1
    for r in range(ROWS):
        owner = owner_ref[r]

        @pl.when(owner >= 0)
        def _():
            inverse[owner * CAP + pos_ref[r]] = 192 + r

    lane = iota((8, 256), 1)
    part = iota((8, 256), 0)
    tiles = []
    for e in range(ENT):
        slot = slot_ref[0, e % CAP, e // CAP]
        want = jnp.where(part < 6, 32 * part + slot, jnp.where(part == 6, inverse[e], -1))
        tiles.append((lane == want).astype(F32))
    pick = jnp.concatenate(tiles, axis=0).astype(BF)
    packed = jnp.dot(pick, stack[...], preferred_element_type=F32).astype(BF)
    out_ref[...] = packed.reshape(PEERS, 16, HALF)


def pack(slots, owner, pos, conv_pool, query):
    return pl.pallas_call(
        pack_kernel,
        out_shape=jax.ShapeDtypeStruct((PEERS, 16, HALF), BF),
        in_specs=[SM, SM, SM, VM, VM],
        out_specs=VM,
        scratch_shapes=[pltpu.VMEM((256, HALF), BF), pltpu.SMEM((ENT,), I32)],
        compiler_params=params(16),
        cost_estimate=cost(2 * 256 * 256 * HALF, 1 << 20),
        name="pack_first",
    )(slots, owner, pos, conv_pool, query)


def gather_kernel(slot_ref, pool_ref, out_ref, buf, sems):
    def copy(e):
        return pltpu.make_async_copy(
            pool_ref.at[slot_ref[0, e % CAP, e // CAP]], buf.at[e], sems.at[e]
        )

    for e in range(ENT):
        copy(e).start()

    for e in range(ENT):
        copy(e).wait()
        out_ref[e] = buf[e].astype(BF)


def gather_states(slots, ssm_pool):
    return pl.pallas_call(
        gather_kernel,
        out_shape=jax.ShapeDtypeStruct((ENT, NS, EC), BF),
        in_specs=[SM, HB],
        out_specs=VM,
        scratch_shapes=[pltpu.VMEM((ENT, NS, EC), F32), pltpu.SemaphoreType.DMA((ENT,))],
        compiler_params=params(16),
        cost_estimate=cost(1 << 20, 6 << 20),
        name="gather_states",
    )(slots, ssm_pool)


def weigh_kernel(pages_ref, lens_ref, pool_ref, weight_ref, vt_ref, count):
    lens = lens_ref[...]
    full = lens // PAGE
    rest = lens - full * PAGE
    page_id = iota((POOL, 128), 0)
    total = jnp.zeros((POOL, 128), F32)
    last = jnp.full((1, 128), -1, I32)
    for j in range(CTX // PAGE):
        page = pages_ref[j : j + 1, :]
        total += jnp.where(page_id == jnp.where(j < full, page, -1), 1.0, 0.0)
        last = jnp.where(j == full, page, last)
    count[...] = total
    token = iota((PAGE, 128), 0)
    tail = jnp.where(token < rest, 1.0, 0.0)

    def body(p, carry):
        here = jnp.broadcast_to(count[pl.ds(p, 1), :], (PAGE, 128))
        here += jnp.where(last == p, tail, 0.0)
        weight_ref[p] = here.astype(BF)
        return carry

    lax.fori_loop(0, POOL, body, 0, unroll=8)
    for c in range(TOK // CHUNK):
        pages = CHUNK // PAGE
        values = pool_ref[c * pages : (c + 1) * pages, :, HD:].reshape(CHUNK, HD)
        vt_ref[:, c * CHUNK : (c + 1) * CHUNK] = values.astype(F32).T.astype(BF)


def weigh(pages, lens, kv_pool):
    return pl.pallas_call(
        weigh_kernel,
        out_shape=(
            jax.ShapeDtypeStruct((POOL, PAGE, 128), BF),
            jax.ShapeDtypeStruct((HD, TOK), BF),
        ),
        in_specs=[VM, VM, VM],
        out_specs=(VM, VM),
        scratch_shapes=[pltpu.VMEM((POOL, 128), F32)],
        compiler_params=params(16),
        cost_estimate=cost(1 << 20, 6 << 20),
        name="weigh_pool",
    )(pages, lens, kv_pool)


def serve_kernel(recv_ref, pool_ref, weight_ref, vt_ref, out_ref, scores, back):
    lane = iota((ENT, 256), 1)
    pick = (lane == 8 * iota((ENT, 256), 0) + 6).astype(F32).astype(BF)
    recv = recv_ref[...].reshape(256, HALF)
    query = jnp.dot(pick, recv, preferred_element_type=F32).astype(BF)
    query = jnp.concatenate([query[:, h * HD : (h + 1) * HD] for h in range(HEADS)], axis=0)
    scale = LOG2E / math.sqrt(HD)
    pages = CHUNK // PAGE

    def first(c, top):
        keys = pool_ref[pl.ds(c * pages, pages), :, 0:HD].reshape(CHUNK, HD)
        raw = lax.dot_general(keys, query, (((1,), (1,)), ((), ())), preferred_element_type=F32)
        weight = weight_ref[pl.ds(c * pages, pages)].reshape(CHUNK, 128).astype(F32)
        weight = jnp.concatenate([weight, weight], axis=1)
        raw = jnp.where(weight > 0.0, raw * scale, NEG)
        scores[pl.ds(c * CHUNK, CHUNK), :] = raw
        return jnp.maximum(top, jnp.max(raw.reshape(CHUNK // 8, 8, 256), axis=0))

    top = lax.fori_loop(0, TOK // CHUNK, first, jnp.full((8, 256), NEG, F32))
    top = jnp.max(top, axis=0, keepdims=True)

    def second(c, carry):
        total, mix = carry
        raw = scores[pl.ds(c * CHUNK, CHUNK), :]
        weight = weight_ref[pl.ds(c * pages, pages)].reshape(CHUNK, 128).astype(F32)
        weight = jnp.concatenate([weight, weight], axis=1)
        prob = (jnp.exp2(raw - top) * weight).astype(BF)
        total += jnp.sum(prob.astype(F32).reshape(CHUNK // 8, 8, 256), axis=0)
        start = pl.multiple_of(c * CHUNK, CHUNK)
        mix += jnp.dot(vt_ref[:, pl.ds(start, CHUNK)], prob, preferred_element_type=F32)
        return total, mix

    total, mix = lax.fori_loop(
        0, TOK // CHUNK, second, (jnp.zeros((8, 256), F32), jnp.zeros((HD, 256), F32))
    )
    total = jnp.sum(total, axis=0, keepdims=True)
    lse = top * LN2 + jnp.log(total)
    high = lse.astype(BF).astype(F32)
    mid = (lse - high).astype(BF).astype(F32)
    low = lse - high - mid
    row = iota((HD, 256), 0)
    pieces = jnp.where(row < 32, high, jnp.where(row < 64, mid, low))
    mix = (mix * (1.0 / total)).T
    pieces = pieces.T
    for h in range(HEADS):
        back[pl.ds(h, ENT, 16), :] = mix[h * ENT : (h + 1) * ENT, :]
        back[pl.ds(8 + h, ENT, 16), :] = pieces[h * ENT : (h + 1) * ENT, :]
    out_ref[...] = back[...].astype(BF).reshape(PEERS, 32, HD)


def serve(recv, kv_pool, weight, vt):
    return pl.pallas_call(
        serve_kernel,
        out_shape=jax.ShapeDtypeStruct((PEERS, 32, HD), BF),
        in_specs=[VM] * 4,
        out_specs=VM,
        scratch_shapes=[pltpu.VMEM((TOK, 256), F32), pltpu.VMEM((ENT * 16, HD), F32)],
        compiler_params=params(24),
        cost_estimate=cost(4 * TOK * 256 * HD, 6 << 20),
        name="serve_pool",
    )(recv, kv_pool, weight, vt)


BLK = 4


def resident_kernel(len_ref, query_ref, new_ref, cache_ref, mix_ref, lse_ref, score_ref, heads):
    step = pl.program_id(0)

    @pl.when(step == 0)
    def _():
        for h in range(HEADS):
            heads[pl.ds(h, ROWS, 8), :] = query_ref[:, h * HD : (h + 1) * HD].astype(F32)

    scale = LOG2E / math.sqrt(HD)
    token = iota((8, CTX), 1)
    for b in range(BLK):
        r = step * BLK + b
        wide = heads[pl.ds(pl.multiple_of(r * 8, 8), 8), :]
        query = wide.astype(BF)
        keys = cache_ref[b, :, 0:HD]
        raw = lax.dot_general(query, keys, (((1,), (1,)), ((), ())), preferred_element_type=F32)
        live = token < len_ref[r]
        raw = jnp.where(live, raw * scale, NEG)
        top = jnp.max(raw, axis=1, keepdims=True)
        prob = jnp.where(live, jnp.exp2(raw - top), 0.0).astype(BF)
        total = jnp.sum(prob.astype(F32), axis=1, keepdims=True)
        mix = jnp.dot(prob, cache_ref[b, :, HD:], preferred_element_type=F32)
        mix_ref[b] = mix * (1.0 / total)
        lse_ref[b] = jnp.broadcast_to(top * LN2 + jnp.log(total), (8, HD))
        new = jnp.sum(wide * new_ref[b], axis=1, keepdims=True) * (1.0 / math.sqrt(HD))
        score_ref[b] = jnp.broadcast_to(new, (8, HD))


def resident(lens, query, new_key, kv_cache):
    tile = pl.BlockSpec((BLK, 8, HD), lambda i: (i, 0, 0))
    shape = jax.ShapeDtypeStruct((ROWS, 8, HD), F32)
    return pl.pallas_call(
        resident_kernel,
        grid=(ROWS // BLK,),
        out_shape=(shape, shape, shape),
        in_specs=[
            SM,
            pl.BlockSpec((ROWS, HEADS * HD), lambda i: (0, 0)),
            pl.BlockSpec((BLK, 1, HD), lambda i: (i, 0, 0)),
            pl.BlockSpec((BLK, CTX, 2 * HD), lambda i: (i, 0, 0)),
        ],
        out_specs=(tile, tile, tile),
        scratch_shapes=[pltpu.VMEM((ROWS * 8, HD), F32)],
        compiler_params=params(16),
        cost_estimate=cost(4 * ROWS * 8 * CTX * HD, 9 << 20),
        name="resident_attention",
    )(lens, query, new_key, kv_cache)


def mix_kernel(
    owner_ref, pos_ref, recv_ref, conv_ref, x_ref, weight_ref, bias_ref, proj_ref,
    mixed_ref, window_ref, part_ref, send_ref,
):
    sub = iota((ROWS, 256), 0)
    lane = iota((ROWS, 256), 1)
    source = jnp.full((ROWS, 256), -1, I32)
    for r in range(ROWS):
        source = jnp.where(sub == r, source_of(owner_ref, pos_ref, r), source)
    base = jnp.where(source >= 0, source * 8, -8)
    pick = jnp.concatenate([(lane == base + k).astype(F32) for k in range(6)], axis=0).astype(BF)
    recv = recv_ref[...].reshape(256, HALF)
    prev = jnp.dot(pick, recv, preferred_element_type=F32)
    came = source[:, 0:1] >= 0
    x = x_ref[...]
    total = x.astype(F32) * weight_ref[3:4, :].astype(F32)
    window_ref[2] = x
    for j in range(3):
        here = jnp.concatenate(
            [prev[64 * j : 64 * j + 32], prev[64 * j + 32 : 64 * j + 64]], axis=1
        )
        tap = jnp.where(came, here, conv_ref[j].astype(F32))
        if j > 0:
            window_ref[j - 1] = tap.astype(BF)
        total += tap * weight_ref[j : j + 1, :].astype(F32)
    total += bias_ref[...]
    mixed = (total / (1.0 + jnp.exp(-total))).astype(BF)
    mixed_ref[...] = mixed
    part = lax.dot_general(
        mixed, proj_ref[...], (((1,), (1,)), ((), ())), preferred_element_type=F32
    )
    part_ref[...] = part
    send_ref[...] = part.astype(BF)


def mix(owner, pos, recv, conv_state, x_in, weight, bias, proj_t):
    wide = proj_t.shape[0]
    return pl.pallas_call(
        mix_kernel,
        out_shape=(
            jax.ShapeDtypeStruct((ROWS, EC), BF),
            jax.ShapeDtypeStruct((3, ROWS, EC), BF),
            jax.ShapeDtypeStruct((ROWS, wide), F32),
            jax.ShapeDtypeStruct((ROWS, wide), BF),
        ),
        in_specs=[SM, SM] + [VM] * 6,
        out_specs=(VM, VM, VM, VM),
        compiler_params=params(16),
        cost_estimate=cost(2 * ROWS * EC * wide, 4 << 20),
        name="mix_input",
    )(owner, pos, recv, conv_state, x_in, weight, bias, proj_t)


def step_kernel(*refs):
    part_ref = refs[0]
    others = refs[1:8]
    gain_ref, tail_gain_ref, proj_ref, bias_ref, mixed_ref, dt_ref, drive_ref, tail_ref = refs[8:]
    proj = part_ref[...]
    for other in others:
        proj += other[...].astype(F32)
    low = proj[:, 0:RANK]
    mean = jnp.sum(low * low, axis=1, keepdims=True) * (1.0 / RANK)
    normed = (low * lax.rsqrt(mean + 1e-6) * gain_ref[...]).astype(BF)
    dt = jnp.dot(normed, proj_ref[...], preferred_element_type=F32) + bias_ref[...]
    dt = jnp.maximum(dt, 0.0) + jnp.log1p(jnp.exp(-jnp.abs(dt)))
    dt_ref[...] = dt
    drive_ref[...] = dt * mixed_ref[...].astype(F32)
    tail = proj[:, RANK : RANK + 2 * NS]
    square = tail * tail
    front = iota((ROWS, 2 * NS), 1) < NS
    mean_b = jnp.sum(jnp.where(front, square, 0.0), axis=1, keepdims=True) * (1.0 / NS)
    mean_c = jnp.sum(jnp.where(front, 0.0, square), axis=1, keepdims=True) * (1.0 / NS)
    scale = lax.rsqrt(jnp.where(front, mean_b, mean_c) + 1e-6)
    tail_ref[...] = (tail * scale * tail_gain_ref[...]).astype(BF).astype(F32)


def step_size(part, others, gain, tail_gain, proj, bias, mixed):
    return pl.pallas_call(
        step_kernel,
        out_shape=(
            jax.ShapeDtypeStruct((ROWS, EC), F32),
            jax.ShapeDtypeStruct((ROWS, EC), F32),
            jax.ShapeDtypeStruct((ROWS, 2 * NS), F32),
        ),
        in_specs=[VM] * 13,
        out_specs=(VM, VM, VM),
        compiler_params=params(16),
        cost_estimate=cost(2 * ROWS * EC * RANK, 3 << 20),
        name="step_size",
    )(part, *others, gain, tail_gain, proj, bias, mixed)


GROUP = 8


def state_kernel(
    owner_ref, pos_ref, recv_ref, state_ref, dt_ref, drive_ref, tail_ref, decay_ref, skip_ref,
    z_ref, mixed_ref, new_ref, out_ref, local, prev, made, read, in_sems, out_sems,
):
    def fetch(r):
        return pltpu.make_async_copy(state_ref.at[r], local.at[r], in_sems.at[r])

    def store(i):
        rows = pl.ds(pl.multiple_of(i * GROUP, GROUP), GROUP)
        return pltpu.make_async_copy(made.at[i], new_ref.at[rows], out_sems.at[i])

    def begin(r, carry):
        @pl.when(owner_ref[r] < 0)
        def _():
            fetch(r).start()

        return carry

    lax.fori_loop(0, ROWS, begin, 0)

    def body(i, carry):
        for b in range(GROUP):
            r = i * GROUP + b
            source = source_of(owner_ref, pos_ref, r)

            @pl.when(source >= 0)
            def _():
                prev[b] = recv_ref[jnp.maximum(source, 0)].astype(F32)

            @pl.when(source < 0)
            def _():
                fetch(r).wait()
                prev[b] = local[r]

        rows = pl.ds(pl.multiple_of(i * GROUP, GROUP), GROUP)

        def column(c, inner):
            cols = pl.ds(pl.multiple_of(c * 128, 128), 128)
            dt = dt_ref[rows, cols]
            drive = drive_ref[rows, cols]
            decay = decay_ref[:, cols]
            sums = []
            for b in range(GROUP):
                r = i * GROUP + b
                inject = tail_ref[r, 0:NS, :]
                read_out = tail_ref[r, NS:, :]
                keep = jnp.exp(-dt[b : b + 1, :] * decay)
                new = keep * prev[b, :, cols] + drive[b : b + 1, :] * inject
                made[i, b, :, cols] = new
                sums.append(jnp.sum(new * read_out, axis=0, keepdims=True))
            read[rows, cols] = jnp.concatenate(sums, axis=0)
            return inner

        lax.fori_loop(0, EC // 128, column, 0)
        store(i).start()
        return carry

    lax.fori_loop(0, ROWS // GROUP, body, 0)
    z = z_ref[...].astype(F32)
    gate = z / (1.0 + jnp.exp(-z))
    mixed = mixed_ref[...].astype(F32)
    out_ref[...] = ((read[...] + skip_ref[...] * mixed) * gate).astype(BF)
    for i in range(ROWS // GROUP):
        store(i).wait()


def update_state(owner, pos, recv, state, dt, drive, tail, decay, skip, z, mixed):
    return pl.pallas_call(
        state_kernel,
        out_shape=(
            jax.ShapeDtypeStruct((ROWS, NS, EC), F32),
            jax.ShapeDtypeStruct((ROWS, EC), BF),
        ),
        in_specs=[SM, SM, VM, HB] + [VM] * 7,
        out_specs=(HB, VM),
        scratch_shapes=[
            pltpu.VMEM((ROWS, NS, EC), F32),
            pltpu.VMEM((GROUP, NS, EC), F32),
            pltpu.VMEM((ROWS // GROUP, GROUP, NS, EC), F32),
            pltpu.VMEM((ROWS, EC), F32),
            pltpu.SemaphoreType.DMA((ROWS,)),
            pltpu.SemaphoreType.DMA((ROWS // GROUP,)),
        ],
        compiler_params=params(24),
        cost_estimate=cost(16 << 20, 10 << 20),
        name="update_state",
    )(owner, pos, recv, state, dt, drive, tail, decay, skip, z, mixed)


def finish_kernel(
    owner_ref, pos_ref, recv_ref, mix_ref, lse_ref, score_ref, value_ref, out_ref, made, part
):
    for r in range(ROWS):
        source = source_of(owner_ref, pos_ref, r)
        tile = recv_ref[jnp.maximum(source, 0)].astype(F32)
        there = tile[8:16, 0:1] + tile[8:16, 32:33] + tile[8:16, 64:65]
        came = source >= 0
        lse = jnp.where(came, there, lse_ref[r])
        mix = jnp.where(came, tile[0:8, :], mix_ref[r])
        score = score_ref[r]
        peak = jnp.maximum(lse, score)
        old = jnp.exp(lse - peak)
        new = jnp.exp(score - peak)
        value = value_ref[r]
        made[8 * r : 8 * r + 8, :] = (mix * old + new * value) / (old + new)
    for h in range(HEADS):
        out_ref[:, h * HD : (h + 1) * HD] = made[pl.ds(h, ROWS, 8), :].astype(BF)


def finish(owner, pos, recv, mix, lse, score, value):
    return pl.pallas_call(
        finish_kernel,
        out_shape=jax.ShapeDtypeStruct((ROWS, HEADS * HD), BF),
        in_specs=[SM, SM] + [VM] * 5,
        out_specs=VM,
        scratch_shapes=[pltpu.VMEM((ROWS * 8, HD), F32), pltpu.VMEM((8, HD), F32)],
        compiler_params=params(16),
        cost_estimate=cost(1 << 16, 1 << 19),
        name="join_new_token",
    )(owner, pos, recv, mix, lse, score, value)


def swap(values):
    return lax.all_to_all(values, "rep", split_axis=0, concat_axis=0, tiled=True)


def shards(
    x_in, z_gate, conv_state, conv_pool, ssm_state, ssm_pool, conv_weight, conv_bias, x_proj,
    dt_gain, b_gain, c_gain, dt_proj, dt_bias, decay_rate, skip, query, new_kv, kv_cache, kv_pool,
    ctx_len, row_owner, row_pos, swap_slot, swap_lens, swap_pages,
):
    slots = swap_slot.transpose(0, 2, 1)
    first = swap(pack(slots, row_owner, row_pos, conv_pool.transpose(1, 0, 2), query))
    states = gather_states(slots, ssm_pool)
    second = swap(states.reshape(PEERS, CAP, NS, EC)).reshape(ENT, NS, EC)

    new_key = new_kv[:, None, 0:HD].astype(F32)
    new_value = new_kv[:, None, HD:].astype(F32)
    mix_here, lse_here, score = resident(ctx_len, query, new_key, kv_cache)
    pages = jnp.tile(swap_pages[0].reshape(ENT, CTX // PAGE).T, (1, 4))
    lens = jnp.tile(swap_lens[0].reshape(1, ENT), (1, 4))
    weight, vt = weigh(pages, lens, kv_pool)
    served = serve(first, kv_pool, weight, vt)
    third = swap(served).reshape(ENT, 16, HD)

    mixed, window, part, send = mix(
        row_owner, row_pos, first, conv_state.transpose(1, 0, 2), x_in, conv_weight,
        conv_bias.reshape(1, EC), x_proj.T,
    )
    tp = lax.axis_size("tp")
    others = [
        lax.ppermute(send, "tp", [(i, (i + s) % tp) for i in range(tp)]) for s in range(1, tp)
    ]
    dt, drive, tail = step_size(
        part, others, dt_gain.reshape(1, RANK), jnp.concatenate([b_gain, c_gain]).reshape(1, 2 * NS),
        dt_proj, dt_bias.reshape(1, EC), mixed,
    )
    tail = jnp.broadcast_to(tail[:, :, None], (ROWS, 2 * NS, 128))
    new_ssm, mamba_out = update_state(
        row_owner, row_pos, second, ssm_state, dt, drive, tail, decay_rate, skip.reshape(1, EC),
        z_gate, mixed,
    )
    attn_out = finish(row_owner, row_pos, third, mix_here, lse_here, score, new_value)
    return (mamba_out, attn_out, new_ssm, window.transpose(1, 0, 2))


def solution(mesh):
    in_specs = (
        P("rep", "tp"), P("rep", "tp"), P("rep", None, "tp"), P("rep", None, "tp"),
        P("rep", None, "tp"), P("rep", None, "tp"), P(None, "tp"), P("tp"), P("tp", None),
        P(), P(), P(), P(None, "tp"), P("tp"), P(None, "tp"), P("tp"), P("rep", "tp"),
        P("rep", "tp"), P("rep", None, "tp"), P("rep", None, "tp"), P("rep"), P("rep"), P("rep"),
        P("rep", None, None), P("rep", None, None), P("rep", None, None, None),
    )
    out_specs = (P("rep", "tp"), P("rep", "tp"), P("rep", None, "tp"), P("rep", None, "tp"))
    return jax.shard_map(shards, mesh=mesh, in_specs=in_specs, out_specs=out_specs, check_vma=False)
```

time: 275 us -> 97 us (0.35)
  the two profiles are of different devices: /device:TPU:1 before, /device:TPU:0 now
where the time goes in v1:
time: 97 us; the launch traced here: 95.6 us
  Pallas kernels  37.6 us (39%)
  starting transfers between devices  26.6 us (27%)
  local copies, waits for them, and re-layouts  21.2 us (22%)
  waiting for transfers between devices  9.17 us (9%)
  between operations  1.03 us (1%)
    unnamed x67, local copies, waits for them, and re-layouts  19.9 us
    all_to_all x3, starting transfers between devices, swap(): lax.all_to_all(values, 'rep', split_axis=0, concat_axis=0, tiled=True)  18.8 us
    all_to_all x3, waiting for transfers between devices, swap(): lax.all_to_all(values, 'rep', split_axis=0, concat_axis=0, tiled=True)  9.15 us
    pallas_call x1, Pallas kernels, resident(): pl.pallas_call(resident_kernel, grid=(ROWS // BLK,), out_shape=(shape, sh...  9.13 us
    pallas_call x1, Pallas kernels, update_state(): pl.pallas_call(state_kernel, out_shape=(jax.ShapeDtypeStruct((ROWS, NS, E...  7.86 us
    ppermute x7, starting transfers between devices, shards(): lax.ppermute(send, 'tp', [(i, (i + s) % tp) for i in range(tp)])  7.82 us
    pallas_call x1, Pallas kernels, serve(): pl.pallas_call(serve_kernel, out_shape=jax.ShapeDtypeStruct((PEERS, 32, H...  7.24 us
    pallas_call x1, Pallas kernels, gather_states(): pl.pallas_call(gather_kernel, out_shape=jax.ShapeDtypeStruct((ENT, NS, EC...  6.63 us
  transfers between devices with their start and end apart: 10, of which 2 were waited for; matrix products, arithmetic and copies ran while one was open for 2% of the time, Pallas kernels for 22%

profile of v1, /device:TPU:0, one launch (start us, length us, event | category | flops | bytes accessed | tf_op | source)
XLA Modules:
  0.0 95.6 jit_solution(4120247274616054520)
XLA Ops:
  0.7 1.1 %copy-done.12 = bf16[32,3,2048]{2,0,1:T(8,128)(2,1)S(1)} copy-done((bf16[32,3,2048]{2,0,1:T(8,128)(2,1)S(1)}, bf16[32,3,2048]{2,0,1:T(8,128)(2,1)}, u32[]{:S(2)}) %copy-start.12) | copy-done | bytes 393240
  1.8 0.8 copy-done.13
  2.6 0.7 copy-done.22
  3.3 0.7 copy-done.24
  3.9 0.7 copy-done.26
  4.6 1.8 %pack_first.1 = bf16[16,16,1024]{2,1,0:T(8,128)(2,1)} custom-call(s32[1,2,16]{2,1,0:T(2,128)S(1)} %bitcast.30, s32[32]{0:T(128)S(1)} %copy-done.22, s32[32]{0:T(128)S(1)} %copy-done.24, bf16[3,32,2048]{2,1,0:T(8,128)(2,1)S(1)} %bitcast.24, bf16[32,1024]{1,0:T(8,128)(2,1)S(1)} %copy-done.13), custom_call_target="tpu_custom_call" | custom-call | flops 134217728 | bytes 1048576 | tf_op jit(solution)/shard_map/pack_first/pallas_call | solution.py:85
  6.4 8.0 %all-to-all-start.1 = ((bf16[16,16,1024]{2,1,0:T(8,128)(2,1)}), bf16[16,16,1024]{2,1,0:T(8,128)(2,1)S(1)}, u32[]{:S(2)}, u32[]{:S(2)}) async-start(bf16[16,16,1024]{2,1,0:T(8,128)(2,1)} %pack_first.1), calls=%async_computation.1 | async-start | bytes 1048576 | tf_op jit(solution)/shard_map/all_to_all | solution.py:501
  14.3 0.8 copy.33
  15.1 0.1 tile.21
  15.2 0.1 tile.23.lens_ref
  15.3 0.8 copy.32
  16.1 0.1 tile.20.pages_ref
  16.2 1.2 %weigh_pool.1 = (bf16[256,16,128]{2,1,0:T(8,128)(2,1)S(1)}, bf16[128,4096]{1,0:T(8,128)(2,1)S(1)}) custom-call(s32[32,128]{1,0:T(8,128)S(1)} %tile.20.pages_ref, s32[1,128]{1,0:T(1,128)S(1)} %tile.23.lens_ref, bf16[256,16,256]{2,1,0:T(8,128)(2,1)S(1)} %copy-done), custom_call_target="tpu_custom_call" | custom-call | flops 1048576 | bytes 6291456 | tf_op jit(solution)/shard_map/weigh_pool/pallas_call | solution.py:153
  17.4 0.0 copy-start.7
  17.5 1.0 %copy-done.7 = bf16[256,16,128]{2,1,0:T(8,128)(2,1)} copy-done((bf16[256,16,128]{2,1,0:T(8,128)(2,1)}, bf16[256,16,128]{2,1,0:T(8,128)(2,1)S(1)}, u32[]{:S(2)}) %copy-start.7) | copy-done | bytes 1048600
  18.4 1.0 %copy-done.9 = bf16[128,4096]{1,0:T(8,128)(2,1)} copy-done((bf16[128,4096]{1,0:T(8,128)(2,1)}, bf16[128,4096]{1,0:T(8,128)(2,1)S(1)}, u32[]{:S(2)}) %copy-start.9) | copy-done | bytes 1048600
  19.4 6.5 %all-to-all-done.1.recv_ref = bf16[16,16,1024]{2,1,0:T(8,128)(2,1)S(1)} async-done(((bf16[16,16,1024]{2,1,0:T(8,128)(2,1)}), bf16[16,16,1024]{2,1,0:T(8,128)(2,1)S(1)}, u32[]{:S(2)}, u32[]{:S(2)}) %all-to-all-start.1) | async-done | bytes 524320 | tf_op jit(solution)/shard_map/all_to_all | solution.py:501
  25.9 1.2 %copy-done.8 = bf16[256,16,128]{2,1,0:T(8,128)(2,1)S(1)} copy-done((bf16[256,16,128]{2,1,0:T(8,128)(2,1)S(1)}, bf16[256,16,128]{2,1,0:T(8,128)(2,1)}, u32[]{:S(2)}) %copy-start.8) | copy-done | bytes 1048600
  27.1 1.2 %copy-done.10 = bf16[128,4096]{1,0:T(8,128)(2,1)S(1)} copy-done((bf16[128,4096]{1,0:T(8,128)(2,1)S(1)}, bf16[128,4096]{1,0:T(8,128)(2,1)}, u32[]{:S(2)}) %copy-start.10) | copy-done | bytes 1048600
  28.3 7.2 %serve_pool.1 = bf16[16,32,128]{2,1,0:T(8,128)(2,1)} custom-call(bf16[16,16,1024]{2,1,0:T(8,128)(2,1)S(1)} %all-to-all-done.1.recv_ref, bf16[256,16,256]{2,1,0:T(8,128)(2,1)S(1)} %copy-done, bf16[256,16,128]{2,1,0:T(8,128)(2,1)S(1)} %copy-done.8, bf16[128,4096]{1,0:T(8,128)(2,1)S(1)} %copy-done.10), custom_call_target="tpu_custom_call" | custom-call | flops 536870912 | bytes 6291456 | tf_op jit(solution)/shard_map/serve_pool/pallas_call | solution.py:219
  35.6 3.5 %all-to-all-start.2 = ((bf16[16,32,128]{2,1,0:T(8,128)(2,1)}), bf16[16,32,128]{2,1,0:T(8,128)(2,1)S(1)}, u32[]{:S(2)}, u32[]{:S(2)}) async-start(bf16[16,32,128]{2,1,0:T(8,128)(2,1)} %serve_pool.1), calls=%async_computation.2 | async-start | bytes 262144 | tf_op jit(solution)/shard_map/all_to_all | solution.py:501
  39.1 2.2 %copy-done.4 = f32[32,16,2048]{2,1,0:T(8,128)S(1)} copy-done((f32[32,16,2048]{2,1,0:T(8,128)S(1)}, f32[32,16,2048]{2,1,0:T(8,128)}, u32[]{:S(2)}) %copy-start.4) | copy-done | bytes 4194328
  41.3 6.6 %gather_states.1 = bf16[32,16,2048]{2,1,0:T(8,128)(2,1)S(1)} custom-call(s32[1,2,16]{2,1,0:T(2,128)S(1)} %bitcast.31, f32[32,16,2048]{2,1,0:T(8,128)S(1)} %copy-done.4), custom_call_target="tpu_custom_call" | custom-call | flops 1048576 | bytes 6291456 | tf_op jit(solution)/shard_map/gather_states/pallas_call | solution.py:112
  47.9 0.0 copy-start.2
  47.9 1.3 %copy-done.2 = bf16[32,16,2048]{2,1,0:T(8,128)(2,1)} copy-done((bf16[32,16,2048]{2,1,0:T(8,128)(2,1)}, bf16[32,16,2048]{2,1,0:T(8,128)(2,1)S(1)}, u32[]{:S(2)}) %copy-start.2) | copy-done | bytes 2097176
  49.3 0.0 copy-start.23
  49.3 0.0 copy-start.25
  49.3 0.0 copy-start.14
  49.3 7.3 %all-to-all-start = ((bf16[16,2,16,2048]{3,2,1,0:T(8,128)(2,1)}), bf16[16,2,16,2048]{3,2,1,0:T(8,128)(2,1)S(1)}, u32[]{:S(2)}, u32[]{:S(2)}) async-start(bf16[16,2,16,2048]{3,2,1,0:T(8,128)(2,1)} %bitcast.20), calls=%async_computation | async-start | bytes 4194304 | tf_op jit(solution)/shard_map/all_to_all | solution.py:501
  56.6 0.0 copy-start.31
  56.6 0.0 copy-start.32
  56.7 1.6 %copy-done.5 = bf16[2048,544]{0,1:T(8,128)(2,1)S(1)} copy-done((bf16[2048,544]{0,1:T(8,128)(2,1)S(1)}, bf16[2048,544]{0,1:T(8,128)(2,1)}, u32[]{:S(2)}) %copy-start.5) | copy-done | bytes 2228248
  58.3 1.7 %mix_input.1 = (bf16[32,2048]{1,0:T(8,128)(2,1)S(1)}, bf16[3,32,2048]{2,1,0:T(8,128)(2,1)}, f32[32,544]{1,0:T(8,128)S(1)}, bf16[32,544]{1,0:T(8,128)(2,1)S(1)}) custom-call(s32[32]{0:T(128)S(1)} %copy-done.23, s32[32]{0:T(128)S(1)} %copy-done.25, bf16[16,16,1024]{2,1,0:T(8,128)(2,1)S(1)} %all-to-all-done.1.recv_ref, bf16[3,32,2048]{2,1,0:T(8,128)(2,1)S(1)} %bitcast.23, ...), custom_call_target="tpu_custom_call" | custom-call | flops 71303168 | bytes 4194304 | tf_op jit(solution)/shard_map/mix_input/pallas_call | solution.py:320
  60.0 0.6 collective-permute-start.6
  60.6 2.4 %collective-permute-start.5 = (bf16[32,544]{1,0:T(8,128)(2,1)S(1)}, bf16[32,544]{1,0:T(8,128)(2,1)S(1)}, u32[]{:S(2)}, u32[]{:S(2)}) collective-permute-start(bf16[32,544]{1,0:T(8,128)(2,1)S(1)} %get-tuple-element.19), channel_id=1, source_target_pairs={{0,6},{1,7},{2,0},{3,1},{4,2},{5,3},{6,4},{7,5},{8,14},{9,15},{10,... | collective-permute-start | bytes 104456 | tf_op jit(solution)/shard_map/ppermute | solution.py:529
  63.1 0.5 collective-permute-start.4
  63.5 2.9 %collective-permute-start.3 = (bf16[32,544]{1,0:T(8,128)(2,1)S(1)}, bf16[32,544]{1,0:T(8,128)(2,1)S(1)}, u32[]{:S(2)}, u32[]{:S(2)}) collective-permute-start(bf16[32,544]{1,0:T(8,128)(2,1)S(1)} %get-tuple-element.19), channel_id=1, source_target_pairs={{0,4},{1,5},{2,6},{3,7},{4,0},{5,1},{6,2},{7,3},{8,12},{9,13},{10,... | collective-permute-start | bytes 104456 | tf_op jit(solution)/shard_map/ppermute | solution.py:529
  66.4 0.3 collective-permute-start.1
  66.7 1.1 %collective-permute-start = (bf16[32,544]{1,0:T(8,128)(2,1)S(1)}, bf16[32,544]{1,0:T(8,128)(2,1)S(1)}, u32[]{:S(2)}, u32[]{:S(2)}) collective-permute-start(bf16[32,544]{1,0:T(8,128)(2,1)S(1)} %get-tuple-element.19), channel_id=1, source_target_pairs={{0,1},{1,2},{2,3},{3,4},{4,5},{5,6},{6,7},{7,0},{8,9},{9,10},{10,1... | collective-permute-start | bytes 104456 | tf_op jit(solution)/shard_map/ppermute | solution.py:529
  67.9 0.1 maximum_bitcast_fusion.refs_9_
  68.0 3.4 %copy-done.1 = bf16[32,512,256]{2,1,0:T(8,128)(2,1)S(1)} copy-done((bf16[32,512,256]{2,1,0:T(8,128)(2,1)S(1)}, bf16[32,512,256]{2,1,0:T(8,128)(2,1)}, u32[]{:S(2)}) %copy-start.1) | copy-done | bytes 8388632
  71.3 9.1 %resident_attention.1 = (f32[32,8,128]{2,1,0:T(8,128)S(1)}, f32[32,8,128]{2,1,0:T(8,128)S(1)}, f32[32,8,128]{2,1,0:T(8,128)S(1)}) custom-call(s32[32]{0:T(128)S(1)} %copy-done.29, bf16[32,1024]{1,0:T(8,128)(2,1)S(1)} %copy-done.14, f32[32,1,128]{2,1,0:T(1,128)S(1)} %bitcast.25, bf16[32,512,256]{2,1,0:T(8,128)(2,1)S(1)} %copy-done.1), custom_call_target="tpu_custom_call" | custom-call | flops 67108864 | bytes 9437184 | tf_op jit(solution)/shard_map/resident_attention/pallas_call | solution.py:265
  80.6 0.6 step_size.1
  81.2 1.5 %join_new_token.1 = bf16[32,1024]{1,0:T(8,128)(2,1)} custom-call(s32[32]{0:T(128)S(1)} %copy-done.23, s32[32]{0:T(128)S(1)} %copy-done.25, bf16[32,16,128]{2,1,0:T(8,128)(2,1)S(1)} %bitcast.22, f32[32,8,128]{2,1,0:T(8,128)S(1)} %get-tuple-element.27.mix_ref, f32[32,8,128]{2,1,0:T(8,128)S(1)} %get-tuple-element.28.lse_ref, ...), custom_call_target="tpu_custom_call" | custom-call | flops 65536 | bytes 524288 | tf_op jit(solution)/shard_map/join_new_token/pallas_call | solution.py:488
  82.7 2.7 %all-to-all-done = bf16[16,2,16,2048]{3,2,1,0:T(8,128)(2,1)S(1)} async-done(((bf16[16,2,16,2048]{3,2,1,0:T(8,128)(2,1)}), bf16[16,2,16,2048]{3,2,1,0:T(8,128)(2,1)S(1)}, u32[]{:S(2)}, u32[]{:S(2)}) %all-to-all-start) | async-done | bytes 2097184 | tf_op jit(solution)/shard_map/all_to_all | solution.py:501
  85.4 0.2 broadcast_in_dim.2.tail_ref
  85.6 2.2 %copy-done.3 = f32[32,16,2048]{2,1,0:T(8,128)S(1)} copy-done((f32[32,16,2048]{2,1,0:T(8,128)S(1)}, f32[32,16,2048]{2,1,0:T(8,128)}, u32[]{:S(2)}) %copy-start.3) | copy-done | bytes 4194328
  87.8 7.9 %update_state.1 = (f32[32,16,2048]{2,1,0:T(8,128)}, bf16[32,2048]{1,0:T(8,128)(2,1)}) custom-call(s32[32]{0:T(128)S(1)} %copy-done.23, s32[32]{0:T(128)S(1)} %copy-done.25, bf16[32,16,2048]{2,1,0:T(8,128)(2,1)S(1)} %bitcast.19, f32[32,16,2048]{2,1,0:T(8,128)S(1)} %copy-done.3, f32[32,2048]{1,0:T(8,128)S(1)} %get-tuple-element.21.dt_ref, ...), custom_call_target="tpu_custom_call" | custom-call | flops 16777216 | bytes 10485760 | tf_op jit(solution)/shard_map/update_state/pallas_call | solution.py:445
  (57 shorter events, 0.1 us)
Async XLA Ops:
  0.6 15.6 %copy-start = (bf16[256,16,256]{2,1,0:T(8,128)(2,1)S(1)}, bf16[256,16,256]{2,1,0:T(8,128)(2,1)}, u32[]{:S(2)}) copy-start(bf16[256,16,256]{2,1,0:T(8,128)(2,1)} %pool_ref.5) | copy-start | bytes 6291460
  0.6 1.1 %copy-start.12 = (bf16[32,3,2048]{2,0,1:T(8,128)(2,1)S(1)}, bf16[32,3,2048]{2,0,1:T(8,128)(2,1)}, u32[]{:S(2)}) copy-start(bf16[32,3,2048]{2,0,1:T(8,128)(2,1)} %param.29) | copy-start | bytes 1179652
  1.8 0.8 copy-start.13
  2.6 0.7 copy-start.22
  3.3 0.7 copy-start.24
  3.9 0.7 copy-start.26
  6.4 19.5 %all-to-all-start.1 = ((bf16[16,16,1024]{2,1,0:T(8,128)(2,1)}), bf16[16,16,1024]{2,1,0:T(8,128)(2,1)S(1)}, u32[]{:S(2)}, u32[]{:S(2)}) async-start(bf16[16,16,1024]{2,1,0:T(8,128)(2,1)} %pack_first.1), calls=%async_computation.1 | async-start | bytes 1048576 | tf_op jit(solution)/shard_map/all_to_all | solution.py:501
  17.4 1.0 %copy-start.7 = (bf16[256,16,128]{2,1,0:T(8,128)(2,1)}, bf16[256,16,128]{2,1,0:T(8,128)(2,1)S(1)}, u32[]{:S(2)}) copy-start(bf16[256,16,128]{2,1,0:T(8,128)(2,1)S(1)} %get-tuple-element.25.weight_ref) | copy-start | bytes 3145732
  18.4 1.0 %copy-start.9 = (bf16[128,4096]{1,0:T(8,128)(2,1)}, bf16[128,4096]{1,0:T(8,128)(2,1)S(1)}, u32[]{:S(2)}) copy-start(bf16[128,4096]{1,0:T(8,128)(2,1)S(1)} %get-tuple-element.26.vt_ref) | copy-start | bytes 3145732
  25.9 1.2 %copy-start.8 = (bf16[256,16,128]{2,1,0:T(8,128)(2,1)S(1)}, bf16[256,16,128]{2,1,0:T(8,128)(2,1)}, u32[]{:S(2)}) copy-start(bf16[256,16,128]{2,1,0:T(8,128)(2,1)} %copy-done.7) | copy-start | bytes 3145732
  27.1 1.2 %copy-start.10 = (bf16[128,4096]{1,0:T(8,128)(2,1)S(1)}, bf16[128,4096]{1,0:T(8,128)(2,1)}, u32[]{:S(2)}) copy-start(bf16[128,4096]{1,0:T(8,128)(2,1)} %copy-done.9) | copy-start | bytes 3145732
  28.3 10.8 %copy-start.27 = (s32[1,16,2]{1,2,0:T(2,128)S(1)}, s32[1,16,2]{1,2,0:T(2,128)}, u32[]{:S(2)}) copy-start(s32[1,16,2]{1,2,0:T(2,128)} %param.49) | copy-start | bytes 388
  35.6 13.7 %all-to-all-start.2 = ((bf16[16,32,128]{2,1,0:T(8,128)(2,1)}), bf16[16,32,128]{2,1,0:T(8,128)(2,1)S(1)}, u32[]{:S(2)}, u32[]{:S(2)}) async-start(bf16[16,32,128]{2,1,0:T(8,128)(2,1)} %serve_pool.1), calls=%async_computation.2 | async-start | bytes 262144 | tf_op jit(solution)/shard_map/all_to_all | solution.py:501
  39.1 2.2 %copy-start.4 = (f32[32,16,2048]{2,1,0:T(8,128)S(1)}, f32[32,16,2048]{2,1,0:T(8,128)}, u32[]{:S(2)}) copy-start(f32[32,16,2048]{2,1,0:T(8,128)} %pool_ref.3) | copy-start | bytes 12582916
  47.9 1.3 %copy-start.2 = (bf16[32,16,2048]{2,1,0:T(8,128)(2,1)}, bf16[32,16,2048]{2,1,0:T(8,128)(2,1)S(1)}, u32[]{:S(2)}) copy-start(bf16[32,16,2048]{2,1,0:T(8,128)(2,1)S(1)} %gather_states.1) | copy-start | bytes 6291460
  49.2 7.4 %copy-start.11 = (bf16[32,3,2048]{2,0,1:T(8,128)(2,1)S(1)}, bf16[32,3,2048]{2,0,1:T(8,128)(2,1)}, u32[]{:S(2)}) copy-start(bf16[32,3,2048]{2,0,1:T(8,128)(2,1)} %param.28) | copy-start | bytes 1179652
  49.2 7.4 %copy-start.17 = (bf16[32,2048]{1,0:T(8,128)(2,1)S(1)}, bf16[32,2048]{1,0:T(8,128)(2,1)}, u32[]{:S(2)}) copy-start(bf16[32,2048]{1,0:T(8,128)(2,1)} %x_ref.1) | copy-start | bytes 393220
  49.2 7.4 %copy-start.18 = (bf16[4,2048]{1,0:T(4,128)(2,1)S(1)}, bf16[4,2048]{1,0:T(4,128)(2,1)}, u32[]{:S(2)}) copy-start(bf16[4,2048]{1,0:T(4,128)(2,1)} %weight_ref.1) | copy-start | bytes 49156
  49.2 7.4 %copy-start.19 = (f32[2048]{0:T(1024)S(1)}, f32[2048]{0:T(1024)}, u32[]{:S(2)}) copy-start(f32[2048]{0:T(1024)} %param.33) | copy-start | bytes 24580
  49.3 7.4 %copy-start.23 = (s32[32]{0:T(128)S(1)}, s32[32]{0:T(128)}, u32[]{:S(2)}) copy-start(s32[32]{0:T(128)} %owner_ref.7) | copy-start | bytes 388
  49.3 7.4 %copy-start.25 = (s32[32]{0:T(128)S(1)}, s32[32]{0:T(128)}, u32[]{:S(2)}) copy-start(s32[32]{0:T(128)} %pos_ref.7) | copy-start | bytes 388
  49.3 13.8 %copy-start.30 = (bf16[32,256]{1,0:T(8,128)(2,1)S(1)}, bf16[32,256]{1,0:T(8,128)(2,1)}, u32[]{:S(2)}) copy-start(bf16[32,256]{1,0:T(8,128)(2,1)} %param.43) | copy-start | bytes 49156
  49.3 18.6 %copy-start.14 = (bf16[32,1024]{1,0:T(8,128)(2,1)S(1)}, bf16[32,1024]{1,0:T(8,128)(2,1)}, u32[]{:S(2)}) copy-start(bf16[32,1024]{1,0:T(8,128)(2,1)} %query_ref.3) | copy-start | bytes 196612
  49.3 36.1 %all-to-all-start = ((bf16[16,2,16,2048]{3,2,1,0:T(8,128)(2,1)}), bf16[16,2,16,2048]{3,2,1,0:T(8,128)(2,1)S(1)}, u32[]{:S(2)}, u32[]{:S(2)}) async-start(bf16[16,2,16,2048]{3,2,1,0:T(8,128)(2,1)} %bitcast.20), calls=%async_computation | async-start | bytes 4194304 | tf_op jit(solution)/shard_map/all_to_all | solution.py:501
  56.6 11.3 %copy-start.31 = (f32[16]{0:T(128)S(1)}, f32[16]{0:T(128)}, u32[]{:S(2)}) copy-start(f32[16]{0:T(128)} %param.37) | copy-start | bytes 196
  56.6 11.2 %copy-start.32 = (f32[16]{0:T(128)S(1)}, f32[16]{0:T(128)}, u32[]{:S(2)}) copy-start(f32[16]{0:T(128)} %param.36) | copy-start | bytes 196
  56.6 11.3 %copy-start.29 = (s32[32]{0:T(128)S(1)}, s32[32]{0:T(128)}, u32[]{:S(2)}) copy-start(s32[32]{0:T(128)} %len_ref.1) | copy-start | bytes 388
  56.7 1.6 %copy-start.5 = (bf16[2048,544]{0,1:T(8,128)(2,1)S(1)}, bf16[2048,544]{0,1:T(8,128)(2,1)}, u32[]{:S(2)}) copy-start(bf16[2048,544]{0,1:T(8,128)(2,1)} %param.34) | copy-start | bytes 6684676
  60.0 6.4 %collective-permute-start.6 = (bf16[32,544]{1,0:T(8,128)(2,1)S(1)}, bf16[32,544]{1,0:T(8,128)(2,1)S(1)}, u32[]{:S(2)}, u32[]{:S(2)}) collective-permute-start(bf16[32,544]{1,0:T(8,128)(2,1)S(1)} %get-tuple-element.19), channel_id=1, source_target_pairs={{0,7},{1,0},{2,1},{3,2},{4,3},{5,4},{6,5},{7,6},{8,15},{9,8},{10,9... | collective-permute-start | bytes 104456 | tf_op jit(solution)/shard_map/ppermute | solution.py:529
  60.6 6.1 %collective-permute-start.5 = (bf16[32,544]{1,0:T(8,128)(2,1)S(1)}, bf16[32,544]{1,0:T(8,128)(2,1)S(1)}, u32[]{:S(2)}, u32[]{:S(2)}) collective-permute-start(bf16[32,544]{1,0:T(8,128)(2,1)S(1)} %get-tuple-element.19), channel_id=1, source_target_pairs={{0,6},{1,7},{2,0},{3,1},{4,2},{5,3},{6,4},{7,5},{8,14},{9,15},{10,... | collective-permute-start | bytes 104456 | tf_op jit(solution)/shard_map/ppermute | solution.py:529
  63.1 17.5 %collective-permute-start.4 = (bf16[32,544]{1,0:T(8,128)(2,1)S(1)}, bf16[32,544]{1,0:T(8,128)(2,1)S(1)}, u32[]{:S(2)}, u32[]{:S(2)}) collective-permute-start(bf16[32,544]{1,0:T(8,128)(2,1)S(1)} %get-tuple-element.19), channel_id=1, source_target_pairs={{0,5},{1,6},{2,7},{3,0},{4,1},{5,2},{6,3},{7,4},{8,13},{9,14},{10,... | collective-permute-start | bytes 104456 | tf_op jit(solution)/shard_map/ppermute | solution.py:529
  63.5 17.0 %collective-permute-start.3 = (bf16[32,544]{1,0:T(8,128)(2,1)S(1)}, bf16[32,544]{1,0:T(8,128)(2,1)S(1)}, u32[]{:S(2)}, u32[]{:S(2)}) collective-permute-start(bf16[32,544]{1,0:T(8,128)(2,1)S(1)} %get-tuple-element.19), channel_id=1, source_target_pairs={{0,4},{1,5},{2,6},{3,7},{4,0},{5,1},{6,2},{7,3},{8,12},{9,13},{10,... | collective-permute-start | bytes 104456 | tf_op jit(solution)/shard_map/ppermute | solution.py:529
  66.4 14.1 %collective-permute-start.2 = (bf16[32,544]{1,0:T(8,128)(2,1)S(1)}, bf16[32,544]{1,0:T(8,128)(2,1)S(1)}, u32[]{:S(2)}, u32[]{:S(2)}) collective-permute-start(bf16[32,544]{1,0:T(8,128)(2,1)S(1)} %get-tuple-element.19), channel_id=1, source_target_pairs={{0,3},{1,4},{2,5},{3,6},{4,7},{5,0},{6,1},{7,2},{8,11},{9,12},{10,... | collective-permute-start | bytes 104456 | tf_op jit(solution)/shard_map/ppermute | solution.py:529
  66.4 14.1 %collective-permute-start.1 = (bf16[32,544]{1,0:T(8,128)(2,1)S(1)}, bf16[32,544]{1,0:T(8,128)(2,1)S(1)}, u32[]{:S(2)}, u32[]{:S(2)}) collective-permute-start(bf16[32,544]{1,0:T(8,128)(2,1)S(1)} %get-tuple-element.19), channel_id=1, source_target_pairs={{0,2},{1,3},{2,4},{3,5},{4,6},{5,7},{6,0},{7,1},{8,10},{9,11},{10,... | collective-permute-start | bytes 104456 | tf_op jit(solution)/shard_map/ppermute | solution.py:529
  66.7 13.8 %collective-permute-start = (bf16[32,544]{1,0:T(8,128)(2,1)S(1)}, bf16[32,544]{1,0:T(8,128)(2,1)S(1)}, u32[]{:S(2)}, u32[]{:S(2)}) collective-permute-start(bf16[32,544]{1,0:T(8,128)(2,1)S(1)} %get-tuple-element.19), channel_id=1, source_target_pairs={{0,1},{1,2},{2,3},{3,4},{4,5},{5,6},{6,7},{7,0},{8,9},{9,10},{10,1... | collective-permute-start | bytes 104456 | tf_op jit(solution)/shard_map/ppermute | solution.py:529
  68.0 3.4 %copy-start.1 = (bf16[32,512,256]{2,1,0:T(8,128)(2,1)S(1)}, bf16[32,512,256]{2,1,0:T(8,128)(2,1)}, u32[]{:S(2)}) copy-start(bf16[32,512,256]{2,1,0:T(8,128)(2,1)} %cache_ref.1) | copy-start | bytes 25165828
  71.3 9.2 %copy-start.6 = (bf16[512,2048]{1,0:T(8,128)(2,1)S(1)}, bf16[512,2048]{1,0:T(8,128)(2,1)}, u32[]{:S(2)}) copy-start(bf16[512,2048]{1,0:T(8,128)(2,1)} %refs_10_.1) | copy-start | bytes 6291460
  71.3 9.2 %copy-start.20 = (f32[2048]{0:T(1024)S(1)}, f32[2048]{0:T(1024)}, u32[]{:S(2)}) copy-start(f32[2048]{0:T(1024)} %param.39) | copy-start | bytes 24580
  71.3 9.2 %copy-start.28 = (f32[512]{0:T(512)S(1)}, f32[512]{0:T(512)}, u32[]{:S(2)}) copy-start(f32[512]{0:T(512)} %param.35) | copy-start | bytes 6148
  80.5 5.1 %copy-start.15 = (f32[16,2048]{1,0:T(8,128)S(1)}, f32[16,2048]{1,0:T(8,128)}, u32[]{:S(2)}) copy-start(f32[16,2048]{1,0:T(8,128)} %decay_ref.1) | copy-start | bytes 393220
  80.5 5.1 %copy-start.16 = (bf16[32,2048]{1,0:T(8,128)(2,1)S(1)}, bf16[32,2048]{1,0:T(8,128)(2,1)}, u32[]{:S(2)}) copy-start(bf16[32,2048]{1,0:T(8,128)(2,1)} %z_ref.1) | copy-start | bytes 393220
  80.5 5.1 %copy-start.21 = (f32[2048]{0:T(1024)S(1)}, f32[2048]{0:T(1024)}, u32[]{:S(2)}) copy-start(f32[2048]{0:T(1024)} %param.41) | copy-start | bytes 24580
  85.6 2.2 %copy-start.3 = (f32[32,16,2048]{2,1,0:T(8,128)S(1)}, f32[32,16,2048]{2,1,0:T(8,128)}, u32[]{:S(2)}) copy-start(f32[32,16,2048]{2,1,0:T(8,128)} %state_ref.1) | copy-start | bytes 12582916

commit v2 on v1

v2 whole, which is shorter than its diff:
```python
import functools
import math

import jax
import jax.numpy as jnp
from jax import lax
from jax.experimental import pallas as pl
from jax.experimental.pallas import tpu as pltpu
from jax.sharding import PartitionSpec as P

BF = jnp.bfloat16
F32 = jnp.float32
I32 = jnp.int32
PEERS = 16
CAP = 2
LAST = 15
ENT = PEERS * CAP
ROWS = 32
EC = 2048
HALF = EC // 2
NS = 16
RANK = 512
HEADS = 8
HD = 128
CTX = 512
PAGE = 16
POOL = 256
TOK = POOL * PAGE
CHUNK = 256
LOG2E = 1.4426950408889634
LN2 = 0.6931471805599453
NEG = -1e30

VM = pl.BlockSpec(memory_space=pltpu.VMEM)
SM = pl.BlockSpec(memory_space=pltpu.SMEM)
AN = pl.BlockSpec(memory_space=pl.ANY)
HB = pl.BlockSpec(memory_space=pltpu.HBM)
WIDE = EC + HD
BIAS = math.sqrt(HD) / LOG2E


def iota(shape, dim):
    return lax.broadcasted_iota(I32, shape, dim)


def params(mib):
    return pltpu.CompilerParams(vmem_limit_bytes=mib * 1024 * 1024)


ALONE = pltpu.CompilerParams(vmem_limit_bytes=65716224)


def cost(flops, byts):
    return pl.CostEstimate(flops=flops, bytes_accessed=byts, transcendentals=0)


def pack_kernel(
    slot_hbm, owner_hbm, pos_hbm, conv_ref, query_ref, out_ref,
    stack, made, inverse, slot_ref, owner_ref, pos_ref, sems,
):
    copies = [
        pltpu.make_async_copy(slot_hbm, slot_ref, sems.at[0]),
        pltpu.make_async_copy(owner_hbm, owner_ref, sems.at[1]),
        pltpu.make_async_copy(pos_hbm, pos_ref, sems.at[2]),
        pltpu.make_async_copy(query_ref, stack.at[192:224], sems.at[3]),
    ]
    for k in range(6):
        j, h = k // 2, k % 2
        copies.append(
            pltpu.make_async_copy(
                conv_ref.at[j, :, h * HALF : (h + 1) * HALF],
                stack.at[32 * k : 32 * k + 32],
                sems.at[4 + k],
            )
        )
    for copy in copies:
        copy.start()
    stack[224:256, :] = jnp.zeros((32, HALF), BF)
    for e in range(ENT):
        inverse[e] = -1
    for copy in copies[:3]:
        copy.wait()
    for r in range(ROWS):
        owner = owner_ref[r]

        @pl.when(owner >= 0)
        def _():
            inverse[(LAST - owner) * CAP + pos_ref[r]] = 192 + r

    lane = iota((8, 256), 1)
    part = iota((8, 256), 0)
    tiles = []
    for e in range(ENT):
        slot = slot_ref[0, e % CAP, LAST - e // CAP]
        want = jnp.where(part < 6, 32 * part + slot, jnp.where(part == 6, inverse[e], -1))
        tiles.append((lane == want).astype(F32))
    pick = jnp.concatenate(tiles, axis=0).astype(BF)
    for copy in copies[3:]:
        copy.wait()
    gone = []
    for k in range(4):
        packed = jnp.dot(pick[64 * k : 64 * k + 64], stack[...], preferred_element_type=F32)
        made[4 * k : 4 * k + 4] = packed.astype(BF).reshape(4, 16, HALF)
        part = slice(4 * k, 4 * k + 4)
        gone.append(pltpu.make_async_copy(made.at[part], out_ref.at[part], sems.at[k]))
        gone[k].start()
    for copy in gone:
        copy.wait()


def pack(slots, owner, pos, conv_pool, query):
    return pl.pallas_call(
        pack_kernel,
        out_shape=jax.ShapeDtypeStruct((PEERS, 16, HALF), BF),
        in_specs=[HB] * 5,
        out_specs=HB,
        scratch_shapes=[
            pltpu.VMEM((256, HALF), BF),
            pltpu.VMEM((PEERS, 16, HALF), BF),
            pltpu.SMEM((ENT,), I32),
            pltpu.SMEM((1, CAP, PEERS), I32),
            pltpu.SMEM((ROWS,), I32),
            pltpu.SMEM((ROWS,), I32),
            pltpu.SemaphoreType.DMA((10,)),
        ],
        compiler_params=ALONE,
        cost_estimate=cost(2 * 256 * 256 * HALF, 1 << 20),
        name="pack_first",
    )(slots, owner, pos, conv_pool, query)


def prepare_kernel(
    slot_hbm, pages_hbm, lens_hbm, ssm_ref, states_ref, bias_ref, rest_ref,
    slot_ref, pages_ref, lens_ref, states, packed, sems, in_sems, out_sems,
):
    first = pltpu.make_async_copy(slot_hbm, slot_ref, sems.at[0])
    first.start()
    lists = [
        pltpu.make_async_copy(pages_hbm, pages_ref, sems.at[1]),
        pltpu.make_async_copy(lens_hbm, lens_ref, sems.at[2]),
    ]
    for copy in lists:
        copy.start()
    first.wait()

    def fetch(k):
        return pltpu.make_async_copy(
            ssm_ref.at[8 * k : 8 * k + 8], states.at[8 * k : 8 * k + 8], in_sems.at[k]
        )

    def give(k):
        return pltpu.make_async_copy(
            packed.at[8 * k : 8 * k + 8], states_ref.at[8 * k : 8 * k + 8, :, 0:EC], out_sems.at[k]
        )

    for k in range(4):
        fetch(k).start()
    for copy in lists:
        copy.wait()

    full = jnp.zeros((1, 128), F32)
    rest = jnp.zeros((1, 128), F32)
    pages = jnp.zeros((CTX // PAGE, 128), F32)
    for place in range(CAP):
        want = iota((PEERS, 128), 1) % ENT == (LAST - iota((PEERS, 128), 0)) * CAP + place
        want = want.astype(F32)
        lens = lens_ref[0, place : place + 1, :]
        count = lens // PAGE
        full += jnp.dot(count.astype(F32), want, preferred_element_type=F32)
        rest += jnp.dot((lens - count * PAGE).astype(F32), want, preferred_element_type=F32)
        pages += lax.dot_general(
            pages_ref[0, :, place, :].astype(F32), want, (((0,), (0,)), ((), ())),
            preferred_element_type=F32,
        )
    page_id = iota((POOL, 128), 0).astype(F32)
    total = jnp.zeros((POOL, 128), F32)
    last = jnp.full((1, 128), -1.0, F32)
    for j in range(CTX // PAGE):
        page = pages[j : j + 1, :]
        total += jnp.where(page_id == jnp.where(full > j, page, -1.0), 1.0, 0.0)
        last = jnp.where(full == j, page, last)

    def bias(count):
        return jnp.where(count > 0.0, jnp.log2(jnp.maximum(count, 1.0)) * BIAS, NEG)

    bias_ref[0] = bias(total)
    bias_ref[1] = bias(total + jnp.where(page_id == last, 1.0, 0.0))
    rest_ref[...] = rest
    for k in range(4):
        fetch(k).wait()
    for k in range(4):
        for e in range(8 * k, 8 * k + 8):
            packed[e] = states[slot_ref[0, e % CAP, LAST - e // CAP]].astype(BF)
        give(k).start()
    for k in range(4):
        give(k).wait()


def prepare(slots, pages, lens, ssm_pool):
    return pl.pallas_call(
        prepare_kernel,
        out_shape=(
            jax.ShapeDtypeStruct((ENT, NS, WIDE), BF),
            jax.ShapeDtypeStruct((2, POOL, 128), F32),
            jax.ShapeDtypeStruct((1, 128), F32),
        ),
        in_specs=[HB] * 4,
        out_specs=(HB, VM, VM),
        scratch_shapes=[
            pltpu.SMEM((1, CAP, PEERS), I32),
            pltpu.VMEM((1, PEERS, CAP, CTX // PAGE), I32),
            pltpu.VMEM((1, CAP, PEERS), I32),
            pltpu.VMEM((ENT, NS, EC), F32),
            pltpu.VMEM((ENT, NS, EC), BF),
            pltpu.SemaphoreType.DMA((3,)),
            pltpu.SemaphoreType.DMA((4,)),
            pltpu.SemaphoreType.DMA((4,)),
        ],
        compiler_params=ALONE,
        cost_estimate=cost(1 << 20, 6 << 20),
        name="prepare_owner",
    )(slots, pages, lens, ssm_pool)


PARTS = 4


def serve_kernel(
    recv_hbm, bias_hbm, rest_hbm, pool_hbm, send_ref, out_ref, flag_ref,
    recv_ref, bias_ref, rest_ref, pool_ref, scores, back, slab, sems,
):
    loads = [
        pltpu.make_async_copy(recv_hbm, recv_ref, sems.at[0]),
        pltpu.make_async_copy(bias_hbm, bias_ref, sems.at[1]),
        pltpu.make_async_copy(rest_hbm, rest_ref, sems.at[2]),
    ]
    for k in range(PARTS):
        part = slice(k * POOL // PARTS, (k + 1) * POOL // PARTS)
        loads.append(pltpu.make_async_copy(pool_hbm.at[part], pool_ref.at[part], sems.at[3 + k]))
    for copy in loads:
        copy.start()
    lane = iota((ENT, 256), 1)
    pick = (lane == 8 * iota((ENT, 256), 0) + 6).astype(F32).astype(BF)
    loads[0].wait()
    recv = recv_ref[...].reshape(256, HALF)
    query = jnp.dot(pick, recv, preferred_element_type=F32).astype(BF)
    query = jnp.concatenate([query[:, h * HD : (h + 1) * HD] for h in range(HEADS)], axis=0)
    scale = LOG2E / math.sqrt(HD)
    pages = CHUNK // PAGE
    loads[1].wait()
    loads[2].wait()
    held = iota((PAGE, 128), 0).astype(F32) < rest_ref[...]

    top = jnp.full((8, 256), NEG, F32)
    for c in range(TOK // CHUNK):
        if c % (TOK // CHUNK // PARTS) == 0:
            loads[3 + c // (TOK // CHUNK // PARTS)].wait()
        keys = pool_ref[c * pages : (c + 1) * pages, :, 0:HD].reshape(CHUNK, HD)
        raw = lax.dot_general(keys, query, (((1,), (1,)), ((), ())), preferred_element_type=F32)
        bias = jnp.concatenate(
            [
                jnp.where(held, bias_ref[1, p : p + 1, :], bias_ref[0, p : p + 1, :])
                for p in range(c * pages, (c + 1) * pages)
            ],
            axis=0,
        )
        raw = raw + jnp.concatenate([bias, bias], axis=1)
        scores[c * CHUNK : (c + 1) * CHUNK, :] = raw
        top = jnp.maximum(top, jnp.max(raw.reshape(CHUNK // 8, 8, 256), axis=0))
    top = jnp.max(top, axis=0, keepdims=True)

    mix = jnp.zeros((HD, 256), F32)
    total = jnp.zeros((8, 256), F32)
    for c in range(TOK // CHUNK):
        raw = scores[c * CHUNK : (c + 1) * CHUNK, :]
        prob = jnp.exp2((raw - top) * scale).astype(BF)
        total += jnp.sum(prob.astype(F32).reshape(CHUNK // 8, 8, 256), axis=0)
        mix += lax.dot_general(
            pool_ref[c * pages : (c + 1) * pages, :, HD:].reshape(CHUNK, HD), prob,
            (((0,), (0,)), ((), ())), preferred_element_type=F32,
        )
    total = jnp.sum(total, axis=0, keepdims=True)
    lse = top * (1.0 / math.sqrt(HD)) + jnp.log(total)
    high = lse.astype(BF).astype(F32)
    mid = (lse - high).astype(BF).astype(F32)
    low = lse - high - mid
    row = iota((HD, 256), 0)
    pieces = jnp.where(row < 32, high, jnp.where(row < 64, mid, low)).T
    mix = (mix * (1.0 / total)).T
    for h in range(HEADS):
        back[pl.ds(h, ENT, 16), :] = mix[h * ENT : (h + 1) * ENT, :]
        back[pl.ds(8 + h, ENT, 16), :] = pieces[h * ENT : (h + 1) * ENT, :]
    slab[...] = back[...].astype(BF).reshape(ENT, 16, HD)
    copy = pltpu.make_async_copy(slab, out_ref.at[:, :, EC:WIDE], sems.at[0])
    copy.start()
    flag_ref[...] = top[:, 0:HD]
    copy.wait()


def serve(recv, bias, rest, kv_pool, send):
    return pl.pallas_call(
        serve_kernel,
        out_shape=(
            jax.ShapeDtypeStruct((ENT, NS, WIDE), BF),
            jax.ShapeDtypeStruct((1, HD), F32),
        ),
        in_specs=[HB] * 4 + [AN],
        out_specs=(AN, VM),
        input_output_aliases={4: 0},
        scratch_shapes=[
            pltpu.VMEM((PEERS, 16, HALF), BF),
            pltpu.VMEM((2, POOL, 128), F32),
            pltpu.VMEM((1, 128), F32),
            pltpu.VMEM((POOL, PAGE, 2 * HD), BF),
            pltpu.VMEM((TOK, 256), F32),
            pltpu.VMEM((ENT * 16, HD), F32),
            pltpu.VMEM((ENT, 16, HD), BF),
            pltpu.SemaphoreType.DMA((3 + PARTS,)),
        ],
        compiler_params=ALONE,
        cost_estimate=cost(4 * TOK * 256 * HD, 6 << 20),
        name="serve_pool",
    )(recv, bias, rest, kv_pool, send)


BLK = 8


def resident_kernel(
    flag_ref, len_ref, query_ref, new_ref, cache_ref, mix_ref, score_ref, heads
):
    step = pl.program_id(0)

    @pl.when(step == 0)
    def _():
        for h in range(HEADS):
            heads[pl.ds(h, ROWS, 8), :] = query_ref[:, h * HD : (h + 1) * HD].astype(F32)

    scale = LOG2E / math.sqrt(HD)
    rows = BLK * 8
    wide = heads[pl.ds(pl.multiple_of(step * rows, rows), rows), :]
    query = wide.astype(BF)
    raw = []
    lens = []
    for b in range(BLK):
        raw.append(
            lax.dot_general(
                query[8 * b : 8 * b + 8], cache_ref[b, :, 0:HD], (((1,), (1,)), ((), ())),
                preferred_element_type=F32,
            )
        )
        lens.append(jnp.full((8, CTX), len_ref[step * BLK + b], I32))
    raw = jnp.concatenate(raw, axis=0)
    live = iota((rows, CTX), 1) < jnp.concatenate(lens, axis=0)
    raw = jnp.where(live, raw * scale, NEG)
    top = jnp.max(raw, axis=1, keepdims=True)
    prob = jnp.exp2(raw - top).astype(BF)
    total = jnp.sum(prob.astype(F32), axis=1, keepdims=True)
    mix = jnp.concatenate(
        [
            jnp.dot(prob[8 * b : 8 * b + 8], cache_ref[b, :, HD:], preferred_element_type=F32)
            for b in range(BLK)
        ],
        axis=0,
    )
    new = new_ref[...].astype(F32)
    key = jnp.concatenate(
        [jnp.broadcast_to(new[b : b + 1, 0:HD], (8, HD)) for b in range(BLK)], axis=0
    )
    value = jnp.concatenate(
        [jnp.broadcast_to(new[b : b + 1, HD:], (8, HD)) for b in range(BLK)], axis=0
    )
    score = jnp.sum(wide * key, axis=1, keepdims=True) * scale
    peak = jnp.maximum(top, score)
    old = jnp.exp2(top - peak)
    add = jnp.exp2(score - peak)
    mix_ref[...] = (mix * old + add * value) / (total * old + add)
    score_ref[...] = jnp.broadcast_to(score * LN2, (rows, HD))


def resident(flag, lens, query, new_kv, kv_cache):
    tile = pl.BlockSpec((BLK * 8, HD), lambda i: (i, 0))
    shape = jax.ShapeDtypeStruct((ROWS * 8, HD), F32)
    return pl.pallas_call(
        resident_kernel,
        grid=(ROWS // BLK,),
        out_shape=(shape, shape),
        in_specs=[
            AN,
            SM,
            pl.BlockSpec((ROWS, HEADS * HD), lambda i: (0, 0)),
            pl.BlockSpec((BLK, 2 * HD), lambda i: (i, 0)),
            pl.BlockSpec((BLK, CTX, 2 * HD), lambda i: (i, 0, 0)),
        ],
        out_specs=(tile, tile),
        scratch_shapes=[pltpu.VMEM((ROWS * 8, HD), F32)],
        compiler_params=params(58),
        cost_estimate=cost(4 * ROWS * 8 * CTX * HD, 9 << 20),
        name="resident_attention",
    )(flag, lens, query, new_kv, kv_cache)


def mix_kernel(
    flag_ref, source_ref, recv_ref, conv_ref, x_ref, weight_ref, bias_ref, proj_ref,
    mixed_ref, window_ref, part_ref, send_ref,
):
    sub = iota((ROWS, 256), 0)
    lane = iota((ROWS, 256), 1)
    source = jnp.full((ROWS, 256), -1, I32)
    for r in range(ROWS):
        source = jnp.where(sub == r, source_ref[r], source)
    base = jnp.where(source >= 0, source * 8, -8)
    pick = jnp.concatenate([(lane == base + k).astype(F32) for k in range(6)], axis=0).astype(BF)
    recv = recv_ref[...].reshape(256, HALF)
    prev = jnp.dot(pick, recv, preferred_element_type=F32)
    came = source[:, 0:1] >= 0
    x = x_ref[...]
    total = x.astype(F32) * weight_ref[3:4, :].astype(F32)
    window_ref[2] = x
    for j in range(3):
        here = jnp.concatenate(
            [prev[64 * j : 64 * j + 32], prev[64 * j + 32 : 64 * j + 64]], axis=1
        )
        tap = jnp.where(came, here, conv_ref[j].astype(F32))
        if j > 0:
            window_ref[j - 1] = tap.astype(BF)
        total += tap * weight_ref[j : j + 1, :].astype(F32)
    total += bias_ref[...]
    mixed = (total / (1.0 + jnp.exp(-total))).astype(BF)
    mixed_ref[...] = mixed
    part = lax.dot_general(
        mixed, proj_ref[...], (((1,), (1,)), ((), ())), preferred_element_type=F32
    )
    part_ref[...] = part
    send_ref[...] = part.astype(BF)


def mix(flag, source, recv, conv_state, x_in, weight, bias, proj_t):
    wide = proj_t.shape[0]
    return pl.pallas_call(
        mix_kernel,
        out_shape=(
            jax.ShapeDtypeStruct((ROWS, EC), BF),
            jax.ShapeDtypeStruct((3, ROWS, EC), BF),
            jax.ShapeDtypeStruct((ROWS, wide), F32),
            jax.ShapeDtypeStruct((ROWS, wide), BF),
        ),
        in_specs=[AN, SM] + [VM] * 6,
        out_specs=(VM, VM, VM, VM),
        compiler_params=ALONE,
        cost_estimate=cost(2 * ROWS * EC * wide, 4 << 20),
        name="mix_input",
    )(flag, source, recv, conv_state, x_in, weight, bias, proj_t)


GROUP = 8


def advance(prev, dt, decay, drive, inject):
    return jnp.exp2(dt * decay) * prev + drive * inject


def step_kernel(*refs):
    source_ref, part_ref = refs[0:2]
    others = refs[2:9]
    (
        gain_ref, tail_gain_ref, proj_ref, bias_ref, mixed_ref, skip_ref, z_ref, decay_ref, state_ref,
        dt_ref, drive_ref, inject_ref, read_ref, gate_ref, base_ref, new_ref,
        local, made, flat, in_sems, out_sems,
    ) = refs[9:]

    def fetch(r):
        return pltpu.make_async_copy(state_ref.at[r], local.at[r], in_sems.at[r])

    def store(r):
        return pltpu.make_async_copy(made.at[r], new_ref.at[r], out_sems.at[r])

    for r in range(ROWS):

        @pl.when(source_ref[r] < 0)
        def _():
            fetch(r).start()

    proj = part_ref[...]
    for other in others:
        proj += other[...].astype(F32)
    low = proj[:, 0:RANK]
    mean = jnp.sum(low * low, axis=1, keepdims=True) * (1.0 / RANK)
    normed = (low * lax.rsqrt(mean + 1e-6) * gain_ref[...]).astype(BF)
    dt = jnp.dot(normed, proj_ref[...], preferred_element_type=F32) + bias_ref[...]
    dt = jnp.maximum(dt, 0.0) + jnp.log1p(jnp.exp(-jnp.abs(dt)))
    mixed = mixed_ref[...].astype(F32)
    drive = dt * mixed
    dt = dt * (-LOG2E)
    for r in range(ROWS):
        dt_ref[r] = dt[r : r + 1, :]
        drive_ref[r] = drive[r : r + 1, :]
    z = z_ref[...].astype(F32)
    gate = z / (1.0 + jnp.exp(-z))
    gate_ref[...] = gate
    base_ref[...] = skip_ref[...] * mixed * gate
    tail = proj[:, RANK : RANK + 2 * NS]
    square = tail * tail
    front = iota((ROWS, 2 * NS), 1) < NS
    mean_b = jnp.sum(jnp.where(front, square, 0.0), axis=1, keepdims=True) * (1.0 / NS)
    mean_c = jnp.sum(jnp.where(front, 0.0, square), axis=1, keepdims=True) * (1.0 / NS)
    scale = lax.rsqrt(jnp.where(front, mean_b, mean_c) + 1e-6)
    tail = (tail * scale * tail_gain_ref[...]).astype(BF)
    lane = iota((2 * NS, 128), 1)
    spread = (iota((2 * NS, 128), 0) == NS + lane % NS).astype(F32).astype(BF)
    read = jnp.dot(tail, spread, preferred_element_type=F32)
    own = iota((ROWS, 128), 1) // NS == iota((ROWS, 128), 0) % GROUP
    read_ref[...] = jnp.where(own, read, 0.0)
    many = (iota((ROWS * NS, ROWS), 0) // NS == iota((ROWS * NS, ROWS), 1)).astype(F32).astype(BF)
    each = jnp.dot(many, tail, preferred_element_type=F32)
    mine = iota((ROWS * NS, 2 * NS), 0) % NS == iota((ROWS * NS, 2 * NS), 1)
    each = jnp.where(mine, each, 0.0).astype(BF)
    inject = jnp.dot(each, jnp.ones((2 * NS, 128), BF), preferred_element_type=F32)
    inject_ref[...] = inject.reshape(ROWS, NS, 128)

    def body(i, carry):
        for b in range(GROUP):
            r = i * GROUP + b

            @pl.when(source_ref[r] < 0)
            def _():
                fetch(r).wait()
                inject = jnp.concatenate([inject_ref[r]] * 4, axis=1)
                for c in range(EC // 512):
                    cols = slice(c * 512, (c + 1) * 512)
                    new = advance(
                        local[r, :, cols], dt_ref[r, :, cols], decay_ref[:, cols],
                        drive_ref[r, :, cols], inject,
                    )
                    made[r, :, cols] = new
                    flat[b * NS : (b + 1) * NS, cols] = new.astype(BF)
                store(r).start()

            @pl.when(source_ref[r] >= 0)
            def _():
                flat[b * NS : (b + 1) * NS, :] = jnp.zeros((NS, EC), BF)

        rows = pl.ds(pl.multiple_of(i * GROUP, GROUP), GROUP)
        sums = jnp.dot(read_ref[rows, :].astype(BF), flat[...], preferred_element_type=F32)
        base_ref[rows, :] += sums * gate_ref[rows, :]
        return carry

    lax.fori_loop(0, ROWS // GROUP, body, 0)
    for r in range(ROWS):

        @pl.when(source_ref[r] < 0)
        def _():
            store(r).wait()


def step_size(source, part, others, *operands):
    return pl.pallas_call(
        step_kernel,
        out_shape=(
            jax.ShapeDtypeStruct((ROWS, 1, EC), F32),
            jax.ShapeDtypeStruct((ROWS, 1, EC), F32),
            jax.ShapeDtypeStruct((ROWS, NS, 128), F32),
            jax.ShapeDtypeStruct((ROWS, 128), F32),
            jax.ShapeDtypeStruct((ROWS, EC), F32),
            jax.ShapeDtypeStruct((ROWS, EC), F32),
            jax.ShapeDtypeStruct((ROWS, NS, EC), F32),
        ),
        in_specs=[SM] + [VM] * 16 + [HB],
        out_specs=(VM,) * 6 + (HB,),
        scratch_shapes=[
            pltpu.VMEM((ROWS, NS, EC), F32),
            pltpu.VMEM((ROWS, NS, EC), F32),
            pltpu.VMEM((GROUP * NS, EC), BF),
            pltpu.SemaphoreType.DMA((ROWS,)),
            pltpu.SemaphoreType.DMA((ROWS,)),
        ],
        compiler_params=params(56),
        cost_estimate=cost(2 * ROWS * EC * RANK, 12 << 20),
        name="step_and_resident",
    )(source, part, *others, *operands)


def tail_kernel(
    source_ref, recv_hbm, dt_hbm, drive_hbm, inject_hbm, read_hbm, decay_hbm,
    gate_hbm, base_hbm, mix_hbm, score_hbm, new_kv_hbm, kept_ref,
    new_ref, out_hbm, attn_hbm,
    dt_ref, drive_ref, inject_ref, read_ref, decay_ref, gate_ref, base_ref, mix_ref, score_ref,
    new_kv_ref, out_ref, attn_ref,
    came, made, flat, sums, other, pieces, sems, in_sems, out_sems,
):
    def fetch(k):
        part = slice(k * GROUP, (k + 1) * GROUP)
        return pltpu.make_async_copy(recv_hbm.at[part], came.at[part], in_sems.at[k])

    pairs = [
        (dt_hbm, dt_ref), (drive_hbm, drive_ref), (inject_hbm, inject_ref), (read_hbm, read_ref),
        (decay_hbm, decay_ref), (mix_hbm, mix_ref), (gate_hbm, gate_ref), (base_hbm, base_ref),
        (score_hbm, score_ref), (new_kv_hbm, new_kv_ref),
    ]
    loads = [pltpu.make_async_copy(a, b, sems.at[k]) for k, (a, b) in enumerate(pairs)]
    for copy in loads[:5]:
        copy.start()
    for k in range(ENT // GROUP):
        fetch(k).start()
    for copy in loads[5:]:
        copy.start()
    for copy in loads[:6]:
        copy.wait()
    for k in range(ENT // GROUP):
        fetch(k).wait()

    def store(r):
        return pltpu.make_async_copy(made.at[r], new_ref.at[r], out_sems.at[r])

    def store_all(i):
        rows = pl.ds(pl.multiple_of(i * GROUP, GROUP), GROUP)
        return pltpu.make_async_copy(made.at[rows], new_ref.at[rows], out_sems.at[i * GROUP])

    def leave(i, act):
        count = jnp.int32(0)
        for b in range(GROUP):
            count += jnp.where(source_ref[i * GROUP + b] >= 0, 1, 0)

        @pl.when(count == GROUP)
        def _():
            act(store_all(i))

        @pl.when(count < GROUP)
        def _():
            for b in range(GROUP):
                r = i * GROUP + b

                @pl.when(source_ref[r] >= 0)
                def _():
                    act(store(r))

    lane = iota((8, HD), 1)
    huge = jnp.where(lane < 32, -NEG, 0.0)

    def body(i, carry):
        for b in range(GROUP):
            r = i * GROUP + b
            source = source_ref[r]
            here = pl.ds(pl.multiple_of(8 * r, 8), 8)

            @pl.when(source >= 0)
            def _():
                tile = came[source, :, EC:WIDE].astype(F32)
                other[here, :] = tile[0:8, :]
                pieces[here, :] = tile[8:16, :]
                inject = jnp.concatenate([inject_ref[r]] * 4, axis=1)
                for c in range(EC // 512):
                    cols = slice(c * 512, (c + 1) * 512)
                    new = advance(
                        came[source, :, cols].astype(F32), dt_ref[r, :, cols],
                        decay_ref[:, cols], drive_ref[r, :, cols], inject,
                    )
                    made[r, :, cols] = new
                    flat[b * NS : (b + 1) * NS, cols] = new.astype(BF)

            @pl.when(source < 0)
            def _():
                other[here, :] = mix_ref[here, :]
                pieces[here, :] = huge
                flat[b * NS : (b + 1) * NS, :] = jnp.zeros((NS, EC), BF)

        leave(i, lambda copy: copy.start())
        rows = pl.ds(pl.multiple_of(i * GROUP, GROUP), GROUP)
        sums[rows, :] = jnp.dot(
            read_ref[rows, :].astype(BF), flat[...], preferred_element_type=F32
        )
        return carry

    lax.fori_loop(0, ROWS // GROUP, body, 0)
    for copy in loads[6:]:
        copy.wait()
    out_ref[...] = (sums[...] * gate_ref[...] + base_ref[...]).astype(BF)
    give_out = pltpu.make_async_copy(out_ref, out_hbm, sems.at[0])
    give_out.start()
    lse = pieces[:, 0:1] + pieces[:, 32:33] + pieces[:, 64:65]
    score = score_ref[...]
    peak = jnp.maximum(lse, score)
    old = jnp.exp(lse - peak)
    new = jnp.exp(score - peak)
    value = new_kv_ref[:, HD:].astype(F32)
    value = jnp.concatenate(
        [jnp.broadcast_to(value[r : r + 1, :], (8, HD)) for r in range(ROWS)], axis=0
    )
    pieces[...] = (other[...] * old + new * value) / (old + new)
    for h in range(HEADS):
        attn_ref[:, h * HD : (h + 1) * HD] = pieces[pl.ds(h, ROWS, 8), :].astype(BF)
    give_attn = pltpu.make_async_copy(attn_ref, attn_hbm, sems.at[1])
    give_attn.start()
    give_out.wait()
    give_attn.wait()
    for i in range(ROWS // GROUP):
        leave(i, lambda copy: copy.wait())


def tail(*operands):
    return pl.pallas_call(
        tail_kernel,
        out_shape=(
            jax.ShapeDtypeStruct((ROWS, NS, EC), F32),
            jax.ShapeDtypeStruct((ROWS, EC), BF),
            jax.ShapeDtypeStruct((ROWS, HEADS * HD), BF),
        ),
        in_specs=[SM] + [HB] * 11 + [AN],
        out_specs=(AN, HB, HB),
        input_output_aliases={12: 0},
        scratch_shapes=[
            pltpu.VMEM((ROWS, 1, EC), F32),
            pltpu.VMEM((ROWS, 1, EC), F32),
            pltpu.VMEM((ROWS, NS, 128), F32),
            pltpu.VMEM((ROWS, 128), F32),
            pltpu.VMEM((NS, EC), F32),
            pltpu.VMEM((ROWS, EC), F32),
            pltpu.VMEM((ROWS, EC), F32),
            pltpu.VMEM((ROWS * 8, HD), F32),
            pltpu.VMEM((ROWS * 8, HD), F32),
            pltpu.VMEM((ROWS, 2 * HD), BF),
            pltpu.VMEM((ROWS, EC), BF),
            pltpu.VMEM((ROWS, HEADS * HD), BF),
            pltpu.VMEM((ROWS, NS, WIDE), BF),
            pltpu.VMEM((ROWS, NS, EC), F32),
            pltpu.VMEM((GROUP * NS, EC), BF),
            pltpu.VMEM((ROWS, EC), F32),
            pltpu.VMEM((ROWS * 8, HD), F32),
            pltpu.VMEM((ROWS * 8, HD), F32),
            pltpu.SemaphoreType.DMA((10,)),
            pltpu.SemaphoreType.DMA((ENT // GROUP,)),
            pltpu.SemaphoreType.DMA((ROWS,)),
        ],
        compiler_params=ALONE,
        cost_estimate=cost(16 << 20, 8 << 20),
        name="update_and_join",
    )(*operands)


def swap(values):
    order = [[LAST - p for p in range(PEERS)]]
    return lax.all_to_all(
        values, "rep", split_axis=0, concat_axis=0, tiled=True, axis_index_groups=order
    )


def shards(
    x_in, z_gate, conv_state, conv_pool, ssm_state, ssm_pool, conv_weight, conv_bias, x_proj,
    dt_gain, b_gain, c_gain, dt_proj, dt_bias, decay_rate, skip, query, new_kv, kv_cache, kv_pool,
    ctx_len, row_owner, row_pos, swap_slot, swap_lens, swap_pages,
):
    slots = swap_slot.transpose(0, 2, 1)
    first = swap(pack(slots, row_owner, row_pos, conv_pool.transpose(1, 0, 2), query))
    source = jnp.where(row_owner >= 0, (LAST - row_owner) * CAP + row_pos, -1)
    states, bias, rest = prepare(slots, swap_pages, swap_lens.transpose(0, 2, 1), ssm_pool)
    states, flag = serve(first, bias, rest, kv_pool, states)
    second = swap(states.reshape(PEERS, CAP * NS, WIDE)).reshape(ENT, NS, WIDE)

    mixed, window, part, send = mix(
        flag, source, first, conv_state.transpose(1, 0, 2), x_in, conv_weight,
        conv_bias.reshape(1, EC), x_proj.T,
    )
    tp = lax.axis_size("tp")
    others = [
        lax.ppermute(send, "tp", [(i, (i + s) % tp) for i in range(tp)]) for s in range(1, tp)
    ]
    mix_here, score = resident(flag, ctx_len, query, new_kv, kv_cache)
    dt, drive, inject, read, gate, base, kept = step_size(
        source, part, others, dt_gain.reshape(1, RANK),
        jnp.concatenate([b_gain, c_gain]).reshape(1, 2 * NS), dt_proj, dt_bias.reshape(1, EC), mixed,
        skip.reshape(1, EC), z_gate, decay_rate, ssm_state,
    )
    new_ssm, mamba_out, attn_out = tail(
        source, second, dt, drive, inject, read, decay_rate, gate, base, mix_here, score, new_kv, kept
    )
    return (mamba_out, attn_out, new_ssm, window.transpose(1, 0, 2))


def solution(mesh):
    in_specs = (
        P("rep", "tp"), P("rep", "tp"), P("rep", None, "tp"), P("rep", None, "tp"),
        P("rep", None, "tp"), P("rep", None, "tp"), P(None, "tp"), P("tp"), P("tp", None),
        P(), P(), P(), P(None, "tp"), P("tp"), P(None, "tp"), P("tp"), P("rep", "tp"),
        P("rep", "tp"), P("rep", None, "tp"), P("rep", None, "tp"), P("rep"), P("rep"), P("rep"),
        P("rep", None, None), P("rep", None, None), P("rep", None, None, None),
    )
    out_specs = (P("rep", "tp"), P("rep", "tp"), P("rep", None, "tp"), P("rep", None, "tp"))
    return jax.shard_map(shards, mesh=mesh, in_specs=in_specs, out_specs=out_specs, check_vma=False)
```

time: 97 us -> 69.5 us (0.72)
  the two profiles are of different devices: /device:TPU:0 before, /device:TPU:1 now
where the time goes in v2:
time: 69.5 us; the launch traced here: 68.8 us
  Pallas kernels  34.7 us (50%)
  starting transfers between devices  28.5 us (41%)
  waiting for transfers between devices  2.14 us (3%)
  local copies, waits for them, and re-layouts  1.44 us (2%)
  other arithmetic  1.17 us (2%)
  between operations  0.82 us (1%)
    all_to_all x2, starting transfers between devices, swap(): lax.all_to_all(values, 'rep', split_axis=0, concat_axis=0, tiled=True, ax...  18.2 us
    ppermute x7, starting transfers between devices, shards(): lax.ppermute(send, 'tp', [(i, (i + s) % tp) for i in range(tp)])  10.3 us
    pallas_call x1, Pallas kernels, step_size(): pl.pallas_call(step_kernel, out_shape=(jax.ShapeDtypeStruct((ROWS, 1, EC)...  6.79 us
    pallas_call x1, Pallas kernels, resident(): pl.pallas_call(resident_kernel, grid=(ROWS // BLK,), out_shape=(shape, sh...  5.93 us
    pallas_call x1, Pallas kernels, tail(): pl.pallas_call(tail_kernel, out_shape=(jax.ShapeDtypeStruct((ROWS, NS, EC...  5.67 us
    pallas_call x1, Pallas kernels, serve(): pl.pallas_call(serve_kernel, out_shape=(jax.ShapeDtypeStruct((ENT, NS, WI...  5.36 us
    pallas_call x1, Pallas kernels, prepare(): pl.pallas_call(prepare_kernel, out_shape=(jax.ShapeDtypeStruct((ENT, NS,...  5.05 us
    pallas_call x1, Pallas kernels, mix(): pl.pallas_call(mix_kernel, out_shape=(jax.ShapeDtypeStruct((ROWS, EC), BF...  3.65 us
  transfers between devices with their start and end apart: 9, of which 1 were waited for; matrix products, arithmetic and copies ran while one was open for 2% of the time, Pallas kernels for 31%

profile of v2, /device:TPU:1, one launch (start us, length us, event | category | flops | bytes accessed | tf_op | source)
XLA Modules:
  0.0 68.8 jit_solution(9597672486399219325)
XLA Ops:
  0.6 2.3 %pack_first.1 = bf16[16,16,1024]{2,1,0:T(8,128)(2,1)} custom-call(s32[1,2,16]{2,1,0:T(2,128)} %bitcast.21, s32[32]{0:T(128)} %owner_hbm.1, s32[32]{0:T(128)} %pos_hbm.1, bf16[3,32,2048]{2,1,0:T(8,128)(2,1)} %bitcast.17, bf16[32,1024]{1,0:T(8,128)(2,1)} %query_ref.3), custom_call_target="tpu_custom_call" | custom-call | flops 134217728 | bytes 1048576 | tf_op jit(solution)/shard_map/pack_first/pallas_call | solution.py:112
  2.9 10.3 %all-to-all-start = ((bf16[16,16,1024]{2,1,0:T(8,128)(2,1)}), bf16[16,16,1024]{2,1,0:T(8,128)(2,1)S(1)}, u32[]{:S(2)}, u32[]{:S(2)}) async-start(bf16[16,16,1024]{2,1,0:T(8,128)(2,1)} %pack_first.1), calls=%async_computation | async-start | bytes 1048576 | tf_op jit(solution)/shard_map/all_to_all | solution.py:742
  13.2 5.0 %prepare_owner.1 = (bf16[32,16,2176]{2,1,0:T(8,128)(2,1)}, f32[2,256,128]{2,1,0:T(8,128)}, f32[1,128]{1,0:T(1,128)}) custom-call(s32[1,2,16]{2,1,0:T(2,128)} %bitcast.22, s32[1,16,2,32]{3,2,1,0:T(2,128)} %pages_hbm.1, s32[1,2,16]{2,1,0:T(2,128)} %bitcast.24, f32[32,16,2048]{2,1,0:T(8,128)} %ssm_ref.1), custom_call_target="tpu_custom_call" | custom-call | flops 1048576 | bytes 6291456 | tf_op jit(solution)/shard_map/prepare_owner/pallas_call | solution.py:200
  18.2 2.1 %all-to-all-done.recv_hbm.recv_ref = bf16[16,16,1024]{2,1,0:T(8,128)(2,1)S(1)} async-done(((bf16[16,16,1024]{2,1,0:T(8,128)(2,1)}), bf16[16,16,1024]{2,1,0:T(8,128)(2,1)S(1)}, u32[]{:S(2)}, u32[]{:S(2)}) %all-to-all-start) | async-done | bytes 524320 | tf_op jit(solution)/shard_map/all_to_all | solution.py:742
  20.3 0.8 %copy-done = bf16[16,16,1024]{2,1,0:T(8,128)(2,1)} copy-done((bf16[16,16,1024]{2,1,0:T(8,128)(2,1)}, bf16[16,16,1024]{2,1,0:T(8,128)(2,1)S(1)}, u32[]{:S(2)}) %copy-start) | copy-done | bytes 524312
  21.1 5.4 %serve_pool.1 = (bf16[32,16,2176]{2,1,0:T(8,128)(2,1)}, f32[1,128]{1,0:T(1,128)}) custom-call(bf16[16,16,1024]{2,1,0:T(8,128)(2,1)} %copy-done, f32[2,256,128]{2,1,0:T(8,128)} %get-tuple-element.25.bias_hbm, f32[1,128]{1,0:T(1,128)} %get-tuple-element.26.rest_hbm, bf16[256,16,256]{2,1,0:T(8,128)(2,1)} %pool_hbm.1, ...), custom_call_target="tpu_custom_call", output_to_operand_aliasing={{0}: (4, {})} | custom-call | flops 536870912 | bytes 6291456 | tf_op jit(solution)/shard_map/serve_pool/pallas_call | solution.py:301
  26.5 0.0 copy-start.8
  26.5 0.0 copy-start.9
  26.5 7.9 %all-to-all-start.1 = ((bf16[16,32,2176]{2,1,0:T(8,128)(2,1)}), bf16[16,32,2176]{2,1,0:T(8,128)(2,1)}, u32[]{:S(2)}, u32[]{:S(2)}) async-start(bf16[16,32,2176]{2,1,0:T(8,128)(2,1)} %bitcast.14), calls=%async_computation.1 | async-start | bytes 4456448 | tf_op jit(solution)/shard_map/all_to_all | solution.py:742
  34.4 0.0 copy-done.8
  34.4 0.0 copy-done.9
  34.4 0.0 copy-start.10
  34.4 0.0 copy-start.11
  34.4 0.5 compare_select_fusion.source_ref.refs_0_
  35.0 3.7 %mix_input.1 = (bf16[32,2048]{1,0:T(8,128)(2,1)}, bf16[3,32,2048]{2,1,0:T(8,128)(2,1)}, f32[32,544]{1,0:T(8,128)}, bf16[32,544]{1,0:T(8,128)(2,1)}) custom-call(f32[1,128]{1,0:T(1,128)} %get-tuple-element.29.flag_ref, s32[32]{0:T(128)} %compare_select_fusion.source_ref.refs_0_, bf16[16,16,1024]{2,1,0:T(8,128)(2,1)} %copy-done, ...), custom_call_target="tpu_custom_call" | custom-call | flops 71303168 | bytes 4194304 | tf_op jit(solution)/shard_map/mix_input/pallas_call | solution.py:440
  38.6 2.1 %collective-permute-start.6 = (bf16[32,544]{1,0:T(8,128)(2,1)}, bf16[32,544]{1,0:T(8,128)(2,1)S(1)}, u32[]{:S(2)}, u32[]{:S(2)}) collective-permute-start(bf16[32,544]{1,0:T(8,128)(2,1)} %get-tuple-element.31), channel_id=1, source_target_pairs={{0,7},{1,0},{2,1},{3,2},{4,3},{5,4},{6,5},{7,6},{8,15},{9,8},{10,9... | collective-permute-start | bytes 104456 | tf_op jit(solution)/shard_map/ppermute | solution.py:765
  40.7 2.7 %collective-permute-start.5 = (bf16[32,544]{1,0:T(8,128)(2,1)}, bf16[32,544]{1,0:T(8,128)(2,1)S(1)}, u32[]{:S(2)}, u32[]{:S(2)}) collective-permute-start(bf16[32,544]{1,0:T(8,128)(2,1)} %get-tuple-element.31), channel_id=1, source_target_pairs={{0,6},{1,7},{2,0},{3,1},{4,2},{5,3},{6,4},{7,5},{8,14},{9,15},{10,... | collective-permute-start | bytes 104456 | tf_op jit(solution)/shard_map/ppermute | solution.py:765
  43.4 0.7 collective-permute-start.4
  44.1 1.1 %collective-permute-start.3 = (bf16[32,544]{1,0:T(8,128)(2,1)}, bf16[32,544]{1,0:T(8,128)(2,1)S(1)}, u32[]{:S(2)}, u32[]{:S(2)}) collective-permute-start(bf16[32,544]{1,0:T(8,128)(2,1)} %get-tuple-element.31), channel_id=1, source_target_pairs={{0,4},{1,5},{2,6},{3,7},{4,0},{5,1},{6,2},{7,3},{8,12},{9,13},{10,... | collective-permute-start | bytes 104456 | tf_op jit(solution)/shard_map/ppermute | solution.py:765
  45.2 2.1 %collective-permute-start.2 = (bf16[32,544]{1,0:T(8,128)(2,1)}, bf16[32,544]{1,0:T(8,128)(2,1)S(1)}, u32[]{:S(2)}, u32[]{:S(2)}) collective-permute-start(bf16[32,544]{1,0:T(8,128)(2,1)} %get-tuple-element.31), channel_id=1, source_target_pairs={{0,3},{1,4},{2,5},{3,6},{4,7},{5,0},{6,1},{7,2},{8,11},{9,12},{10,... | collective-permute-start | bytes 104456 | tf_op jit(solution)/shard_map/ppermute | solution.py:765
  47.3 0.0 collective-permute-done.6.refs_8_
  47.3 0.7 %collective-permute-start.1 = (bf16[32,544]{1,0:T(8,128)(2,1)}, bf16[32,544]{1,0:T(8,128)(2,1)S(1)}, u32[]{:S(2)}, u32[]{:S(2)}) collective-permute-start(bf16[32,544]{1,0:T(8,128)(2,1)} %get-tuple-element.31), channel_id=1, source_target_pairs={{0,2},{1,3},{2,4},{3,5},{4,6},{5,7},{6,0},{7,1},{8,10},{9,11},{10,... | collective-permute-start | bytes 104456 | tf_op jit(solution)/shard_map/ppermute | solution.py:765
  48.0 0.0 collective-permute-done.5.refs_7_
  48.0 0.9 %collective-permute-start = (bf16[32,544]{1,0:T(8,128)(2,1)}, bf16[32,544]{1,0:T(8,128)(2,1)S(1)}, u32[]{:S(2)}, u32[]{:S(2)}) collective-permute-start(bf16[32,544]{1,0:T(8,128)(2,1)} %get-tuple-element.31), channel_id=1, source_target_pairs={{0,1},{1,2},{2,3},{3,4},{4,5},{5,6},{6,7},{7,0},{8,9},{9,10},{10,1... | collective-permute-start | bytes 104456 | tf_op jit(solution)/shard_map/ppermute | solution.py:765
  49.0 0.0 copy-done.10
  49.0 0.0 copy-done.11
  49.0 0.6 maximum_bitcast_fusion.refs_10_
  49.6 5.9 %resident_attention.1 = (f32[256,128]{1,0:T(8,128)}, f32[256,128]{1,0:T(8,128)}) custom-call(f32[1,128]{1,0:T(1,128)} %get-tuple-element.29.flag_ref, s32[32]{0:T(128)} %len_ref.1, bf16[32,1024]{1,0:T(8,128)(2,1)} %query_ref.3, bf16[32,256]{1,0:T(8,128)(2,1)} %new_kv_hbm.1, bf16[32,512,256]{2,1,0:T(8,128)(2,1)} %cache_ref.1), custom_call_target="tpu_custom_call" | custom-call | flops 67108864 | bytes 9437184 | tf_op jit(solution)/shard_map/resident_attention/pallas_call | solution.py:384
  55.5 0.0 copy-done.1
  55.5 0.0 copy-done.2
  55.6 0.0 collective-permute-done.4.refs_6_
  55.6 0.0 copy-start.3
  55.6 0.0 collective-permute-done.3.refs_5_
  55.6 0.0 copy-start.4
  55.6 0.0 collective-permute-done.2.refs_4_
  55.6 0.0 copy-start.5
  55.6 0.0 collective-permute-done.1.refs_3_
  55.6 0.0 copy-start.6
  55.6 0.0 collective-permute-done.refs_2_
  55.6 0.0 copy-start.7
  55.7 0.5 copy-done.3
  56.2 0.0 copy-done.4
  56.2 0.0 copy-done.5
  56.2 0.0 copy-done.6
  56.2 0.0 copy-done.7
  56.3 6.8 %step_and_resident.1 = (f32[32,1,2048]{2,1,0:T(1,128)}, f32[32,1,2048]{2,1,0:T(1,128)}, f32[32,16,128]{2,1,0:T(8,128)}, f32[32,128]{1,0:T(8,128)}, f32[32,2048]{...) custom-call(s32[32]{0:T(128)} %compare_select_fusion.source_ref.refs_0_, f32[32,544]{1,0:T(8,128)} %get-tuple-element.30.refs_1_, ...), custom_call_target="tpu_custom_call" | custom-call | flops 67108864 | bytes 12582912 | tf_op jit(solution)/shard_map/step_and_resident/pallas_call | solution.py:557
  63.1 0.0 all-to-all-done.1
  63.1 5.7 %update_and_join.1 = (f32[32,16,2048]{2,1,0:T(8,128)}, bf16[32,2048]{1,0:T(8,128)(2,1)}, bf16[32,1024]{1,0:T(8,128)(2,1)}) custom-call(s32[32]{0:T(128)} %compare_select_fusion.source_ref.refs_0_, bf16[32,16,2176]{2,1,0:T(8,128)(2,1)} %bitcast.4.recv_hbm, f32[32,1,2048]{2,1,0:T(1,128)} %get-tuple-element.33.dt_hbm, ...), custom_call_target="tpu_custom_call", output_to_operand_aliasing={{0}: (12, {})} | custom-call | flops 16777216 | bytes 8388608 | tf_op jit(solution)/shard_map/update_and_join/pallas_call | solution.py:701
  (3 shorter events, 0.0 us)
Async XLA Ops:
  2.9 17.4 %all-to-all-start = ((bf16[16,16,1024]{2,1,0:T(8,128)(2,1)}), bf16[16,16,1024]{2,1,0:T(8,128)(2,1)S(1)}, u32[]{:S(2)}, u32[]{:S(2)}) async-start(bf16[16,16,1024]{2,1,0:T(8,128)(2,1)} %pack_first.1), calls=%async_computation | async-start | bytes 1048576 | tf_op jit(solution)/shard_map/all_to_all | solution.py:742
  20.3 0.8 %copy-start = (bf16[16,16,1024]{2,1,0:T(8,128)(2,1)}, bf16[16,16,1024]{2,1,0:T(8,128)(2,1)S(1)}, u32[]{:S(2)}) copy-start(bf16[16,16,1024]{2,1,0:T(8,128)(2,1)S(1)} %all-to-all-done.recv_hbm.recv_ref) | copy-start | bytes 1572868
  26.5 7.9 %copy-start.8 = (s32[32]{0:T(128)S(1)}, s32[32]{0:T(128)}, u32[]{:S(2)}) copy-start(s32[32]{0:T(128)} %owner_hbm.1) | copy-start | bytes 388
  26.5 7.9 %copy-start.9 = (s32[32]{0:T(128)S(1)}, s32[32]{0:T(128)}, u32[]{:S(2)}) copy-start(s32[32]{0:T(128)} %pos_hbm.1) | copy-start | bytes 388
  26.5 36.6 %all-to-all-start.1 = ((bf16[16,32,2176]{2,1,0:T(8,128)(2,1)}), bf16[16,32,2176]{2,1,0:T(8,128)(2,1)}, u32[]{:S(2)}, u32[]{:S(2)}) async-start(bf16[16,32,2176]{2,1,0:T(8,128)(2,1)} %bitcast.14), calls=%async_computation.1 | async-start | bytes 4456448 | tf_op jit(solution)/shard_map/all_to_all | solution.py:742
  34.4 14.5 %copy-start.10 = (f32[16]{0:T(128)S(1)}, f32[16]{0:T(128)}, u32[]{:S(2)}) copy-start(f32[16]{0:T(128)} %param.37) | copy-start | bytes 196
  34.4 14.5 %copy-start.11 = (f32[16]{0:T(128)S(1)}, f32[16]{0:T(128)}, u32[]{:S(2)}) copy-start(f32[16]{0:T(128)} %param.36) | copy-start | bytes 196
  38.6 8.7 %collective-permute-start.6 = (bf16[32,544]{1,0:T(8,128)(2,1)}, bf16[32,544]{1,0:T(8,128)(2,1)S(1)}, u32[]{:S(2)}, u32[]{:S(2)}) collective-permute-start(bf16[32,544]{1,0:T(8,128)(2,1)} %get-tuple-element.31), channel_id=1, source_target_pairs={{0,7},{1,0},{2,1},{3,2},{4,3},{5,4},{6,5},{7,6},{8,15},{9,8},{10,9... | collective-permute-start | bytes 104456 | tf_op jit(solution)/shard_map/ppermute | solution.py:765
  40.7 7.3 %collective-permute-start.5 = (bf16[32,544]{1,0:T(8,128)(2,1)}, bf16[32,544]{1,0:T(8,128)(2,1)S(1)}, u32[]{:S(2)}, u32[]{:S(2)}) collective-permute-start(bf16[32,544]{1,0:T(8,128)(2,1)} %get-tuple-element.31), channel_id=1, source_target_pairs={{0,6},{1,7},{2,0},{3,1},{4,2},{5,3},{6,4},{7,5},{8,14},{9,15},{10,... | collective-permute-start | bytes 104456 | tf_op jit(solution)/shard_map/ppermute | solution.py:765
  43.4 12.1 %collective-permute-start.4 = (bf16[32,544]{1,0:T(8,128)(2,1)}, bf16[32,544]{1,0:T(8,128)(2,1)S(1)}, u32[]{:S(2)}, u32[]{:S(2)}) collective-permute-start(bf16[32,544]{1,0:T(8,128)(2,1)} %get-tuple-element.31), channel_id=1, source_target_pairs={{0,5},{1,6},{2,7},{3,0},{4,1},{5,2},{6,3},{7,4},{8,13},{9,14},{10,... | collective-permute-start | bytes 104456 | tf_op jit(solution)/shard_map/ppermute | solution.py:765
  44.1 11.5 %collective-permute-start.3 = (bf16[32,544]{1,0:T(8,128)(2,1)}, bf16[32,544]{1,0:T(8,128)(2,1)S(1)}, u32[]{:S(2)}, u32[]{:S(2)}) collective-permute-start(bf16[32,544]{1,0:T(8,128)(2,1)} %get-tuple-element.31), channel_id=1, source_target_pairs={{0,4},{1,5},{2,6},{3,7},{4,0},{5,1},{6,2},{7,3},{8,12},{9,13},{10,... | collective-permute-start | bytes 104456 | tf_op jit(solution)/shard_map/ppermute | solution.py:765
  45.2 10.4 %collective-permute-start.2 = (bf16[32,544]{1,0:T(8,128)(2,1)}, bf16[32,544]{1,0:T(8,128)(2,1)S(1)}, u32[]{:S(2)}, u32[]{:S(2)}) collective-permute-start(bf16[32,544]{1,0:T(8,128)(2,1)} %get-tuple-element.31), channel_id=1, source_target_pairs={{0,3},{1,4},{2,5},{3,6},{4,7},{5,0},{6,1},{7,2},{8,11},{9,12},{10,... | collective-permute-start | bytes 104456 | tf_op jit(solution)/shard_map/ppermute | solution.py:765
  47.3 8.2 %copy-start.1 = (bf16[32,544]{1,0:T(8,128)(2,1)}, bf16[32,544]{1,0:T(8,128)(2,1)S(1)}, u32[]{:S(2)}) copy-start(bf16[32,544]{1,0:T(8,128)(2,1)S(1)} %collective-permute-done.6.refs_8_) | copy-start | bytes 104452
  47.3 8.3 %collective-permute-start.1 = (bf16[32,544]{1,0:T(8,128)(2,1)}, bf16[32,544]{1,0:T(8,128)(2,1)S(1)}, u32[]{:S(2)}, u32[]{:S(2)}) collective-permute-start(bf16[32,544]{1,0:T(8,128)(2,1)} %get-tuple-element.31), channel_id=1, source_target_pairs={{0,2},{1,3},{2,4},{3,5},{4,6},{5,7},{6,0},{7,1},{8,10},{9,11},{10,... | collective-permute-start | bytes 104456 | tf_op jit(solution)/shard_map/ppermute | solution.py:765
  48.0 7.5 %copy-start.2 = (bf16[32,544]{1,0:T(8,128)(2,1)}, bf16[32,544]{1,0:T(8,128)(2,1)S(1)}, u32[]{:S(2)}) copy-start(bf16[32,544]{1,0:T(8,128)(2,1)S(1)} %collective-permute-done.5.refs_7_) | copy-start | bytes 104452
  48.0 7.6 %collective-permute-start = (bf16[32,544]{1,0:T(8,128)(2,1)}, bf16[32,544]{1,0:T(8,128)(2,1)S(1)}, u32[]{:S(2)}, u32[]{:S(2)}) collective-permute-start(bf16[32,544]{1,0:T(8,128)(2,1)} %get-tuple-element.31), channel_id=1, source_target_pairs={{0,1},{1,2},{2,3},{3,4},{4,5},{5,6},{6,7},{7,0},{8,9},{9,10},{10,1... | collective-permute-start | bytes 104456 | tf_op jit(solution)/shard_map/ppermute | solution.py:765
  55.6 0.6 copy-start.3
  55.6 0.6 copy-start.4
  55.6 0.6 copy-start.5
  55.6 0.6 copy-start.6
  55.6 0.6 copy-start.7

commit v3 on v2

--- a/solution.py
+++ b/solution.py
@@ -85,13 +85,13 @@
 
         @pl.when(owner >= 0)
         def _():
-            inverse[(LAST - owner) * CAP + pos_ref[r]] = 192 + r
+            inverse[owner * CAP + pos_ref[r]] = 192 + r
 
     lane = iota((8, 256), 1)
     part = iota((8, 256), 0)
     tiles = []
     for e in range(ENT):
-        slot = slot_ref[0, e % CAP, LAST - e // CAP]
+        slot = slot_ref[0, e % CAP, e // CAP]
         want = jnp.where(part < 6, 32 * part + slot, jnp.where(part == 6, inverse[e], -1))
         tiles.append((lane == want).astype(F32))
     pick = jnp.concatenate(tiles, axis=0).astype(BF)
@@ -130,18 +130,25 @@
 
 
 def prepare_kernel(
-    slot_hbm, pages_hbm, lens_hbm, ssm_ref, states_ref, bias_ref, rest_ref,
-    slot_ref, pages_ref, lens_ref, states, packed, sems, in_sems, out_sems,
+    slot_hbm, owner_hbm, pos_hbm, pages_hbm, lens_hbm, ssm_ref,
+    states_ref, bias_ref, rest_ref, source_ref, state_source_ref,
+    slot_ref, owner_ref, pos_ref, pages_ref, lens_ref, states, packed, sems, in_sems, out_sems,
 ):
-    first = pltpu.make_async_copy(slot_hbm, slot_ref, sems.at[0])
-    first.start()
+    first = [
+        pltpu.make_async_copy(slot_hbm, slot_ref, sems.at[0]),
+        pltpu.make_async_copy(owner_hbm, owner_ref, sems.at[3]),
+        pltpu.make_async_copy(pos_hbm, pos_ref, sems.at[4]),
+    ]
+    for copy in first:
+        copy.start()
     lists = [
         pltpu.make_async_copy(pages_hbm, pages_ref, sems.at[1]),
         pltpu.make_async_copy(lens_hbm, lens_ref, sems.at[2]),
     ]
     for copy in lists:
         copy.start()
-    first.wait()
+    for copy in first:
+        copy.wait()
 
     def fetch(k):
         return pltpu.make_async_copy(
@@ -155,6 +162,12 @@
 
     for k in range(4):
         fetch(k).start()
+    for r in range(ROWS):
+        owner = owner_ref[r]
+        resumed = owner >= 0
+        pos = pos_ref[r]
+        source_ref[r] = jnp.where(resumed, owner * CAP + pos, -1)
+        state_source_ref[r] = jnp.where(resumed, (LAST - owner) * CAP + pos, -1)
     for copy in lists:
         copy.wait()
 
@@ -196,37 +209,41 @@
         give(k).wait()
 
 
-def prepare(slots, pages, lens, ssm_pool):
+def prepare(slots, owner, pos, pages, lens, ssm_pool):
     return pl.pallas_call(
         prepare_kernel,
         out_shape=(
             jax.ShapeDtypeStruct((ENT, NS, WIDE), BF),
             jax.ShapeDtypeStruct((2, POOL, 128), F32),
             jax.ShapeDtypeStruct((1, 128), F32),
+            jax.ShapeDtypeStruct((ROWS,), I32),
+            jax.ShapeDtypeStruct((ROWS,), I32),
         ),
-        in_specs=[HB] * 4,
-        out_specs=(HB, VM, VM),
+        in_specs=[HB] * 6,
+        out_specs=(HB, VM, VM, SM, SM),
         scratch_shapes=[
             pltpu.SMEM((1, CAP, PEERS), I32),
+            pltpu.SMEM((ROWS,), I32),
+            pltpu.SMEM((ROWS,), I32),
             pltpu.VMEM((1, PEERS, CAP, CTX // PAGE), I32),
             pltpu.VMEM((1, CAP, PEERS), I32),
             pltpu.VMEM((ENT, NS, EC), F32),
             pltpu.VMEM((ENT, NS, EC), BF),
-            pltpu.SemaphoreType.DMA((3,)),
+            pltpu.SemaphoreType.DMA((5,)),
             pltpu.SemaphoreType.DMA((4,)),
             pltpu.SemaphoreType.DMA((4,)),
         ],
         compiler_params=ALONE,
         cost_estimate=cost(1 << 20, 6 << 20),
         name="prepare_owner",
-    )(slots, pages, lens, ssm_pool)
+    )(slots, owner, pos, pages, lens, ssm_pool)
 
 
 PARTS = 4
 
 
 def serve_kernel(
-    recv_hbm, bias_hbm, rest_hbm, pool_hbm, send_ref, out_ref, flag_ref,
+    recv_hbm, bias_hbm, rest_hbm, pool_hbm, send_ref, out_ref,
     recv_ref, bias_ref, rest_ref, pool_ref, scores, back, slab, sems,
 ):
     loads = [
@@ -240,7 +257,9 @@
     for copy in loads:
         copy.start()
     lane = iota((ENT, 256), 1)
-    pick = (lane == 8 * iota((ENT, 256), 0) + 6).astype(F32).astype(BF)
+    entry = iota((ENT, 256), 0)
+    entry = CAP * (LAST - entry // CAP) + entry % CAP
+    pick = (lane == 8 * entry + 6).astype(F32).astype(BF)
     loads[0].wait()
     recv = recv_ref[...].reshape(256, HALF)
     query = jnp.dot(pick, recv, preferred_element_type=F32).astype(BF)
@@ -293,19 +312,15 @@
     slab[...] = back[...].astype(BF).reshape(ENT, 16, HD)
     copy = pltpu.make_async_copy(slab, out_ref.at[:, :, EC:WIDE], sems.at[0])
     copy.start()
-    flag_ref[...] = top[:, 0:HD]
     copy.wait()
 
 
 def serve(recv, bias, rest, kv_pool, send):
     return pl.pallas_call(
         serve_kernel,
-        out_shape=(
-            jax.ShapeDtypeStruct((ENT, NS, WIDE), BF),
-            jax.ShapeDtypeStruct((1, HD), F32),
-        ),
+        out_shape=jax.ShapeDtypeStruct((ENT, NS, WIDE), BF),
         in_specs=[HB] * 4 + [AN],
-        out_specs=(AN, VM),
+        out_specs=AN,
         input_output_aliases={4: 0},
         scratch_shapes=[
             pltpu.VMEM((PEERS, 16, HALF), BF),
@@ -327,7 +342,7 @@
 
 
 def resident_kernel(
-    flag_ref, len_ref, query_ref, new_ref, cache_ref, mix_ref, score_ref, heads
+    after_ref, len_ref, query_ref, new_ref, cache_ref, mix_ref, score_ref, heads
 ):
     step = pl.program_id(0)
 
@@ -378,7 +393,7 @@
     score_ref[...] = jnp.broadcast_to(score * LN2, (rows, HD))
 
 
-def resident(flag, lens, query, new_kv, kv_cache):
+def resident(after, lens, query, new_kv, kv_cache):
     tile = pl.BlockSpec((BLK * 8, HD), lambda i: (i, 0))
     shape = jax.ShapeDtypeStruct((ROWS * 8, HD), F32)
     return pl.pallas_call(
@@ -397,11 +412,11 @@
         compiler_params=params(58),
         cost_estimate=cost(4 * ROWS * 8 * CTX * HD, 9 << 20),
         name="resident_attention",
-    )(flag, lens, query, new_kv, kv_cache)
+    )(after, lens, query, new_kv, kv_cache)
 
 
 def mix_kernel(
-    flag_ref, source_ref, recv_ref, conv_ref, x_ref, weight_ref, bias_ref, proj_ref,
+    after_ref, source_ref, recv_ref, conv_ref, x_ref, weight_ref, bias_ref, proj_ref,
     mixed_ref, window_ref, part_ref, send_ref,
 ):
     sub = iota((ROWS, 256), 0)
@@ -435,7 +450,7 @@
     send_ref[...] = part.astype(BF)
 
 
-def mix(flag, source, recv, conv_state, x_in, weight, bias, proj_t):
+def mix(after, source, recv, conv_state, x_in, weight, bias, proj_t):
     wide = proj_t.shape[0]
     return pl.pallas_call(
         mix_kernel,
@@ -450,7 +465,7 @@
         compiler_params=ALONE,
         cost_estimate=cost(2 * ROWS * EC * wide, 4 << 20),
         name="mix_input",
-    )(flag, source, recv, conv_state, x_in, weight, bias, proj_t)
+    )(after, source, recv, conv_state, x_in, weight, bias, proj_t)
 
 
 GROUP = 8
@@ -464,7 +479,7 @@
     source_ref, part_ref = refs[0:2]
     others = refs[2:9]
     (
-        gain_ref, tail_gain_ref, proj_ref, bias_ref, mixed_ref, skip_ref, z_ref, decay_ref, state_ref,
+        gain_ref, b_gain_ref, c_gain_ref, proj_ref, bias_ref, mixed_ref, skip_ref, z_ref, decay_ref, state_ref,
         dt_ref, drive_ref, inject_ref, read_ref, gate_ref, base_ref, new_ref,
         local, made, flat, in_sems, out_sems,
     ) = refs[9:]
@@ -505,7 +520,8 @@
     mean_b = jnp.sum(jnp.where(front, square, 0.0), axis=1, keepdims=True) * (1.0 / NS)
     mean_c = jnp.sum(jnp.where(front, 0.0, square), axis=1, keepdims=True) * (1.0 / NS)
     scale = lax.rsqrt(jnp.where(front, mean_b, mean_c) + 1e-6)
-    tail = (tail * scale * tail_gain_ref[...]).astype(BF)
+    tail_gain = jnp.concatenate([b_gain_ref[...], c_gain_ref[...]], axis=1)
+    tail = (tail * scale * tail_gain).astype(BF)
     lane = iota((2 * NS, 128), 1)
     spread = (iota((2 * NS, 128), 0) == NS + lane % NS).astype(F32).astype(BF)
     read = jnp.dot(tail, spread, preferred_element_type=F32)
@@ -565,7 +581,7 @@
             jax.ShapeDtypeStruct((ROWS, EC), F32),
             jax.ShapeDtypeStruct((ROWS, NS, EC), F32),
         ),
-        in_specs=[SM] + [VM] * 16 + [HB],
+        in_specs=[SM] + [VM] * 17 + [HB],
         out_specs=(VM,) * 6 + (HB,),
         scratch_shapes=[
             pltpu.VMEM((ROWS, NS, EC), F32),
@@ -581,34 +597,11 @@
 
 
 def tail_kernel(
-    source_ref, recv_hbm, dt_hbm, drive_hbm, inject_hbm, read_hbm, decay_hbm,
-    gate_hbm, base_hbm, mix_hbm, score_hbm, new_kv_hbm, kept_ref,
+    source_ref, came, dt_ref, drive_ref, inject_ref, read_ref, decay_ref,
+    gate_ref, base_ref, mix_ref, score_ref, new_kv_ref, kept_ref,
     new_ref, out_hbm, attn_hbm,
-    dt_ref, drive_ref, inject_ref, read_ref, decay_ref, gate_ref, base_ref, mix_ref, score_ref,
-    new_kv_ref, out_ref, attn_ref,
-    came, made, flat, sums, other, pieces, sems, in_sems, out_sems,
+    out_ref, attn_ref, made, flat, sums, other, pieces, sems, out_sems,
 ):
-    def fetch(k):
-        part = slice(k * GROUP, (k + 1) * GROUP)
-        return pltpu.make_async_copy(recv_hbm.at[part], came.at[part], in_sems.at[k])
-
-    pairs = [
-        (dt_hbm, dt_ref), (drive_hbm, drive_ref), (inject_hbm, inject_ref), (read_hbm, read_ref),
-        (decay_hbm, decay_ref), (mix_hbm, mix_ref), (gate_hbm, gate_ref), (base_hbm, base_ref),
-        (score_hbm, score_ref), (new_kv_hbm, new_kv_ref),
-    ]
-    loads = [pltpu.make_async_copy(a, b, sems.at[k]) for k, (a, b) in enumerate(pairs)]
-    for copy in loads[:5]:
-        copy.start()
-    for k in range(ENT // GROUP):
-        fetch(k).start()
-    for copy in loads[5:]:
-        copy.start()
-    for copy in loads[:6]:
-        copy.wait()
-    for k in range(ENT // GROUP):
-        fetch(k).wait()
-
     def store(r):
         return pltpu.make_async_copy(made.at[r], new_ref.at[r], out_sems.at[r])
 
@@ -672,8 +665,6 @@
         return carry
 
     lax.fori_loop(0, ROWS // GROUP, body, 0)
-    for copy in loads[6:]:
-        copy.wait()
     out_ref[...] = (sums[...] * gate_ref[...] + base_ref[...]).astype(BF)
     give_out = pltpu.make_async_copy(out_ref, out_hbm, sems.at[0])
     give_out.start()
@@ -705,30 +696,18 @@
             jax.ShapeDtypeStruct((ROWS, EC), BF),
             jax.ShapeDtypeStruct((ROWS, HEADS * HD), BF),
         ),
-        in_specs=[SM] + [HB] * 11 + [AN],
+        in_specs=[SM] + [VM] * 11 + [AN],
         out_specs=(AN, HB, HB),
         input_output_aliases={12: 0},
         scratch_shapes=[
-            pltpu.VMEM((ROWS, 1, EC), F32),
-            pltpu.VMEM((ROWS, 1, EC), F32),
-            pltpu.VMEM((ROWS, NS, 128), F32),
-            pltpu.VMEM((ROWS, 128), F32),
-            pltpu.VMEM((NS, EC), F32),
-            pltpu.VMEM((ROWS, EC), F32),
-            pltpu.VMEM((ROWS, EC), F32),
-            pltpu.VMEM((ROWS * 8, HD), F32),
-            pltpu.VMEM((ROWS * 8, HD), F32),
-            pltpu.VMEM((ROWS, 2 * HD), BF),
             pltpu.VMEM((ROWS, EC), BF),
             pltpu.VMEM((ROWS, HEADS * HD), BF),
-            pltpu.VMEM((ROWS, NS, WIDE), BF),
             pltpu.VMEM((ROWS, NS, EC), F32),
             pltpu.VMEM((GROUP * NS, EC), BF),
             pltpu.VMEM((ROWS, EC), F32),
             pltpu.VMEM((ROWS * 8, HD), F32),
             pltpu.VMEM((ROWS * 8, HD), F32),
             pltpu.SemaphoreType.DMA((10,)),
-            pltpu.SemaphoreType.DMA((ENT // GROUP,)),
             pltpu.SemaphoreType.DMA((ROWS,)),
         ],
         compiler_params=ALONE,
@@ -737,10 +716,9 @@
     )(*operands)
 
 
-def swap(values):
-    order = [[LAST - p for p in range(PEERS)]]
+def swap(values, order):
     return lax.all_to_all(
-        values, "rep", split_axis=0, concat_axis=0, tiled=True, axis_index_groups=order
+        values, "rep", split_axis=0, concat_axis=0, tiled=True, axis_index_groups=[order]
     )
 
 
@@ -750,28 +728,30 @@
     ctx_len, row_owner, row_pos, swap_slot, swap_lens, swap_pages,
 ):
     slots = swap_slot.transpose(0, 2, 1)
-    first = swap(pack(slots, row_owner, row_pos, conv_pool.transpose(1, 0, 2), query))
-    source = jnp.where(row_owner >= 0, (LAST - row_owner) * CAP + row_pos, -1)
-    states, bias, rest = prepare(slots, swap_pages, swap_lens.transpose(0, 2, 1), ssm_pool)
-    states, flag = serve(first, bias, rest, kv_pool, states)
-    second = swap(states.reshape(PEERS, CAP * NS, WIDE)).reshape(ENT, NS, WIDE)
+    peers = list(range(PEERS))
+    first = swap(pack(slots, row_owner, row_pos, conv_pool.transpose(1, 0, 2), query), peers)
+    states, bias, rest, source, state_source = prepare(
+        slots, row_owner, row_pos, swap_pages, swap_lens.transpose(0, 2, 1), ssm_pool
+    )
+    states = serve(first, bias, rest, kv_pool, states)
+    second = swap(states.reshape(PEERS, CAP * NS, WIDE), peers[::-1]).reshape(ENT, NS, WIDE)
 
     mixed, window, part, send = mix(
-        flag, source, first, conv_state.transpose(1, 0, 2), x_in, conv_weight,
+        states, source, first, conv_state.transpose(1, 0, 2), x_in, conv_weight,
         conv_bias.reshape(1, EC), x_proj.T,
     )
     tp = lax.axis_size("tp")
     others = [
         lax.ppermute(send, "tp", [(i, (i + s) % tp) for i in range(tp)]) for s in range(1, tp)
     ]
-    mix_here, score = resident(flag, ctx_len, query, new_kv, kv_cache)
+    mix_here, score = resident(states, ctx_len, query, new_kv, kv_cache)
     dt, drive, inject, read, gate, base, kept = step_size(
-        source, part, others, dt_gain.reshape(1, RANK),
-        jnp.concatenate([b_gain, c_gain]).reshape(1, 2 * NS), dt_proj, dt_bias.reshape(1, EC), mixed,
+        state_source, part, others, dt_gain.reshape(1, RANK),
+        b_gain.reshape(1, NS), c_gain.reshape(1, NS), dt_proj, dt_bias.reshape(1, EC), mixed,
         skip.reshape(1, EC), z_gate, decay_rate, ssm_state,
     )
     new_ssm, mamba_out, attn_out = tail(
-        source, second, dt, drive, inject, read, decay_rate, gate, base, mix_here, score, new_kv, kept
+        state_source, second, dt, drive, inject, read, decay_rate, gate, base, mix_here, score, new_kv, kept
     )
     return (mamba_out, attn_out, new_ssm, window.transpose(1, 0, 2))
 

time: 69.5 us -> 67.4 us (0.970)
  waiting for transfers between devices: 2.14 us -> 5.42 us
  starting transfers between devices: 28.5 us -> 25.3 us
  Pallas kernels: 34.7 us -> 33.3 us
  other arithmetic: 1.17 us -> 0 us
    all_to_all x2, starting transfers between devices: 18.2 us -> 14.5 us  [swap(): lax.all_to_all(values, 'rep', split_axis=0, concat_axis=0, tiled=True, ax...]
    all_to_all x2, waiting for transfers between devices: 2.12 us -> 5.4 us  [swap(): lax.all_to_all(values, 'rep', split_axis=0, concat_axis=0, tiled=True, ax...]
    unnamed x24 -> x16, local copies, waits for them, and re-layouts: 1.44 us -> 1.42 us
  transfers between devices with their start and end apart: 9 -> 9, of which waited for: 1 -> 1; matrix products, arithmetic and copies ran while one was open for 2% -> 0% of each run, Pallas kernels for 31% -> 32%
where the time goes in v3:
time: 67.4 us; the launch traced here: 66.2 us
  Pallas kernels  33.3 us (49%)
  starting transfers between devices  25.3 us (38%)
  waiting for transfers between devices  5.42 us (8%)
  local copies, waits for them, and re-layouts  1.42 us (2%)
  between operations  0.78 us (1%)
    all_to_all x2, starting transfers between devices, swap(): lax.all_to_all(values, 'rep', split_axis=0, concat_axis=0, tiled=True, ax...  14.5 us
    ppermute x7, starting transfers between devices, shards(): lax.ppermute(send, 'tp', [(i, (i + s) % tp) for i in range(tp)])  10.8 us
    pallas_call x1, Pallas kernels, step_size(): pl.pallas_call(step_kernel, out_shape=(jax.ShapeDtypeStruct((ROWS, 1, EC)...  6.62 us
    pallas_call x1, Pallas kernels, resident(): pl.pallas_call(resident_kernel, grid=(ROWS // BLK,), out_shape=(shape, sh...  5.93 us
    all_to_all x2, waiting for transfers between devices, swap(): lax.all_to_all(values, 'rep', split_axis=0, concat_axis=0, tiled=True, ax...  5.4 us
    pallas_call x1, Pallas kernels, prepare(): pl.pallas_call(prepare_kernel, out_shape=(jax.ShapeDtypeStruct((ENT, NS,...  5.1 us
    pallas_call x1, Pallas kernels, tail(): pl.pallas_call(tail_kernel, out_shape=(jax.ShapeDtypeStruct((ROWS, NS, EC...  5 us
    pallas_call x1, Pallas kernels, serve(): pl.pallas_call(serve_kernel, out_shape=jax.ShapeDtypeStruct((ENT, NS, WID...  4.74 us
  transfers between devices with their start and end apart: 9, of which 1 were waited for; matrix products, arithmetic and copies ran while one was open for 0% of the time, Pallas kernels for 32%

profile of v3, /device:TPU:1, one launch (start us, length us, event | category | flops | bytes accessed | tf_op | source)
XLA Modules:
  0.0 66.2 jit_solution(13028823965737838117)
XLA Ops:
  0.6 2.3 %pack_first.1 = bf16[16,16,1024]{2,1,0:T(8,128)(2,1)} custom-call(s32[1,2,16]{2,1,0:T(2,128)} %bitcast.21, s32[32]{0:T(128)} %owner_hbm.3, s32[32]{0:T(128)} %pos_hbm.3, bf16[3,32,2048]{2,1,0:T(8,128)(2,1)} %bitcast.17, bf16[32,1024]{1,0:T(8,128)(2,1)} %query_ref.3), custom_call_target="tpu_custom_call" | custom-call | flops 134217728 | bytes 1048576 | tf_op jit(solution)/shard_map/pack_first/pallas_call | solution.py:112
  2.9 8.4 %all-to-all-start = ((bf16[16,16,1024]{2,1,0:T(8,128)(2,1)}), bf16[16,16,1024]{2,1,0:T(8,128)(2,1)S(1)}, u32[]{:S(2)}, u32[]{:S(2)}) async-start(bf16[16,16,1024]{2,1,0:T(8,128)(2,1)} %pack_first.1), calls=%async_computation | async-start | bytes 1048576 | tf_op jit(solution)/shard_map/all_to_all | solution.py:720
  11.3 5.1 %prepare_owner.1 = (bf16[32,16,2176]{2,1,0:T(8,128)(2,1)}, f32[2,256,128]{2,1,0:T(8,128)}, f32[1,128]{1,0:T(1,128)}, s32[32]{0:T(128)}, s32[32]{0:T(128)}) custom-call(s32[1,2,16]{2,1,0:T(2,128)} %bitcast.22, s32[32]{0:T(128)} %owner_hbm.3, s32[32]{0:T(128)} %pos_hbm.3, s32[1,16,2,32]{3,2,1,0:T(2,128)} %pages_hbm.1, s32[1,2,16]{2,1,0:T(2,128)} %bitcast.24, ...), custom_call_target="tpu_custom_call" | custom-call | flops 1048576 | bytes 6291456 | tf_op jit(solution)/shard_map/prepare_owner/pallas_call | solution.py:213
  16.5 5.4 %all-to-all-done.recv_hbm.recv_ref = bf16[16,16,1024]{2,1,0:T(8,128)(2,1)S(1)} async-done(((bf16[16,16,1024]{2,1,0:T(8,128)(2,1)}), bf16[16,16,1024]{2,1,0:T(8,128)(2,1)S(1)}, u32[]{:S(2)}, u32[]{:S(2)}) %all-to-all-start) | async-done | bytes 524320 | tf_op jit(solution)/shard_map/all_to_all | solution.py:720
  21.9 0.0 copy-start
  21.9 0.8 %copy-done = bf16[16,16,1024]{2,1,0:T(8,128)(2,1)} copy-done((bf16[16,16,1024]{2,1,0:T(8,128)(2,1)}, bf16[16,16,1024]{2,1,0:T(8,128)(2,1)S(1)}, u32[]{:S(2)}) %copy-start) | copy-done | bytes 524312
  22.7 4.7 %serve_pool.1.after_ref = bf16[32,16,2176]{2,1,0:T(8,128)(2,1)} custom-call(bf16[16,16,1024]{2,1,0:T(8,128)(2,1)} %copy-done, f32[2,256,128]{2,1,0:T(8,128)} %get-tuple-element.26.bias_hbm, f32[1,128]{1,0:T(1,128)} %get-tuple-element.27.rest_hbm, bf16[256,16,256]{2,1,0:T(8,128)(2,1)} %pool_hbm.1, ...), custom_call_target="tpu_custom_call", output_to_operand_aliasing={{}: (4, {})} | custom-call | flops 536870912 | bytes 6291456 | tf_op jit(solution)/shard_map/serve_pool/pallas_call | solution.py:319
  27.4 6.1 %all-to-all-start.1 = ((bf16[16,32,2176]{2,1,0:T(8,128)(2,1)}), bf16[16,32,2176]{2,1,0:T(8,128)(2,1)}, u32[]{:S(2)}, u32[]{:S(2)}) async-start(bf16[16,32,2176]{2,1,0:T(8,128)(2,1)} %bitcast.14), calls=%async_computation.1 | async-start | bytes 4456448 | tf_op jit(solution)/shard_map/all_to_all | solution.py:720
  33.5 3.6 %mix_input.1 = (bf16[32,2048]{1,0:T(8,128)(2,1)}, bf16[3,32,2048]{2,1,0:T(8,128)(2,1)}, f32[32,544]{1,0:T(8,128)}, bf16[32,544]{1,0:T(8,128)(2,1)}) custom-call(bf16[32,16,2176]{2,1,0:T(8,128)(2,1)} %serve_pool.1.after_ref, s32[32]{0:T(128)} %get-tuple-element.29.source_ref, bf16[16,16,1024]{2,1,0:T(8,128)(2,1)} %copy-done, bf16[3,32,2048]{2,1,0:T(8,128)(2,1)} %bitcast.16, ...), custom_call_target="tpu_custom_call" | custom-call | flops 71303168 | bytes 4194304 | tf_op jit(solution)/shard_map/mix_input/pallas_call | solution.py:455
  37.1 2.6 %collective-permute-start.6 = (bf16[32,544]{1,0:T(8,128)(2,1)}, bf16[32,544]{1,0:T(8,128)(2,1)S(1)}, u32[]{:S(2)}, u32[]{:S(2)}) collective-permute-start(bf16[32,544]{1,0:T(8,128)(2,1)} %get-tuple-element.31), channel_id=1, source_target_pairs={{0,7},{1,0},{2,1},{3,2},{4,3},{5,4},{6,5},{7,6},{8,15},{9,8},{10,9... | collective-permute-start | bytes 104456 | tf_op jit(solution)/shard_map/ppermute | solution.py:745
  39.7 2.7 %collective-permute-start.5 = (bf16[32,544]{1,0:T(8,128)(2,1)}, bf16[32,544]{1,0:T(8,128)(2,1)S(1)}, u32[]{:S(2)}, u32[]{:S(2)}) collective-permute-start(bf16[32,544]{1,0:T(8,128)(2,1)} %get-tuple-element.31), channel_id=1, source_target_pairs={{0,6},{1,7},{2,0},{3,1},{4,2},{5,3},{6,4},{7,5},{8,14},{9,15},{10,... | collective-permute-start | bytes 104456 | tf_op jit(solution)/shard_map/ppermute | solution.py:745
  42.4 0.7 %collective-permute-start.4 = (bf16[32,544]{1,0:T(8,128)(2,1)}, bf16[32,544]{1,0:T(8,128)(2,1)S(1)}, u32[]{:S(2)}, u32[]{:S(2)}) collective-permute-start(bf16[32,544]{1,0:T(8,128)(2,1)} %get-tuple-element.31), channel_id=1, source_target_pairs={{0,5},{1,6},{2,7},{3,0},{4,1},{5,2},{6,3},{7,4},{8,13},{9,14},{10,... | collective-permute-start | bytes 104456 | tf_op jit(solution)/shard_map/ppermute | solution.py:745
  43.1 0.6 collective-permute-start.3
  43.7 2.6 %collective-permute-start.2 = (bf16[32,544]{1,0:T(8,128)(2,1)}, bf16[32,544]{1,0:T(8,128)(2,1)S(1)}, u32[]{:S(2)}, u32[]{:S(2)}) collective-permute-start(bf16[32,544]{1,0:T(8,128)(2,1)} %get-tuple-element.31), channel_id=1, source_target_pairs={{0,3},{1,4},{2,5},{3,6},{4,7},{5,0},{6,1},{7,2},{8,11},{9,12},{10,... | collective-permute-start | bytes 104456 | tf_op jit(solution)/shard_map/ppermute | solution.py:745
  46.3 0.0 collective-permute-done.6.refs_8_
  46.3 0.0 copy-start.1
  46.3 0.7 %collective-permute-start.1 = (bf16[32,544]{1,0:T(8,128)(2,1)}, bf16[32,544]{1,0:T(8,128)(2,1)S(1)}, u32[]{:S(2)}, u32[]{:S(2)}) collective-permute-start(bf16[32,544]{1,0:T(8,128)(2,1)} %get-tuple-element.31), channel_id=1, source_target_pairs={{0,2},{1,3},{2,4},{3,5},{4,6},{5,7},{6,0},{7,1},{8,10},{9,11},{10,... | collective-permute-start | bytes 104456 | tf_op jit(solution)/shard_map/ppermute | solution.py:745
  47.0 0.0 collective-permute-done.5.refs_7_
  47.0 0.0 copy-start.2
  47.0 0.9 %collective-permute-start = (bf16[32,544]{1,0:T(8,128)(2,1)}, bf16[32,544]{1,0:T(8,128)(2,1)S(1)}, u32[]{:S(2)}, u32[]{:S(2)}) collective-permute-start(bf16[32,544]{1,0:T(8,128)(2,1)} %get-tuple-element.31), channel_id=1, source_target_pairs={{0,1},{1,2},{2,3},{3,4},{4,5},{5,6},{6,7},{7,0},{8,9},{9,10},{10,1... | collective-permute-start | bytes 104456 | tf_op jit(solution)/shard_map/ppermute | solution.py:745
  47.9 5.9 %resident_attention.1 = (f32[256,128]{1,0:T(8,128)}, f32[256,128]{1,0:T(8,128)}) custom-call(bf16[32,16,2176]{2,1,0:T(8,128)(2,1)} %serve_pool.1.after_ref, s32[32]{0:T(128)} %len_ref.1, bf16[32,1024]{1,0:T(8,128)(2,1)} %query_ref.3, bf16[32,256]{1,0:T(8,128)(2,1)} %new_kv_ref.1, bf16[32,512,256]{2,1,0:T(8,128)(2,1)} %cache_ref.1), custom_call_target="tpu_custom_call" | custom-call | flops 67108864 | bytes 9437184 | tf_op jit(solution)/shard_map/resident_attention/pallas_call | solution.py:399
  53.9 0.0 copy-done.1
  53.9 0.0 copy-done.2
  53.9 0.0 collective-permute-done.4.refs_6_
  53.9 0.0 copy-start.3
  53.9 0.0 collective-permute-done.3.refs_5_
  53.9 0.0 copy-start.4
  53.9 0.0 collective-permute-done.2.refs_4_
  53.9 0.0 copy-start.5
  53.9 0.0 collective-permute-done.1.refs_3_
  54.0 0.0 copy-start.6
  54.0 0.0 collective-permute-done.refs_2_
  54.0 0.0 copy-start.7
  54.0 0.5 copy-done.3
  54.5 0.0 copy-done.4
  54.5 0.0 copy-done.5
  54.6 0.0 copy-done.6
  54.6 0.0 copy-done.7
  54.6 6.6 %step_and_resident.1 = (f32[32,1,2048]{2,1,0:T(1,128)}, f32[32,1,2048]{2,1,0:T(1,128)}, f32[32,16,128]{2,1,0:T(8,128)}, f32[32,128]{1,0:T(8,128)}, f32[32,2048]{...) custom-call(s32[32]{0:T(128)} %get-tuple-element.25.refs_0_.source_ref, f32[32,544]{1,0:T(8,128)} %get-tuple-element.30.refs_1_, ...), custom_call_target="tpu_custom_call" | custom-call | flops 67108864 | bytes 12582912 | tf_op jit(solution)/shard_map/step_and_resident/pallas_call | solution.py:573
  61.2 0.0 all-to-all-done.1
  61.2 5.0 %update_and_join.1 = (f32[32,16,2048]{2,1,0:T(8,128)}, bf16[32,2048]{1,0:T(8,128)(2,1)}, bf16[32,1024]{1,0:T(8,128)(2,1)}) custom-call(s32[32]{0:T(128)} %get-tuple-element.25.refs_0_.source_ref, bf16[32,16,2176]{2,1,0:T(8,128)(2,1)} %bitcast.4.came, f32[32,1,2048]{2,1,0:T(1,128)} %get-tuple-element.33.dt_ref, ...), custom_call_target="tpu_custom_call", output_to_operand_aliasing={{0}: (12, {})} | custom-call | flops 16777216 | bytes 8388608 | tf_op jit(solution)/shard_map/update_and_join/pallas_call | solution.py:692
Async XLA Ops:
  2.9 19.0 %all-to-all-start = ((bf16[16,16,1024]{2,1,0:T(8,128)(2,1)}), bf16[16,16,1024]{2,1,0:T(8,128)(2,1)S(1)}, u32[]{:S(2)}, u32[]{:S(2)}) async-start(bf16[16,16,1024]{2,1,0:T(8,128)(2,1)} %pack_first.1), calls=%async_computation | async-start | bytes 1048576 | tf_op jit(solution)/shard_map/all_to_all | solution.py:720
  21.9 0.8 %copy-start = (bf16[16,16,1024]{2,1,0:T(8,128)(2,1)}, bf16[16,16,1024]{2,1,0:T(8,128)(2,1)S(1)}, u32[]{:S(2)}) copy-start(bf16[16,16,1024]{2,1,0:T(8,128)(2,1)S(1)} %all-to-all-done.recv_hbm.recv_ref) | copy-start | bytes 1572868
  27.4 33.8 %all-to-all-start.1 = ((bf16[16,32,2176]{2,1,0:T(8,128)(2,1)}), bf16[16,32,2176]{2,1,0:T(8,128)(2,1)}, u32[]{:S(2)}, u32[]{:S(2)}) async-start(bf16[16,32,2176]{2,1,0:T(8,128)(2,1)} %bitcast.14), calls=%async_computation.1 | async-start | bytes 4456448 | tf_op jit(solution)/shard_map/all_to_all | solution.py:720
  37.1 9.2 %collective-permute-start.6 = (bf16[32,544]{1,0:T(8,128)(2,1)}, bf16[32,544]{1,0:T(8,128)(2,1)S(1)}, u32[]{:S(2)}, u32[]{:S(2)}) collective-permute-start(bf16[32,544]{1,0:T(8,128)(2,1)} %get-tuple-element.31), channel_id=1, source_target_pairs={{0,7},{1,0},{2,1},{3,2},{4,3},{5,4},{6,5},{7,6},{8,15},{9,8},{10,9... | collective-permute-start | bytes 104456 | tf_op jit(solution)/shard_map/ppermute | solution.py:745
  39.7 7.3 %collective-permute-start.5 = (bf16[32,544]{1,0:T(8,128)(2,1)}, bf16[32,544]{1,0:T(8,128)(2,1)S(1)}, u32[]{:S(2)}, u32[]{:S(2)}) collective-permute-start(bf16[32,544]{1,0:T(8,128)(2,1)} %get-tuple-element.31), channel_id=1, source_target_pairs={{0,6},{1,7},{2,0},{3,1},{4,2},{5,3},{6,4},{7,5},{8,14},{9,15},{10,... | collective-permute-start | bytes 104456 | tf_op jit(solution)/shard_map/ppermute | solution.py:745
  42.4 11.5 %collective-permute-start.4 = (bf16[32,544]{1,0:T(8,128)(2,1)}, bf16[32,544]{1,0:T(8,128)(2,1)S(1)}, u32[]{:S(2)}, u32[]{:S(2)}) collective-permute-start(bf16[32,544]{1,0:T(8,128)(2,1)} %get-tuple-element.31), channel_id=1, source_target_pairs={{0,5},{1,6},{2,7},{3,0},{4,1},{5,2},{6,3},{7,4},{8,13},{9,14},{10,... | collective-permute-start | bytes 104456 | tf_op jit(solution)/shard_map/ppermute | solution.py:745
  43.1 10.8 %collective-permute-start.3 = (bf16[32,544]{1,0:T(8,128)(2,1)}, bf16[32,544]{1,0:T(8,128)(2,1)S(1)}, u32[]{:S(2)}, u32[]{:S(2)}) collective-permute-start(bf16[32,544]{1,0:T(8,128)(2,1)} %get-tuple-element.31), channel_id=1, source_target_pairs={{0,4},{1,5},{2,6},{3,7},{4,0},{5,1},{6,2},{7,3},{8,12},{9,13},{10,... | collective-permute-start | bytes 104456 | tf_op jit(solution)/shard_map/ppermute | solution.py:745
  43.7 10.2 %collective-permute-start.2 = (bf16[32,544]{1,0:T(8,128)(2,1)}, bf16[32,544]{1,0:T(8,128)(2,1)S(1)}, u32[]{:S(2)}, u32[]{:S(2)}) collective-permute-start(bf16[32,544]{1,0:T(8,128)(2,1)} %get-tuple-element.31), channel_id=1, source_target_pairs={{0,3},{1,4},{2,5},{3,6},{4,7},{5,0},{6,1},{7,2},{8,11},{9,12},{10,... | collective-permute-start | bytes 104456 | tf_op jit(solution)/shard_map/ppermute | solution.py:745
  46.3 7.6 %copy-start.1 = (bf16[32,544]{1,0:T(8,128)(2,1)}, bf16[32,544]{1,0:T(8,128)(2,1)S(1)}, u32[]{:S(2)}) copy-start(bf16[32,544]{1,0:T(8,128)(2,1)S(1)} %collective-permute-done.6.refs_8_) | copy-start | bytes 104452
  46.3 7.6 %collective-permute-start.1 = (bf16[32,544]{1,0:T(8,128)(2,1)}, bf16[32,544]{1,0:T(8,128)(2,1)S(1)}, u32[]{:S(2)}, u32[]{:S(2)}) collective-permute-start(bf16[32,544]{1,0:T(8,128)(2,1)} %get-tuple-element.31), channel_id=1, source_target_pairs={{0,2},{1,3},{2,4},{3,5},{4,6},{5,7},{6,0},{7,1},{8,10},{9,11},{10,... | collective-permute-start | bytes 104456 | tf_op jit(solution)/shard_map/ppermute | solution.py:745
  47.0 6.9 %copy-start.2 = (bf16[32,544]{1,0:T(8,128)(2,1)}, bf16[32,544]{1,0:T(8,128)(2,1)S(1)}, u32[]{:S(2)}) copy-start(bf16[32,544]{1,0:T(8,128)(2,1)S(1)} %collective-permute-done.5.refs_7_) | copy-start | bytes 104452
  47.0 7.0 %collective-permute-start = (bf16[32,544]{1,0:T(8,128)(2,1)}, bf16[32,544]{1,0:T(8,128)(2,1)S(1)}, u32[]{:S(2)}, u32[]{:S(2)}) collective-permute-start(bf16[32,544]{1,0:T(8,128)(2,1)} %get-tuple-element.31), channel_id=1, source_target_pairs={{0,1},{1,2},{2,3},{3,4},{4,5},{5,6},{6,7},{7,0},{8,9},{9,10},{10,1... | collective-permute-start | bytes 104456 | tf_op jit(solution)/shard_map/ppermute | solution.py:745
  53.9 0.6 copy-start.3
  53.9 0.6 copy-start.4
  53.9 0.6 copy-start.5
  54.0 0.6 copy-start.6
  54.0 0.6 copy-start.7

commit v4 on v3

--- a/solution.py
+++ b/solution.py
@@ -13,7 +13,7 @@
 I32 = jnp.int32
 PEERS = 16
 CAP = 2
-LAST = 15
+SIDE = 4
 ENT = PEERS * CAP
 ROWS = 32
 EC = 2048
@@ -41,6 +41,21 @@
 
 def iota(shape, dim):
     return lax.broadcasted_iota(I32, shape, dim)
+
+
+def first_peer(chunk):
+    return (chunk + PEERS - SIDE) % PEERS
+
+
+def first_chunk(peer):
+    return (peer + SIDE) % PEERS
+
+
+def second_peer(chunk):
+    return PEERS - 1 - SIDE * (chunk % SIDE) - chunk // SIDE
+
+
+second_chunk = second_peer
 
 
 def params(mib):
@@ -85,13 +100,13 @@
 
         @pl.when(owner >= 0)
         def _():
-            inverse[owner * CAP + pos_ref[r]] = 192 + r
+            inverse[first_chunk(owner) * CAP + pos_ref[r]] = 192 + r
 
     lane = iota((8, 256), 1)
     part = iota((8, 256), 0)
     tiles = []
     for e in range(ENT):
-        slot = slot_ref[0, e % CAP, e // CAP]
+        slot = slot_ref[0, e % CAP, first_peer(e // CAP)]
         want = jnp.where(part < 6, 32 * part + slot, jnp.where(part == 6, inverse[e], -1))
         tiles.append((lane == want).astype(F32))
     pick = jnp.concatenate(tiles, axis=0).astype(BF)
@@ -163,11 +178,11 @@
     for k in range(4):
         fetch(k).start()
     for r in range(ROWS):
-        owner = owner_ref[r]
-        resumed = owner >= 0
+        resumed = owner_ref[r] >= 0
+        owner = jnp.maximum(owner_ref[r], 0)
         pos = pos_ref[r]
-        source_ref[r] = jnp.where(resumed, owner * CAP + pos, -1)
-        state_source_ref[r] = jnp.where(resumed, (LAST - owner) * CAP + pos, -1)
+        source_ref[r] = jnp.where(resumed, first_chunk(owner) * CAP + pos, -1)
+        state_source_ref[r] = jnp.where(resumed, second_chunk(owner) * CAP + pos, -1)
     for copy in lists:
         copy.wait()
 
@@ -175,7 +190,7 @@
     rest = jnp.zeros((1, 128), F32)
     pages = jnp.zeros((CTX // PAGE, 128), F32)
     for place in range(CAP):
-        want = iota((PEERS, 128), 1) % ENT == (LAST - iota((PEERS, 128), 0)) * CAP + place
+        want = iota((PEERS, 128), 1) % ENT == second_chunk(iota((PEERS, 128), 0)) * CAP + place
         want = want.astype(F32)
         lens = lens_ref[0, place : place + 1, :]
         count = lens // PAGE
@@ -203,7 +218,7 @@
         fetch(k).wait()
     for k in range(4):
         for e in range(8 * k, 8 * k + 8):
-            packed[e] = states[slot_ref[0, e % CAP, LAST - e // CAP]].astype(BF)
+            packed[e] = states[slot_ref[0, e % CAP, second_peer(e // CAP)]].astype(BF)
         give(k).start()
     for k in range(4):
         give(k).wait()
@@ -258,7 +273,7 @@
         copy.start()
     lane = iota((ENT, 256), 1)
     entry = iota((ENT, 256), 0)
-    entry = CAP * (LAST - entry // CAP) + entry % CAP
+    entry = CAP * first_chunk(second_peer(entry // CAP)) + entry % CAP
     pick = (lane == 8 * entry + 6).astype(F32).astype(BF)
     loads[0].wait()
     recv = recv_ref[...].reshape(256, HALF)
@@ -728,13 +743,14 @@
     ctx_len, row_owner, row_pos, swap_slot, swap_lens, swap_pages,
 ):
     slots = swap_slot.transpose(0, 2, 1)
-    peers = list(range(PEERS))
-    first = swap(pack(slots, row_owner, row_pos, conv_pool.transpose(1, 0, 2), query), peers)
+    firsts = [first_peer(p) for p in range(PEERS)]
+    seconds = [second_peer(p) for p in range(PEERS)]
+    first = swap(pack(slots, row_owner, row_pos, conv_pool.transpose(1, 0, 2), query), firsts)
     states, bias, rest, source, state_source = prepare(
         slots, row_owner, row_pos, swap_pages, swap_lens.transpose(0, 2, 1), ssm_pool
     )
     states = serve(first, bias, rest, kv_pool, states)
-    second = swap(states.reshape(PEERS, CAP * NS, WIDE), peers[::-1]).reshape(ENT, NS, WIDE)
+    second = swap(states.reshape(PEERS, CAP * NS, WIDE), seconds).reshape(ENT, NS, WIDE)
 
     mixed, window, part, send = mix(
         states, source, first, conv_state.transpose(1, 0, 2), x_in, conv_weight,

time: 67.4 us -> 65.6 us (0.973)
  waiting for transfers between devices: 5.42 us -> 3.58 us
    all_to_all x2, waiting for transfers between devices: 5.4 us -> 3.56 us  [swap(): lax.all_to_all(values, 'rep', split_axis=0, concat_axis=0, tiled=True, ax...]
where the time goes in v4:
time: 65.6 us; the launch traced here: 65.1 us
  Pallas kernels  33.4 us (51%)
  starting transfers between devices  25.9 us (39%)
  waiting for transfers between devices  3.58 us (5%)
  local copies, waits for them, and re-layouts  1.42 us (2%)
  between operations  0.77 us (1%)
    all_to_all x2, starting transfers between devices, swap(): lax.all_to_all(values, 'rep', split_axis=0, concat_axis=0, tiled=True, ax...  15 us
    ppermute x7, starting transfers between devices, shards(): lax.ppermute(send, 'tp', [(i, (i + s) % tp) for i in range(tp)])  10.9 us
    pallas_call x1, Pallas kernels, step_size(): pl.pallas_call(step_kernel, out_shape=(jax.ShapeDtypeStruct((ROWS, 1, EC)...  6.36 us
    pallas_call x1, Pallas kernels, resident(): pl.pallas_call(resident_kernel, grid=(ROWS // BLK,), out_shape=(shape, sh...  5.93 us
    pallas_call x1, Pallas kernels, tail(): pl.pallas_call(tail_kernel, out_shape=(jax.ShapeDtypeStruct((ROWS, NS, EC...  5.34 us
    pallas_call x1, Pallas kernels, prepare(): pl.pallas_call(prepare_kernel, out_shape=(jax.ShapeDtypeStruct((ENT, NS,...  5.1 us
    pallas_call x1, Pallas kernels, serve(): pl.pallas_call(serve_kernel, out_shape=jax.ShapeDtypeStruct((ENT, NS, WID...  4.75 us
    pallas_call x1, Pallas kernels, mix(): pl.pallas_call(mix_kernel, out_shape=(jax.ShapeDtypeStruct((ROWS, EC), BF...  3.65 us
  transfers between devices with their start and end apart: 9, of which 1 were waited for; matrix products, arithmetic and copies ran while one was open for 0% of the time, Pallas kernels for 32%

profile of v4, /device:TPU:1, one launch (start us, length us, event | category | flops | bytes accessed | tf_op | source)
XLA Modules:
  0.0 65.1 jit_solution(15650902488269988834)
XLA Ops:
  0.6 2.3 %pack_first.1 = bf16[16,16,1024]{2,1,0:T(8,128)(2,1)} custom-call(s32[1,2,16]{2,1,0:T(2,128)} %bitcast.21, s32[32]{0:T(128)} %owner_hbm.3, s32[32]{0:T(128)} %pos_hbm.3, bf16[3,32,2048]{2,1,0:T(8,128)(2,1)} %bitcast.17, bf16[32,1024]{1,0:T(8,128)(2,1)} %query_ref.3), custom_call_target="tpu_custom_call" | custom-call | flops 134217728 | bytes 1048576 | tf_op jit(solution)/shard_map/pack_first/pallas_call | solution.py:127
  2.9 8.6 %all-to-all-start = ((bf16[16,16,1024]{2,1,0:T(8,128)(2,1)}), bf16[16,16,1024]{2,1,0:T(8,128)(2,1)S(1)}, u32[]{:S(2)}, u32[]{:S(2)}) async-start(bf16[16,16,1024]{2,1,0:T(8,128)(2,1)} %pack_first.1), calls=%async_computation | async-start | bytes 1048576 | tf_op jit(solution)/shard_map/all_to_all | solution.py:735
  11.5 5.1 %prepare_owner.1 = (bf16[32,16,2176]{2,1,0:T(8,128)(2,1)}, f32[2,256,128]{2,1,0:T(8,128)}, f32[1,128]{1,0:T(1,128)}, s32[32]{0:T(128)}, s32[32]{0:T(128)}) custom-call(s32[1,2,16]{2,1,0:T(2,128)} %bitcast.22, s32[32]{0:T(128)} %owner_hbm.3, s32[32]{0:T(128)} %pos_hbm.3, s32[1,16,2,32]{3,2,1,0:T(2,128)} %pages_hbm.1, s32[1,2,16]{2,1,0:T(2,128)} %bitcast.24, ...), custom_call_target="tpu_custom_call" | custom-call | flops 1048576 | bytes 6291456 | tf_op jit(solution)/shard_map/prepare_owner/pallas_call | solution.py:228
  16.6 3.6 %all-to-all-done.recv_hbm.recv_ref = bf16[16,16,1024]{2,1,0:T(8,128)(2,1)S(1)} async-done(((bf16[16,16,1024]{2,1,0:T(8,128)(2,1)}), bf16[16,16,1024]{2,1,0:T(8,128)(2,1)S(1)}, u32[]{:S(2)}, u32[]{:S(2)}) %all-to-all-start) | async-done | bytes 524320 | tf_op jit(solution)/shard_map/all_to_all | solution.py:735
  20.2 0.0 copy-start
  20.2 0.8 %copy-done = bf16[16,16,1024]{2,1,0:T(8,128)(2,1)} copy-done((bf16[16,16,1024]{2,1,0:T(8,128)(2,1)}, bf16[16,16,1024]{2,1,0:T(8,128)(2,1)S(1)}, u32[]{:S(2)}) %copy-start) | copy-done | bytes 524312
  21.0 4.8 %serve_pool.1.after_ref = bf16[32,16,2176]{2,1,0:T(8,128)(2,1)} custom-call(bf16[16,16,1024]{2,1,0:T(8,128)(2,1)} %copy-done, f32[2,256,128]{2,1,0:T(8,128)} %get-tuple-element.26.bias_hbm, f32[1,128]{1,0:T(1,128)} %get-tuple-element.27.rest_hbm, bf16[256,16,256]{2,1,0:T(8,128)(2,1)} %pool_hbm.1, ...), custom_call_target="tpu_custom_call", output_to_operand_aliasing={{}: (4, {})} | custom-call | flops 536870912 | bytes 6291456 | tf_op jit(solution)/shard_map/serve_pool/pallas_call | solution.py:334
  25.8 6.4 %all-to-all-start.1 = ((bf16[16,32,2176]{2,1,0:T(8,128)(2,1)}), bf16[16,32,2176]{2,1,0:T(8,128)(2,1)}, u32[]{:S(2)}, u32[]{:S(2)}) async-start(bf16[16,32,2176]{2,1,0:T(8,128)(2,1)} %bitcast.14), calls=%async_computation.1 | async-start | bytes 4456448 | tf_op jit(solution)/shard_map/all_to_all | solution.py:735
  32.1 3.6 %mix_input.1 = (bf16[32,2048]{1,0:T(8,128)(2,1)}, bf16[3,32,2048]{2,1,0:T(8,128)(2,1)}, f32[32,544]{1,0:T(8,128)}, bf16[32,544]{1,0:T(8,128)(2,1)}) custom-call(bf16[32,16,2176]{2,1,0:T(8,128)(2,1)} %serve_pool.1.after_ref, s32[32]{0:T(128)} %get-tuple-element.29.source_ref, bf16[16,16,1024]{2,1,0:T(8,128)(2,1)} %copy-done, bf16[3,32,2048]{2,1,0:T(8,128)(2,1)} %bitcast.16, ...), custom_call_target="tpu_custom_call" | custom-call | flops 71303168 | bytes 4194304 | tf_op jit(solution)/shard_map/mix_input/pallas_call | solution.py:470
  35.8 2.7 %collective-permute-start.6 = (bf16[32,544]{1,0:T(8,128)(2,1)}, bf16[32,544]{1,0:T(8,128)(2,1)S(1)}, u32[]{:S(2)}, u32[]{:S(2)}) collective-permute-start(bf16[32,544]{1,0:T(8,128)(2,1)} %get-tuple-element.31), channel_id=1, source_target_pairs={{0,7},{1,0},{2,1},{3,2},{4,3},{5,4},{6,5},{7,6},{8,15},{9,8},{10,9... | collective-permute-start | bytes 104456 | tf_op jit(solution)/shard_map/ppermute | solution.py:761
  38.5 2.7 %collective-permute-start.5 = (bf16[32,544]{1,0:T(8,128)(2,1)}, bf16[32,544]{1,0:T(8,128)(2,1)S(1)}, u32[]{:S(2)}, u32[]{:S(2)}) collective-permute-start(bf16[32,544]{1,0:T(8,128)(2,1)} %get-tuple-element.31), channel_id=1, source_target_pairs={{0,6},{1,7},{2,0},{3,1},{4,2},{5,3},{6,4},{7,5},{8,14},{9,15},{10,... | collective-permute-start | bytes 104456 | tf_op jit(solution)/shard_map/ppermute | solution.py:761
  41.2 0.7 %collective-permute-start.4 = (bf16[32,544]{1,0:T(8,128)(2,1)}, bf16[32,544]{1,0:T(8,128)(2,1)S(1)}, u32[]{:S(2)}, u32[]{:S(2)}) collective-permute-start(bf16[32,544]{1,0:T(8,128)(2,1)} %get-tuple-element.31), channel_id=1, source_target_pairs={{0,5},{1,6},{2,7},{3,0},{4,1},{5,2},{6,3},{7,4},{8,13},{9,14},{10,... | collective-permute-start | bytes 104456 | tf_op jit(solution)/shard_map/ppermute | solution.py:761
  41.9 0.4 collective-permute-start.3
  42.3 2.7 %collective-permute-start.2 = (bf16[32,544]{1,0:T(8,128)(2,1)}, bf16[32,544]{1,0:T(8,128)(2,1)S(1)}, u32[]{:S(2)}, u32[]{:S(2)}) collective-permute-start(bf16[32,544]{1,0:T(8,128)(2,1)} %get-tuple-element.31), channel_id=1, source_target_pairs={{0,3},{1,4},{2,5},{3,6},{4,7},{5,0},{6,1},{7,2},{8,11},{9,12},{10,... | collective-permute-start | bytes 104456 | tf_op jit(solution)/shard_map/ppermute | solution.py:761
  45.1 0.0 collective-permute-done.6.refs_8_
  45.1 0.0 copy-start.1
  45.1 0.7 %collective-permute-start.1 = (bf16[32,544]{1,0:T(8,128)(2,1)}, bf16[32,544]{1,0:T(8,128)(2,1)S(1)}, u32[]{:S(2)}, u32[]{:S(2)}) collective-permute-start(bf16[32,544]{1,0:T(8,128)(2,1)} %get-tuple-element.31), channel_id=1, source_target_pairs={{0,2},{1,3},{2,4},{3,5},{4,6},{5,7},{6,0},{7,1},{8,10},{9,11},{10,... | collective-permute-start | bytes 104456 | tf_op jit(solution)/shard_map/ppermute | solution.py:761
  45.8 0.0 collective-permute-done.5.refs_7_
  45.8 0.0 copy-start.2
  45.8 0.9 %collective-permute-start = (bf16[32,544]{1,0:T(8,128)(2,1)}, bf16[32,544]{1,0:T(8,128)(2,1)S(1)}, u32[]{:S(2)}, u32[]{:S(2)}) collective-permute-start(bf16[32,544]{1,0:T(8,128)(2,1)} %get-tuple-element.31), channel_id=1, source_target_pairs={{0,1},{1,2},{2,3},{3,4},{4,5},{5,6},{6,7},{7,0},{8,9},{9,10},{10,1... | collective-permute-start | bytes 104456 | tf_op jit(solution)/shard_map/ppermute | solution.py:761
  46.7 5.9 %resident_attention.1 = (f32[256,128]{1,0:T(8,128)}, f32[256,128]{1,0:T(8,128)}) custom-call(bf16[32,16,2176]{2,1,0:T(8,128)(2,1)} %serve_pool.1.after_ref, s32[32]{0:T(128)} %len_ref.1, bf16[32,1024]{1,0:T(8,128)(2,1)} %query_ref.3, bf16[32,256]{1,0:T(8,128)(2,1)} %new_kv_ref.1, bf16[32,512,256]{2,1,0:T(8,128)(2,1)} %cache_ref.1), custom_call_target="tpu_custom_call" | custom-call | flops 67108864 | bytes 9437184 | tf_op jit(solution)/shard_map/resident_attention/pallas_call | solution.py:414
  52.7 0.0 copy-done.1
  52.7 0.0 copy-done.2
  52.7 0.0 collective-permute-done.4.refs_6_
  52.7 0.0 copy-start.3
  52.7 0.0 collective-permute-done.3.refs_5_
  52.7 0.0 copy-start.4
  52.7 0.0 collective-permute-done.2.refs_4_
  52.7 0.0 copy-start.5
  52.7 0.0 collective-permute-done.1.refs_3_
  52.7 0.0 copy-start.6
  52.8 0.0 collective-permute-done.refs_2_
  52.8 0.0 copy-start.7
  52.8 0.5 copy-done.3
  53.3 0.0 copy-done.4
  53.3 0.0 copy-done.5
  53.3 0.0 copy-done.6
  53.4 0.0 copy-done.7
  53.4 6.4 %step_and_resident.1 = (f32[32,1,2048]{2,1,0:T(1,128)}, f32[32,1,2048]{2,1,0:T(1,128)}, f32[32,16,128]{2,1,0:T(8,128)}, f32[32,128]{1,0:T(8,128)}, f32[32,2048]{...) custom-call(s32[32]{0:T(128)} %get-tuple-element.25.refs_0_.source_ref, f32[32,544]{1,0:T(8,128)} %get-tuple-element.30.refs_1_, ...), custom_call_target="tpu_custom_call" | custom-call | flops 67108864 | bytes 12582912 | tf_op jit(solution)/shard_map/step_and_resident/pallas_call | solution.py:588
  59.8 0.0 all-to-all-done.1
  59.8 5.3 %update_and_join.1 = (f32[32,16,2048]{2,1,0:T(8,128)}, bf16[32,2048]{1,0:T(8,128)(2,1)}, bf16[32,1024]{1,0:T(8,128)(2,1)}) custom-call(s32[32]{0:T(128)} %get-tuple-element.25.refs_0_.source_ref, bf16[32,16,2176]{2,1,0:T(8,128)(2,1)} %bitcast.4.came, f32[32,1,2048]{2,1,0:T(1,128)} %get-tuple-element.33.dt_ref, ...), custom_call_target="tpu_custom_call", output_to_operand_aliasing={{0}: (12, {})} | custom-call | flops 16777216 | bytes 8388608 | tf_op jit(solution)/shard_map/update_and_join/pallas_call | solution.py:707
Async XLA Ops:
  2.9 17.3 %all-to-all-start = ((bf16[16,16,1024]{2,1,0:T(8,128)(2,1)}), bf16[16,16,1024]{2,1,0:T(8,128)(2,1)S(1)}, u32[]{:S(2)}, u32[]{:S(2)}) async-start(bf16[16,16,1024]{2,1,0:T(8,128)(2,1)} %pack_first.1), calls=%async_computation | async-start | bytes 1048576 | tf_op jit(solution)/shard_map/all_to_all | solution.py:735
  20.2 0.8 %copy-start = (bf16[16,16,1024]{2,1,0:T(8,128)(2,1)}, bf16[16,16,1024]{2,1,0:T(8,128)(2,1)S(1)}, u32[]{:S(2)}) copy-start(bf16[16,16,1024]{2,1,0:T(8,128)(2,1)S(1)} %all-to-all-done.recv_hbm.recv_ref) | copy-start | bytes 1572868
  25.8 34.0 %all-to-all-start.1 = ((bf16[16,32,2176]{2,1,0:T(8,128)(2,1)}), bf16[16,32,2176]{2,1,0:T(8,128)(2,1)}, u32[]{:S(2)}, u32[]{:S(2)}) async-start(bf16[16,32,2176]{2,1,0:T(8,128)(2,1)} %bitcast.14), calls=%async_computation.1 | async-start | bytes 4456448 | tf_op jit(solution)/shard_map/all_to_all | solution.py:735
  35.8 9.3 %collective-permute-start.6 = (bf16[32,544]{1,0:T(8,128)(2,1)}, bf16[32,544]{1,0:T(8,128)(2,1)S(1)}, u32[]{:S(2)}, u32[]{:S(2)}) collective-permute-start(bf16[32,544]{1,0:T(8,128)(2,1)} %get-tuple-element.31), channel_id=1, source_target_pairs={{0,7},{1,0},{2,1},{3,2},{4,3},{5,4},{6,5},{7,6},{8,15},{9,8},{10,9... | collective-permute-start | bytes 104456 | tf_op jit(solution)/shard_map/ppermute | solution.py:761
  38.5 7.3 %collective-permute-start.5 = (bf16[32,544]{1,0:T(8,128)(2,1)}, bf16[32,544]{1,0:T(8,128)(2,1)S(1)}, u32[]{:S(2)}, u32[]{:S(2)}) collective-permute-start(bf16[32,544]{1,0:T(8,128)(2,1)} %get-tuple-element.31), channel_id=1, source_target_pairs={{0,6},{1,7},{2,0},{3,1},{4,2},{5,3},{6,4},{7,5},{8,14},{9,15},{10,... | collective-permute-start | bytes 104456 | tf_op jit(solution)/shard_map/ppermute | solution.py:761
  41.2 11.5 %collective-permute-start.4 = (bf16[32,544]{1,0:T(8,128)(2,1)}, bf16[32,544]{1,0:T(8,128)(2,1)S(1)}, u32[]{:S(2)}, u32[]{:S(2)}) collective-permute-start(bf16[32,544]{1,0:T(8,128)(2,1)} %get-tuple-element.31), channel_id=1, source_target_pairs={{0,5},{1,6},{2,7},{3,0},{4,1},{5,2},{6,3},{7,4},{8,13},{9,14},{10,... | collective-permute-start | bytes 104456 | tf_op jit(solution)/shard_map/ppermute | solution.py:761
  41.9 10.8 %collective-permute-start.3 = (bf16[32,544]{1,0:T(8,128)(2,1)}, bf16[32,544]{1,0:T(8,128)(2,1)S(1)}, u32[]{:S(2)}, u32[]{:S(2)}) collective-permute-start(bf16[32,544]{1,0:T(8,128)(2,1)} %get-tuple-element.31), channel_id=1, source_target_pairs={{0,4},{1,5},{2,6},{3,7},{4,0},{5,1},{6,2},{7,3},{8,12},{9,13},{10,... | collective-permute-start | bytes 104456 | tf_op jit(solution)/shard_map/ppermute | solution.py:761
  42.3 10.4 %collective-permute-start.2 = (bf16[32,544]{1,0:T(8,128)(2,1)}, bf16[32,544]{1,0:T(8,128)(2,1)S(1)}, u32[]{:S(2)}, u32[]{:S(2)}) collective-permute-start(bf16[32,544]{1,0:T(8,128)(2,1)} %get-tuple-element.31), channel_id=1, source_target_pairs={{0,3},{1,4},{2,5},{3,6},{4,7},{5,0},{6,1},{7,2},{8,11},{9,12},{10,... | collective-permute-start | bytes 104456 | tf_op jit(solution)/shard_map/ppermute | solution.py:761
  45.1 7.6 %copy-start.1 = (bf16[32,544]{1,0:T(8,128)(2,1)}, bf16[32,544]{1,0:T(8,128)(2,1)S(1)}, u32[]{:S(2)}) copy-start(bf16[32,544]{1,0:T(8,128)(2,1)S(1)} %collective-permute-done.6.refs_8_) | copy-start | bytes 104452
  45.1 7.6 %collective-permute-start.1 = (bf16[32,544]{1,0:T(8,128)(2,1)}, bf16[32,544]{1,0:T(8,128)(2,1)S(1)}, u32[]{:S(2)}, u32[]{:S(2)}) collective-permute-start(bf16[32,544]{1,0:T(8,128)(2,1)} %get-tuple-element.31), channel_id=1, source_target_pairs={{0,2},{1,3},{2,4},{3,5},{4,6},{5,7},{6,0},{7,1},{8,10},{9,11},{10,... | collective-permute-start | bytes 104456 | tf_op jit(solution)/shard_map/ppermute | solution.py:761
  45.8 6.9 %copy-start.2 = (bf16[32,544]{1,0:T(8,128)(2,1)}, bf16[32,544]{1,0:T(8,128)(2,1)S(1)}, u32[]{:S(2)}) copy-start(bf16[32,544]{1,0:T(8,128)(2,1)S(1)} %collective-permute-done.5.refs_7_) | copy-start | bytes 104452
  45.8 7.0 %collective-permute-start = (bf16[32,544]{1,0:T(8,128)(2,1)}, bf16[32,544]{1,0:T(8,128)(2,1)S(1)}, u32[]{:S(2)}, u32[]{:S(2)}) collective-permute-start(bf16[32,544]{1,0:T(8,128)(2,1)} %get-tuple-element.31), channel_id=1, source_target_pairs={{0,1},{1,2},{2,3},{3,4},{4,5},{5,6},{6,7},{7,0},{8,9},{9,10},{10,1... | collective-permute-start | bytes 104456 | tf_op jit(solution)/shard_map/ppermute | solution.py:761
  52.7 0.6 copy-start.3
  52.7 0.6 copy-start.4
  52.7 0.6 copy-start.5
  52.7 0.6 copy-start.6
  52.8 0.6 copy-start.7

commit v5 on v4

--- a/solution.py
+++ b/solution.py
@@ -113,10 +113,10 @@
     for copy in copies[3:]:
         copy.wait()
     gone = []
-    for k in range(4):
-        packed = jnp.dot(pick[64 * k : 64 * k + 64], stack[...], preferred_element_type=F32)
-        made[4 * k : 4 * k + 4] = packed.astype(BF).reshape(4, 16, HALF)
-        part = slice(4 * k, 4 * k + 4)
+    for k in range(2):
+        packed = jnp.dot(pick[128 * k : 128 * k + 128], stack[...], preferred_element_type=F32)
+        made[8 * k : 8 * k + 8] = packed.astype(BF).reshape(8, 16, HALF)
+        part = slice(8 * k, 8 * k + 8)
         gone.append(pltpu.make_async_copy(made.at[part], out_ref.at[part], sems.at[k]))
         gone[k].start()
     for copy in gone:
@@ -254,7 +254,7 @@
     )(slots, owner, pos, pages, lens, ssm_pool)
 
 
-PARTS = 4
+PARTS = 2
 
 
 def serve_kernel(

time: 65.6 us -> 65.6 us (level)
  transfers between devices with their start and end apart: 9 -> 9, of which waited for: 1 -> 1; matrix products, arithmetic and copies ran while one was open for 0% -> 0% of each run, Pallas kernels for 32% -> 33%
where the time goes in v5:
time: 65.6 us; the launch traced here: 65 us
  Pallas kernels  33.3 us (51%)
  starting transfers between devices  25.9 us (39%)
  waiting for transfers between devices  3.58 us (5%)
  local copies, waits for them, and re-layouts  1.42 us (2%)
  between operations  0.77 us (1%)
    all_to_all x2, starting transfers between devices, swap(): lax.all_to_all(values, 'rep', split_axis=0, concat_axis=0, tiled=True, ax...  15 us
    ppermute x7, starting transfers between devices, shards(): lax.ppermute(send, 'tp', [(i, (i + s) % tp) for i in range(tp)])  10.9 us
    pallas_call x1, Pallas kernels, step_size(): pl.pallas_call(step_kernel, out_shape=(jax.ShapeDtypeStruct((ROWS, 1, EC)...  6.62 us
    pallas_call x1, Pallas kernels, resident(): pl.pallas_call(resident_kernel, grid=(ROWS // BLK,), out_shape=(shape, sh...  5.93 us
    pallas_call x1, Pallas kernels, prepare(): pl.pallas_call(prepare_kernel, out_shape=(jax.ShapeDtypeStruct((ENT, NS,...  5.1 us
    pallas_call x1, Pallas kernels, tail(): pl.pallas_call(tail_kernel, out_shape=(jax.ShapeDtypeStruct((ROWS, NS, EC...  4.96 us
    pallas_call x1, Pallas kernels, serve(): pl.pallas_call(serve_kernel, out_shape=jax.ShapeDtypeStruct((ENT, NS, WID...  4.86 us
    pallas_call x1, Pallas kernels, mix(): pl.pallas_call(mix_kernel, out_shape=(jax.ShapeDtypeStruct((ROWS, EC), BF...  3.65 us
  transfers between devices with their start and end apart: 9, of which 1 were waited for; matrix products, arithmetic and copies ran while one was open for 0% of the time, Pallas kernels for 33%

profile of v5, /device:TPU:1, one launch (start us, length us, event | category | flops | bytes accessed | tf_op | source)
XLA Modules:
  0.0 65.0 jit_solution(14995781928419801731)
XLA Ops:
  0.6 2.2 %pack_first.1 = bf16[16,16,1024]{2,1,0:T(8,128)(2,1)} custom-call(s32[1,2,16]{2,1,0:T(2,128)} %bitcast.21, s32[32]{0:T(128)} %owner_hbm.3, s32[32]{0:T(128)} %pos_hbm.3, bf16[3,32,2048]{2,1,0:T(8,128)(2,1)} %bitcast.17, bf16[32,1024]{1,0:T(8,128)(2,1)} %query_ref.3), custom_call_target="tpu_custom_call" | custom-call | flops 134217728 | bytes 1048576 | tf_op jit(solution)/shard_map/pack_first/pallas_call | solution.py:127
  2.8 8.6 %all-to-all-start = ((bf16[16,16,1024]{2,1,0:T(8,128)(2,1)}), bf16[16,16,1024]{2,1,0:T(8,128)(2,1)S(1)}, u32[]{:S(2)}, u32[]{:S(2)}) async-start(bf16[16,16,1024]{2,1,0:T(8,128)(2,1)} %pack_first.1), calls=%async_computation | async-start | bytes 1048576 | tf_op jit(solution)/shard_map/all_to_all | solution.py:735
  11.4 5.1 %prepare_owner.1 = (bf16[32,16,2176]{2,1,0:T(8,128)(2,1)}, f32[2,256,128]{2,1,0:T(8,128)}, f32[1,128]{1,0:T(1,128)}, s32[32]{0:T(128)}, s32[32]{0:T(128)}) custom-call(s32[1,2,16]{2,1,0:T(2,128)} %bitcast.22, s32[32]{0:T(128)} %owner_hbm.3, s32[32]{0:T(128)} %pos_hbm.3, s32[1,16,2,32]{3,2,1,0:T(2,128)} %pages_hbm.1, s32[1,2,16]{2,1,0:T(2,128)} %bitcast.24, ...), custom_call_target="tpu_custom_call" | custom-call | flops 1048576 | bytes 6291456 | tf_op jit(solution)/shard_map/prepare_owner/pallas_call | solution.py:228
  16.5 3.6 %all-to-all-done.recv_hbm.recv_ref = bf16[16,16,1024]{2,1,0:T(8,128)(2,1)S(1)} async-done(((bf16[16,16,1024]{2,1,0:T(8,128)(2,1)}), bf16[16,16,1024]{2,1,0:T(8,128)(2,1)S(1)}, u32[]{:S(2)}, u32[]{:S(2)}) %all-to-all-start) | async-done | bytes 524320 | tf_op jit(solution)/shard_map/all_to_all | solution.py:735
  20.1 0.0 copy-start
  20.1 0.8 %copy-done = bf16[16,16,1024]{2,1,0:T(8,128)(2,1)} copy-done((bf16[16,16,1024]{2,1,0:T(8,128)(2,1)}, bf16[16,16,1024]{2,1,0:T(8,128)(2,1)S(1)}, u32[]{:S(2)}) %copy-start) | copy-done | bytes 524312
  20.9 4.9 %serve_pool.1.after_ref = bf16[32,16,2176]{2,1,0:T(8,128)(2,1)} custom-call(bf16[16,16,1024]{2,1,0:T(8,128)(2,1)} %copy-done, f32[2,256,128]{2,1,0:T(8,128)} %get-tuple-element.26.bias_hbm, f32[1,128]{1,0:T(1,128)} %get-tuple-element.27.rest_hbm, bf16[256,16,256]{2,1,0:T(8,128)(2,1)} %pool_hbm.1, ...), custom_call_target="tpu_custom_call", output_to_operand_aliasing={{}: (4, {})} | custom-call | flops 536870912 | bytes 6291456 | tf_op jit(solution)/shard_map/serve_pool/pallas_call | solution.py:334
  25.8 6.4 %all-to-all-start.1 = ((bf16[16,32,2176]{2,1,0:T(8,128)(2,1)}), bf16[16,32,2176]{2,1,0:T(8,128)(2,1)}, u32[]{:S(2)}, u32[]{:S(2)}) async-start(bf16[16,32,2176]{2,1,0:T(8,128)(2,1)} %bitcast.14), calls=%async_computation.1 | async-start | bytes 4456448 | tf_op jit(solution)/shard_map/all_to_all | solution.py:735
  32.2 3.6 %mix_input.1 = (bf16[32,2048]{1,0:T(8,128)(2,1)}, bf16[3,32,2048]{2,1,0:T(8,128)(2,1)}, f32[32,544]{1,0:T(8,128)}, bf16[32,544]{1,0:T(8,128)(2,1)}) custom-call(bf16[32,16,2176]{2,1,0:T(8,128)(2,1)} %serve_pool.1.after_ref, s32[32]{0:T(128)} %get-tuple-element.29.source_ref, bf16[16,16,1024]{2,1,0:T(8,128)(2,1)} %copy-done, bf16[3,32,2048]{2,1,0:T(8,128)(2,1)} %bitcast.16, ...), custom_call_target="tpu_custom_call" | custom-call | flops 71303168 | bytes 4194304 | tf_op jit(solution)/shard_map/mix_input/pallas_call | solution.py:470
  35.8 2.7 %collective-permute-start.6 = (bf16[32,544]{1,0:T(8,128)(2,1)}, bf16[32,544]{1,0:T(8,128)(2,1)S(1)}, u32[]{:S(2)}, u32[]{:S(2)}) collective-permute-start(bf16[32,544]{1,0:T(8,128)(2,1)} %get-tuple-element.31), channel_id=1, source_target_pairs={{0,7},{1,0},{2,1},{3,2},{4,3},{5,4},{6,5},{7,6},{8,15},{9,8},{10,9... | collective-permute-start | bytes 104456 | tf_op jit(solution)/shard_map/ppermute | solution.py:761
  38.5 2.7 %collective-permute-start.5 = (bf16[32,544]{1,0:T(8,128)(2,1)}, bf16[32,544]{1,0:T(8,128)(2,1)S(1)}, u32[]{:S(2)}, u32[]{:S(2)}) collective-permute-start(bf16[32,544]{1,0:T(8,128)(2,1)} %get-tuple-element.31), channel_id=1, source_target_pairs={{0,6},{1,7},{2,0},{3,1},{4,2},{5,3},{6,4},{7,5},{8,14},{9,15},{10,... | collective-permute-start | bytes 104456 | tf_op jit(solution)/shard_map/ppermute | solution.py:761
  41.2 0.7 %collective-permute-start.4 = (bf16[32,544]{1,0:T(8,128)(2,1)}, bf16[32,544]{1,0:T(8,128)(2,1)S(1)}, u32[]{:S(2)}, u32[]{:S(2)}) collective-permute-start(bf16[32,544]{1,0:T(8,128)(2,1)} %get-tuple-element.31), channel_id=1, source_target_pairs={{0,5},{1,6},{2,7},{3,0},{4,1},{5,2},{6,3},{7,4},{8,13},{9,14},{10,... | collective-permute-start | bytes 104456 | tf_op jit(solution)/shard_map/ppermute | solution.py:761
  41.9 0.4 collective-permute-start.3
  42.3 2.8 %collective-permute-start.2 = (bf16[32,544]{1,0:T(8,128)(2,1)}, bf16[32,544]{1,0:T(8,128)(2,1)S(1)}, u32[]{:S(2)}, u32[]{:S(2)}) collective-permute-start(bf16[32,544]{1,0:T(8,128)(2,1)} %get-tuple-element.31), channel_id=1, source_target_pairs={{0,3},{1,4},{2,5},{3,6},{4,7},{5,0},{6,1},{7,2},{8,11},{9,12},{10,... | collective-permute-start | bytes 104456 | tf_op jit(solution)/shard_map/ppermute | solution.py:761
  45.1 0.0 collective-permute-done.6.refs_8_
  45.1 0.0 copy-start.1
  45.1 0.7 %collective-permute-start.1 = (bf16[32,544]{1,0:T(8,128)(2,1)}, bf16[32,544]{1,0:T(8,128)(2,1)S(1)}, u32[]{:S(2)}, u32[]{:S(2)}) collective-permute-start(bf16[32,544]{1,0:T(8,128)(2,1)} %get-tuple-element.31), channel_id=1, source_target_pairs={{0,2},{1,3},{2,4},{3,5},{4,6},{5,7},{6,0},{7,1},{8,10},{9,11},{10,... | collective-permute-start | bytes 104456 | tf_op jit(solution)/shard_map/ppermute | solution.py:761
  45.8 0.0 collective-permute-done.5.refs_7_
  45.8 0.0 copy-start.2
  45.8 0.9 %collective-permute-start = (bf16[32,544]{1,0:T(8,128)(2,1)}, bf16[32,544]{1,0:T(8,128)(2,1)S(1)}, u32[]{:S(2)}, u32[]{:S(2)}) collective-permute-start(bf16[32,544]{1,0:T(8,128)(2,1)} %get-tuple-element.31), channel_id=1, source_target_pairs={{0,1},{1,2},{2,3},{3,4},{4,5},{5,6},{6,7},{7,0},{8,9},{9,10},{10,1... | collective-permute-start | bytes 104456 | tf_op jit(solution)/shard_map/ppermute | solution.py:761
  46.7 5.9 %resident_attention.1 = (f32[256,128]{1,0:T(8,128)}, f32[256,128]{1,0:T(8,128)}) custom-call(bf16[32,16,2176]{2,1,0:T(8,128)(2,1)} %serve_pool.1.after_ref, s32[32]{0:T(128)} %len_ref.1, bf16[32,1024]{1,0:T(8,128)(2,1)} %query_ref.3, bf16[32,256]{1,0:T(8,128)(2,1)} %new_kv_ref.1, bf16[32,512,256]{2,1,0:T(8,128)(2,1)} %cache_ref.1), custom_call_target="tpu_custom_call" | custom-call | flops 67108864 | bytes 9437184 | tf_op jit(solution)/shard_map/resident_attention/pallas_call | solution.py:414
  52.7 0.0 copy-done.1
  52.7 0.0 copy-done.2
  52.7 0.0 collective-permute-done.4.refs_6_
  52.7 0.0 copy-start.3
  52.7 0.0 collective-permute-done.3.refs_5_
  52.7 0.0 copy-start.4
  52.7 0.0 collective-permute-done.2.refs_4_
  52.7 0.0 copy-start.5
  52.7 0.0 collective-permute-done.1.refs_3_
  52.7 0.0 copy-start.6
  52.8 0.0 collective-permute-done.refs_2_
  52.8 0.0 copy-start.7
  52.8 0.5 copy-done.3
  53.3 0.0 copy-done.4
  53.3 0.0 copy-done.5
  53.3 0.0 copy-done.6
  53.4 0.0 copy-done.7
  53.4 6.6 %step_and_resident.1 = (f32[32,1,2048]{2,1,0:T(1,128)}, f32[32,1,2048]{2,1,0:T(1,128)}, f32[32,16,128]{2,1,0:T(8,128)}, f32[32,128]{1,0:T(8,128)}, f32[32,2048]{...) custom-call(s32[32]{0:T(128)} %get-tuple-element.25.refs_0_.source_ref, f32[32,544]{1,0:T(8,128)} %get-tuple-element.30.refs_1_, ...), custom_call_target="tpu_custom_call" | custom-call | flops 67108864 | bytes 12582912 | tf_op jit(solution)/shard_map/step_and_resident/pallas_call | solution.py:588
  60.0 0.0 all-to-all-done.1
  60.0 5.0 %update_and_join.1 = (f32[32,16,2048]{2,1,0:T(8,128)}, bf16[32,2048]{1,0:T(8,128)(2,1)}, bf16[32,1024]{1,0:T(8,128)(2,1)}) custom-call(s32[32]{0:T(128)} %get-tuple-element.25.refs_0_.source_ref, bf16[32,16,2176]{2,1,0:T(8,128)(2,1)} %bitcast.4.came, f32[32,1,2048]{2,1,0:T(1,128)} %get-tuple-element.33.dt_ref, ...), custom_call_target="tpu_custom_call", output_to_operand_aliasing={{0}: (12, {})} | custom-call | flops 16777216 | bytes 8388608 | tf_op jit(solution)/shard_map/update_and_join/pallas_call | solution.py:707
Async XLA Ops:
  2.8 17.3 %all-to-all-start = ((bf16[16,16,1024]{2,1,0:T(8,128)(2,1)}), bf16[16,16,1024]{2,1,0:T(8,128)(2,1)S(1)}, u32[]{:S(2)}, u32[]{:S(2)}) async-start(bf16[16,16,1024]{2,1,0:T(8,128)(2,1)} %pack_first.1), calls=%async_computation | async-start | bytes 1048576 | tf_op jit(solution)/shard_map/all_to_all | solution.py:735
  20.1 0.8 %copy-start = (bf16[16,16,1024]{2,1,0:T(8,128)(2,1)}, bf16[16,16,1024]{2,1,0:T(8,128)(2,1)S(1)}, u32[]{:S(2)}) copy-start(bf16[16,16,1024]{2,1,0:T(8,128)(2,1)S(1)} %all-to-all-done.recv_hbm.recv_ref) | copy-start | bytes 1572868
  25.8 34.3 %all-to-all-start.1 = ((bf16[16,32,2176]{2,1,0:T(8,128)(2,1)}), bf16[16,32,2176]{2,1,0:T(8,128)(2,1)}, u32[]{:S(2)}, u32[]{:S(2)}) async-start(bf16[16,32,2176]{2,1,0:T(8,128)(2,1)} %bitcast.14), calls=%async_computation.1 | async-start | bytes 4456448 | tf_op jit(solution)/shard_map/all_to_all | solution.py:735
  35.8 9.3 %collective-permute-start.6 = (bf16[32,544]{1,0:T(8,128)(2,1)}, bf16[32,544]{1,0:T(8,128)(2,1)S(1)}, u32[]{:S(2)}, u32[]{:S(2)}) collective-permute-start(bf16[32,544]{1,0:T(8,128)(2,1)} %get-tuple-element.31), channel_id=1, source_target_pairs={{0,7},{1,0},{2,1},{3,2},{4,3},{5,4},{6,5},{7,6},{8,15},{9,8},{10,9... | collective-permute-start | bytes 104456 | tf_op jit(solution)/shard_map/ppermute | solution.py:761
  38.5 7.3 %collective-permute-start.5 = (bf16[32,544]{1,0:T(8,128)(2,1)}, bf16[32,544]{1,0:T(8,128)(2,1)S(1)}, u32[]{:S(2)}, u32[]{:S(2)}) collective-permute-start(bf16[32,544]{1,0:T(8,128)(2,1)} %get-tuple-element.31), channel_id=1, source_target_pairs={{0,6},{1,7},{2,0},{3,1},{4,2},{5,3},{6,4},{7,5},{8,14},{9,15},{10,... | collective-permute-start | bytes 104456 | tf_op jit(solution)/shard_map/ppermute | solution.py:761
  41.2 11.5 %collective-permute-start.4 = (bf16[32,544]{1,0:T(8,128)(2,1)}, bf16[32,544]{1,0:T(8,128)(2,1)S(1)}, u32[]{:S(2)}, u32[]{:S(2)}) collective-permute-start(bf16[32,544]{1,0:T(8,128)(2,1)} %get-tuple-element.31), channel_id=1, source_target_pairs={{0,5},{1,6},{2,7},{3,0},{4,1},{5,2},{6,3},{7,4},{8,13},{9,14},{10,... | collective-permute-start | bytes 104456 | tf_op jit(solution)/shard_map/ppermute | solution.py:761
  41.9 10.8 %collective-permute-start.3 = (bf16[32,544]{1,0:T(8,128)(2,1)}, bf16[32,544]{1,0:T(8,128)(2,1)S(1)}, u32[]{:S(2)}, u32[]{:S(2)}) collective-permute-start(bf16[32,544]{1,0:T(8,128)(2,1)} %get-tuple-element.31), channel_id=1, source_target_pairs={{0,4},{1,5},{2,6},{3,7},{4,0},{5,1},{6,2},{7,3},{8,12},{9,13},{10,... | collective-permute-start | bytes 104456 | tf_op jit(solution)/shard_map/ppermute | solution.py:761
  42.3 10.4 %collective-permute-start.2 = (bf16[32,544]{1,0:T(8,128)(2,1)}, bf16[32,544]{1,0:T(8,128)(2,1)S(1)}, u32[]{:S(2)}, u32[]{:S(2)}) collective-permute-start(bf16[32,544]{1,0:T(8,128)(2,1)} %get-tuple-element.31), channel_id=1, source_target_pairs={{0,3},{1,4},{2,5},{3,6},{4,7},{5,0},{6,1},{7,2},{8,11},{9,12},{10,... | collective-permute-start | bytes 104456 | tf_op jit(solution)/shard_map/ppermute | solution.py:761
  45.1 7.6 %copy-start.1 = (bf16[32,544]{1,0:T(8,128)(2,1)}, bf16[32,544]{1,0:T(8,128)(2,1)S(1)}, u32[]{:S(2)}) copy-start(bf16[32,544]{1,0:T(8,128)(2,1)S(1)} %collective-permute-done.6.refs_8_) | copy-start | bytes 104452
  45.1 7.6 %collective-permute-start.1 = (bf16[32,544]{1,0:T(8,128)(2,1)}, bf16[32,544]{1,0:T(8,128)(2,1)S(1)}, u32[]{:S(2)}, u32[]{:S(2)}) collective-permute-start(bf16[32,544]{1,0:T(8,128)(2,1)} %get-tuple-element.31), channel_id=1, source_target_pairs={{0,2},{1,3},{2,4},{3,5},{4,6},{5,7},{6,0},{7,1},{8,10},{9,11},{10,... | collective-permute-start | bytes 104456 | tf_op jit(solution)/shard_map/ppermute | solution.py:761
  45.8 6.9 %copy-start.2 = (bf16[32,544]{1,0:T(8,128)(2,1)}, bf16[32,544]{1,0:T(8,128)(2,1)S(1)}, u32[]{:S(2)}) copy-start(bf16[32,544]{1,0:T(8,128)(2,1)S(1)} %collective-permute-done.5.refs_7_) | copy-start | bytes 104452
  45.8 7.0 %collective-permute-start = (bf16[32,544]{1,0:T(8,128)(2,1)}, bf16[32,544]{1,0:T(8,128)(2,1)S(1)}, u32[]{:S(2)}, u32[]{:S(2)}) collective-permute-start(bf16[32,544]{1,0:T(8,128)(2,1)} %get-tuple-element.31), channel_id=1, source_target_pairs={{0,1},{1,2},{2,3},{3,4},{4,5},{5,6},{6,7},{7,0},{8,9},{9,10},{10,1... | collective-permute-start | bytes 104456 | tf_op jit(solution)/shard_map/ppermute | solution.py:761
  52.7 0.6 copy-start.3
  52.7 0.6 copy-start.4
  52.7 0.6 copy-start.5
  52.7 0.6 copy-start.6
  52.8 0.6 copy-start.7
